TPU v7x, 32 devices: a whole 2x2x4 slice. The times are simulated.
32 devices in a mesh: gx: 4 (over z), gy: 8 (over y, x, core).
Axes of the slice: x: 2, y: 2, z: 4, core: 2. Of those that a mesh axis runs over, the one named last changes fastest.
Arguments:
- observed: bfloat16 [1024, 1024, 128], P('gx', 'gy'), may hold values from -6 to 6
- confidence: bfloat16 [1024, 1024, 128], P('gx', 'gy'), may hold values from 0.1 to 13
- iterate: float32 [1024, 1024, 128], P('gx', 'gy'), may hold values from -24 to 24
- kernel_bank: float32 [3, 64], replicated, may hold values from 0.02 to 1
- tap_index: int32 [3, 33], replicated, may hold values from 0 to 63
- offsets: int32 [3], replicated, may hold values from -4 to 4
- basis_x: bfloat16 [1024, 1024], P('gx'), may hold values from -0.1875 to 0.1875
- basis_y: bfloat16 [1024, 1024], P('gy'), may hold values from -0.1875 to 0.1875
- basis_z: bfloat16 [128, 128], replicated, may hold values from -0.5 to 0.5
- eigen_x: float32 [1024], P('gx'), may hold values from 0.1 to 1
- eigen_y: float32 [1024], replicated, may hold values from 0.1 to 1
- eigen_z: float32 [128], replicated, may hold values from 0.1 to 1
Outputs:
- updated: float32 [1024, 1024, 128], P('gx', 'gy')
- residual: float32 [1024, 1024, 128], P('gx', 'gy')
All inputs are finite; a program needn't handle non-finite values.
Results may differ from a plain program's by a relative error of at most 0.0028.
Values may be sent and summed in bfloat16 or wider, within the bound.
A program may use at most 256 MiB of HBM per device.

v0:
```python
import jax
import jax.numpy as jnp
from jax import lax
from jax.sharding import PartitionSpec as P

HALF = 16
SHIFT = 4
CHUNKS = 2


highest = lax.Precision.HIGHEST
tikhonov = 0.002


def exchange(block, axis, dim, width):
    count = lax.axis_size(axis)
    forward = [(i, i + 1) for i in range(count - 1)]
    backward = [(target, source) for source, target in forward]
    low = lax.ppermute(
        lax.slice_in_dim(block, block.shape[dim] - width, None, axis=dim), axis, forward
    )
    high = lax.ppermute(lax.slice_in_dim(block, 0, width, axis=dim), axis, backward)
    return low, high


def kernels_of(kernel_bank, tap_index):
    entries = jnp.arange(kernel_bank.shape[1], dtype=jnp.int32)
    chosen = tap_index[:, :, None] == entries[None, None, :]
    raw_taps = jnp.sum(jnp.where(chosen, kernel_bank[:, None, :], 0.0), axis=2)
    return raw_taps / jnp.sum(raw_taps, axis=1, keepdims=True)


def band_matrix(kernel, offset, out_count, in_count, margin):
    center = (kernel.shape[0] - 1) // 2
    row_pos = lax.broadcasted_iota(jnp.int32, (out_count, in_count), 0)
    col_pos = lax.broadcasted_iota(jnp.int32, (out_count, in_count), 1)
    position = col_pos - row_pos - margin + center - offset
    tap_ids = jnp.arange(kernel.shape[0], dtype=jnp.int32)
    chosen = position[None, :, :] == tap_ids[:, None, None]
    return jnp.sum(jnp.where(chosen, kernel[:, None, None], 0.0), axis=0)


def split_dot(spec, matrix, block):
    return jnp.einsum(spec, matrix, block.astype(jnp.float32), precision=lax.Precision.HIGH)


def turned(array, axis_name, dim, sign):
    count = lax.axis_size(axis_name)
    size = array.shape[dim] // count
    mine = lax.axis_index(axis_name)
    pieces = [
        lax.dynamic_slice_in_dim(array, lax.rem(mine + sign * step + count, count) * size, size, dim)
        for step in range(count)
    ]
    return jnp.concatenate(pieces, axis=dim)


def swap(block, axis_name, split, concat, sign):
    count = lax.axis_size(axis_name)
    pieces = jnp.split(block, count, axis=split)
    arrived = [pieces[0]]
    for step in range(1, count):
        pairs = [(i, (i + sign * step) % count) for i in range(count)]
        arrived.append(lax.ppermute(pieces[step], axis_name, pairs))
    return jnp.concatenate(arrived, axis=concat)


def blur_xy(along_z, kernels, offsets):
    rim = HALF + SHIFT
    block_x, block_y, _ = along_z.shape
    x_matrix = band_matrix(kernels[0], offsets[0], block_x, block_x + 2 * rim, rim)
    y_matrix = band_matrix(kernels[1], offsets[1], block_y, block_y + 2 * rim, rim)
    low, high = exchange(along_z, "gx", 0, rim)
    extended = jnp.concatenate([low, along_z, high], axis=0)
    along_x = split_dot("ic,cyz->iyz", x_matrix, extended).astype(jnp.bfloat16)
    low, high = exchange(along_x, "gy", 1, rim)
    inner = split_dot("jc,xcz->xjz", y_matrix[:, rim:-rim], along_x)
    rims = jnp.concatenate([low, high], axis=1)
    rim_matrix = jnp.concatenate([y_matrix[:, :rim], y_matrix[:, -rim:]], axis=1)
    return inner + split_dot("jc,xcz->xjz", rim_matrix, rims)


def apply_blur(source, kernels, offsets):
    depth = source.shape[2]
    z_matrix = band_matrix(kernels[2], offsets[2], depth, depth, 0)
    along_z = jnp.einsum("xyc,zc->xyz", source, z_matrix, precision=lax.Precision.HIGH)
    return blur_xy(along_z.astype(jnp.bfloat16), kernels, offsets)


def shards(
    observed,
    confidence,
    iterate,
    kernel_bank,
    tap_index,
    offsets,
    basis_x,
    basis_y,
    basis_z,
    eigen_x,
    eigen_y,
    eigen_z,
):
    kernels = kernels_of(kernel_bank, tap_index)
    adjoint_kernels = kernels[:, ::-1]
    weights = confidence.astype(jnp.float32)
    misfit = observed.astype(jnp.float32) - apply_blur(iterate, kernels, offsets)
    gradient = apply_blur(weights * misfit, adjoint_kernels, -offsets) - tikhonov * iterate
    full_x = lax.all_gather(basis_x, "gx", axis=0, tiled=True)
    full_y = lax.all_gather(basis_y, "gy", axis=0, tiled=True)

    gradient_b = gradient.astype(jnp.bfloat16)
    gx_size = lax.axis_size("gx")
    depth = basis_z.shape[0]
    share_z = depth // gx_size
    chunks = min(CHUNKS, share_z)
    part = share_z // chunks
    z_ahead = turned(basis_z, "gx", 1, 1).reshape(depth, gx_size, chunks, part)
    eigen_part = lax.dynamic_slice_in_dim(eigen_z, lax.axis_index("gx") * share_z, share_z)
    all_x = lax.all_gather(eigen_x, "gx", axis=0, tiled=True)
    share_x = all_x.shape[0] // lax.axis_size("gy")
    part_x = lax.dynamic_slice_in_dim(all_x, lax.axis_index("gy") * share_x, share_x)
    x_rows_behind = turned(full_x, "gx", 0, -1)
    x_ahead = turned(x_rows_behind, "gy", 1, 1)
    x_return = turned(turned(full_x, "gx", 0, 1), "gy", 1, -1)
    y_behind = turned(full_y, "gy", 0, -1)
    y_ahead = turned(full_y, "gy", 0, 1)
    found = []
    for chunk in range(chunks):
        modes = z_ahead[:, :, chunk].reshape(depth, gx_size * part)
        section_one = jnp.einsum(
            "zk,xyz->kxy", modes, gradient_b, preferred_element_type=jnp.float32
        ).astype(jnp.bfloat16)
        lines = swap(section_one, "gx", 0, 1, 1)
        section_two = jnp.einsum(
            "xj,kxy->kjy", x_ahead, lines, preferred_element_type=jnp.float32
        ).astype(jnp.bfloat16)
        lines = swap(section_two, "gy", 1, 2, 1)
        part_z = eigen_part[chunk * part : (chunk + 1) * part]
        inverse = 1.0 / (
            part_x[None, :, None] * eigen_y[None, None, :] * part_z[:, None, None] + tikhonov
        )
        section_four = (
            jnp.einsum("axy,yk->axk", lines, y_behind, preferred_element_type=jnp.float32)
            * inverse
        ).astype(jnp.bfloat16)
        section_five = jnp.einsum(
            "axk,jk->axj", section_four, y_ahead, preferred_element_type=jnp.float32
        ).astype(jnp.bfloat16)
        lines = swap(section_five, "gy", 2, 1, 1)
        section_six = jnp.einsum(
            "jx,kxy->kjy", x_return, lines, preferred_element_type=jnp.float32
        ).astype(jnp.bfloat16)
        found.append(swap(section_six, "gx", 1, 0, 1))
    section_six = jnp.concatenate(found, axis=0)
    basis_z = (
        turned(basis_z, "gx", 1, -1)
        .reshape(depth, gx_size, chunks, part)
        .transpose(0, 2, 1, 3)
        .reshape(depth, depth)
    )
    direction = jnp.einsum("kxy,zk->xyz", section_six, basis_z, preferred_element_type=jnp.float32)
    z_matrix = band_matrix(kernels[2], offsets[2], depth, depth, 0)
    z_modes = jnp.dot(z_matrix, basis_z.astype(jnp.float32), precision=highest)
    along_z = jnp.einsum(
        "kxy,zk->xyz", section_six.astype(jnp.float32), z_modes, precision=lax.Precision.HIGH
    ).astype(jnp.bfloat16)
    local_descent = jnp.sum(gradient * direction)
    descent = lax.psum(local_descent, ("gx", "gy"))
    blurred = blur_xy(along_z, kernels, offsets)
    data_sum, norm_sum = lax.psum(
        (jnp.sum(weights * blurred * blurred), jnp.sum(direction * direction)), ("gx", "gy")
    )
    energy = data_sum + tikhonov * norm_sum
    step_size = descent / energy
    return (iterate + step_size * direction, misfit - step_size * blurred)


def solution(mesh):
    return jax.shard_map(
        shards,
        mesh=mesh,
        in_specs=(
            P("gx", "gy", None),
            P("gx", "gy", None),
            P("gx", "gy", None),
            P(),
            P(),
            P(),
            P("gx", None),
            P("gy", None),
            P(),
            P("gx"),
            P(),
            P(),
        ),
        out_specs=(P("gx", "gy", None), P("gx", "gy", None)),
        check_vma=False,
    )
```

profile of v0, /device:TPU:0, one launch (start us, length us, event | category | flops | bytes accessed | tf_op | source)
XLA Modules:
  0.0 1156.1 jit_solution(7296010660347990047)
XLA Ops:
  80.5 14.2 %copy.127 = bf16[296,128,128]{2,0,1:T(8,128)(2,1)} copy(bf16[296,128,128]{1,2,0:T(8,128)(2,1)} %pad_maximum_fusion) | data formatting | bytes 19398656 | tf_op jit(solution)/shard_map/concatenate | solution.py:74
  111.2 24.7 %fusion.11 = f32[256,128,128]{2,1,0:T(8,128)} fusion(bf16[256,128,128]{2,0,1:T(8,128)(2,1)S(1)} %convolution_convert_fusion.1, f32[128,168]{0,1:T(8,128)S(1)} %select_reduce_fusion.3), kind=kOutput, calls=%fused_computation.27 | convolution fusion | flops 3221225472 | bytes 25231360 | tf_op jit(solution)/shard_map/jc,xcz->xjz/dot_general | solution.py:44
  137.6 14.9 %bitcast_subtract_fusion.1 = f32[256,128,128]{1,2,0:T(8,128)} fusion(f32[256,128,128]{2,1,0:T(8,128)} %fusion.11, bf16[256,128,128]{1,2,0:T(8,128)(2,1)S(1)} %bitcast.123, bf16[256,40,128]{2,0,1:T(8,128)(2,1)} %pad_maximum_fusion.7, f32[128,20]{0,1:T(8,128)S(1)} %get-tuple-element.99, f32[128,20]{0,1:T(8,128)S(1)} %get-tuple-element.98), kind=kOutput, calls=%fused_computation.7 | convolution fusion | flops 1019220992 | bytes 44584960 | tf_op jit(solution)/shard_map/jc,xcz->xjz/dot_general | solution.py:44
  152.5 20.4 %fusion.13 = bf16[256,128,128]{2,1,0:T(8,128)(2,1)} fusion(f32[256,128,128]{1,2,0:T(8,128)} %bitcast_subtract_fusion.1, bf16[256,128,128]{1,2,0:T(8,128)(2,1)} %copy.125, f32[128,128]{1,0:T(8,128)S(1)} %copy-done.19), kind=kOutput, calls=%fused_computation.33 | convolution fusion | flops 3233808384 | bytes 33619968 | tf_op jit(solution)/shard_map/xyc,zc->xyz/dot_general | solution.py:86
  180.5 17.4 %copy.161 = f32[256,128,128]{1,2,0:T(8,128)} copy(f32[256,128,128]{2,1,0:T(8,128)} %param.14) | data formatting | bytes 33554432 | tf_op args[2]
  217.6 26.5 %fusion.14 = bf16[256,128,128]{2,0,1:T(8,128)(2,1)S(1)} fusion(bf16[296,128,128]{2,1,0:T(8,128)(2,1)S(1)} %pad_maximum_fusion.1, f32[256,296]{0,1:T(8,128)S(1)} %select_reduce_fusion.1), kind=kOutput, calls=%fused_computation.34 | convolution fusion | flops 7453278208 | bytes 18391040 | tf_op jit(solution)/shard_map/ic,cyz->iyz/dot_general | solution.py:44
  250.5 24.9 %fusion.9 = f32[256,128,128]{2,1,0:T(8,128)} fusion(bf16[256,128,128]{2,0,1:T(8,128)(2,1)S(1)} %fusion.14, f32[128,168]{0,1:T(8,128)S(1)} %select_reduce_fusion.2), kind=kOutput, calls=%fused_computation.25 | convolution fusion | flops 3221225472 | bytes 25231360 | tf_op jit(solution)/shard_map/jc,xcz->xjz/dot_general | solution.py:44
  294.4 22.8 %bitcast_subtract_fusion = f32[256,128,128]{1,2,0:T(8,128)} fusion(f32[256,128,128]{1,2,0:T(8,128)} %copy.161, f32[256,128,128]{2,1,0:T(8,128)} %fusion.9, bf16[256,40,128]{2,0,1:T(8,128)(2,1)S(1)} %pad_maximum_fusion.8, f32[128,20]{0,1:T(8,128)S(1)} %copy-done.33, f32[128,20]{0,1:T(8,128)S(1)} %copy-done.32), kind=kOutput, calls=%fused_computation.6 | convolution fusion | flops 1019220992 | bytes 52973568 | tf_op jit(solution)/shard_map/jc,xcz->xjz/dot_general | solution.py:44
  342.9 13.3 %collective-permute-done.10 = bf16[16,256,128]{2,0,1:T(8,128)(2,1)} collective-permute-done((bf16[16,256,128]{2,0,1:T(8,128)(2,1)}, bf16[16,256,128]{2,0,1:T(8,128)(2,1)}, u32[]{:S(2)}, u32[]{:S(2)}) %collective-permute-start.10) | collective-permute-done | bytes 1048608 | tf_op jit(solution)/shard_map/ppermute | solution.py:64
  356.3 66.1 %collective-permute-done.9 = bf16[16,256,128]{2,0,1:T(8,128)(2,1)} collective-permute-done((bf16[16,256,128]{2,0,1:T(8,128)(2,1)}, bf16[16,256,128]{2,0,1:T(8,128)(2,1)}, u32[]{:S(2)}, u32[]{:S(2)}) %collective-permute-start.9) | collective-permute-done | bytes 1048608 | tf_op jit(solution)/shard_map/ppermute | solution.py:64
  439.0 42.4 %collective-permute-start.11 = (bf16[16,128,128]{1,2,0:T(8,128)(2,1)S(1)}, bf16[16,128,128]{1,2,0:T(8,128)(2,1)S(1)}, u32[]{:S(2)}, u32[]{:S(2)}) collective-permute-start(bf16[16,128,128]{1,2,0:T(8,128)(2,1)S(1)} %get-tuple-element.69), channel_id=1, source_target_pairs={{0,1},{1,2},{2,3},{3,4},{4,5},{5,6},{6,7},{7,0},{8,9},{9,10},{10,1... | collective-permute-start | bytes 1572872 | tf_op jit(solution)/shard_map/ppermute | solution.py:64
  481.4 30.7 %collective-permute-done.29 = bf16[16,256,128]{2,0,1:T(8,128)(2,1)S(1)} collective-permute-done((bf16[16,256,128]{2,0,1:T(8,128)(2,1)S(1)}, bf16[16,256,128]{2,0,1:T(8,128)(2,1)S(1)}, u32[]{:S(2)}, u32[]{:S(2)}) %collective-permute-start.29) | collective-permute-done | bytes 1048608 | tf_op jit(solution)/shard_map/ppermute | solution.py:64
  532.6 22.0 %collective-permute-done.13 = bf16[16,128,128]{1,2,0:T(8,128)(2,1)S(1)} collective-permute-done((bf16[16,128,128]{1,2,0:T(8,128)(2,1)S(1)}, bf16[16,128,128]{1,2,0:T(8,128)(2,1)S(1)}, u32[]{:S(2)}, u32[]{:S(2)}) %collective-permute-start.13) | collective-permute-done | bytes 524320 | tf_op jit(solution)/shard_map/ppermute | solution.py:64
  554.8 17.2 %collective-permute-start.33 = (bf16[16,128,128]{1,2,0:T(8,128)(2,1)}, bf16[16,128,128]{1,2,0:T(8,128)(2,1)}, u32[]{:S(2)}, u32[]{:S(2)}) collective-permute-start(bf16[16,128,128]{1,2,0:T(8,128)(2,1)} %get-tuple-element.43), channel_id=1, source_target_pairs={{0,3},{1,4},{2,5},{3,6},{4,7},{5,0},{6,1},{7,2},{8,11},{9,12},{10,... | collective-permute-start | bytes 1572872 | tf_op jit(solution)/shard_map/ppermute | solution.py:64
  579.4 13.4 %fusion.33 = bf16[16,128,1024]{2,1,0:T(8,128)(2,1)} fusion(f32[16]{0:T(128)S(1)} %copy-done.42, f32[128,1024]{1,0:T(8,128)} %broadcast_multiply_fusion, bf16[16,128,1024]{1,2,0:T(8,128)(2,1)} %copy-done.29, bf16[1024,1024]{1,0:T(8,128)(2,1)} %copy-done.8, bf16[1024,1024]{1,0:T(8,128)(2,1)S(1)} %copy-done.7), kind=kOutput, calls=%fused_computation.59 | convolution fusion | flops 8602517504 | bytes 13107264 | tf_op jit(solution)/shard_map/axk,jk->axj/dot_general | solution.py:147
  630.6 13.2 %fusion.30 = bf16[16,128,1024]{2,1,0:T(8,128)(2,1)} fusion(f32[16]{0:T(128)S(1)} %copy-done.41, f32[128,1024]{1,0:T(8,128)} %broadcast_multiply_fusion, bf16[16,128,1024]{1,2,0:T(8,128)(2,1)} %copy-done.28, bf16[1024,1024]{1,0:T(8,128)(2,1)} %copy-done.8, bf16[1024,1024]{1,0:T(8,128)(2,1)S(1)} %copy-done.7), kind=kOutput, calls=%fused_computation.57 | convolution fusion | flops 8602517504 | bytes 13107264 | tf_op jit(solution)/shard_map/axk,jk->axj/dot_general | solution.py:147
  680.2 15.4 %collective-permute-done.38 = bf16[16,128,128]{2,1,0:T(8,128)(2,1)S(1)} collective-permute-done((bf16[16,128,128]{2,1,0:T(8,128)(2,1)S(1)}, bf16[16,128,128]{2,1,0:T(8,128)(2,1)S(1)}, u32[]{:S(2)}, u32[]{:S(2)}) %collective-permute-start.38) | collective-permute-done | bytes 524320 | tf_op jit(solution)/shard_map/ppermute | solution.py:64
  717.1 59.2 %collective-permute-done.25 = bf16[16,256,128]{1,2,0:T(8,128)(2,1)S(1)} collective-permute-done((bf16[16,256,128]{1,2,0:T(8,128)(2,1)S(1)}, bf16[16,256,128]{1,2,0:T(8,128)(2,1)S(1)}, u32[]{:S(2)}, u32[]{:S(2)}) %collective-permute-start.25) | collective-permute-done | bytes 1048608 | tf_op jit(solution)/shard_map/ppermute | solution.py:64
  777.4 20.1 %collective-permute-done.26 = bf16[16,256,128]{1,2,0:T(8,128)(2,1)S(1)} collective-permute-done((bf16[16,256,128]{1,2,0:T(8,128)(2,1)S(1)}, bf16[16,256,128]{1,2,0:T(8,128)(2,1)S(1)}, u32[]{:S(2)}, u32[]{:S(2)}) %collective-permute-start.26) | collective-permute-done | bytes 1048608 | tf_op jit(solution)/shard_map/ppermute | solution.py:64
  805.3 23.9 %collective-permute-done.45 = bf16[16,256,128]{1,2,0:T(8,128)(2,1)S(1)} collective-permute-done((bf16[16,256,128]{1,2,0:T(8,128)(2,1)S(1)}, bf16[16,256,128]{1,2,0:T(8,128)(2,1)S(1)}, u32[]{:S(2)}, u32[]{:S(2)}) %collective-permute-start.45) | collective-permute-done | bytes 1048608 | tf_op jit(solution)/shard_map/ppermute | solution.py:64
  830.3 40.5 %collective-permute-done.46 = bf16[16,256,128]{1,2,0:T(8,128)(2,1)S(1)} collective-permute-done((bf16[16,256,128]{1,2,0:T(8,128)(2,1)S(1)}, bf16[16,256,128]{1,2,0:T(8,128)(2,1)S(1)}, u32[]{:S(2)}, u32[]{:S(2)}) %collective-permute-start.46) | collective-permute-done | bytes 1048608 | tf_op jit(solution)/shard_map/ppermute | solution.py:64
  872.9 13.5 %copy.153 = bf16[128,256,128]{0,2,1:T(8,128)(2,1)} copy(bf16[128,256,128]{1,2,0:T(8,128)(2,1)} %constant_dynamic-update-slice_fusion.28) | data formatting | bytes 16777216 | tf_op jit(solution)/shard_map/concatenate | solution.py:155
  893.6 23.9 %collective-permute-start.48 = (bf16[20,128,128]{2,1,0:T(8,128)(2,1)S(1)}, bf16[20,128,128]{2,1,0:T(8,128)(2,1)S(1)}, u32[]{:S(2)}, u32[]{:S(2)}) collective-permute-start(bf16[20,128,128]{2,1,0:T(8,128)(2,1)S(1)} %get-tuple-element.17), channel_id=1, source_target_pairs={{0,8},{8,16},{16,24},{1,9},{9,17},{17,25},{2,10},{10,18},{18,26},{... | collective-permute-start | bytes 1966088 | tf_op jit(solution)/shard_map/ppermute | solution.py:19
  927.8 17.4 %copy.155 = f32[256,128,128]{1,2,0:T(8,128)} copy(f32[256,128,128]{2,1,0:T(8,128)} %get-tuple-element.128) | data formatting | bytes 33554432 | tf_op jit(solution)/shard_map/kxy,zk->xyz/dot_general | solution.py:162
  956.6 23.8 %fusion.17 = bf16[256,128,128]{2,0,1:T(8,128)(2,1)} fusion(bf16[296,128,128]{2,1,0:T(8,128)(2,1)} %pad_maximum_fusion.2, f32[256,296]{0,1:T(8,128)S(1)} %copy-done.12), kind=kOutput, calls=%fused_computation.35 | convolution fusion | flops 7453278208 | bytes 18391040 | tf_op jit(solution)/shard_map/ic,cyz->iyz/dot_general | solution.py:44
  994.5 16.8 %fusion.7 = f32[256,128,128]{2,1,0:T(8,128)} fusion(bf16[256,128,128]{2,0,1:T(8,128)(2,1)} %fusion.17, f32[128,168]{0,1:T(8,128)S(1)} %copy-done.14), kind=kOutput, calls=%fused_computation.23 | convolution fusion | flops 3221225472 | bytes 25231360 | tf_op jit(solution)/shard_map/jc,xcz->xjz/dot_general | solution.py:44
  1012.0 21.0 %fusion.1 = (f32[]{:T(128)}, f32[256,128,128]{2,1,0:T(8,128)}) fusion(bf16[256,128,128]{1,2,0:T(8,128)(2,1)} %copy.125, f32[256,128,128]{2,1,0:T(8,128)} %fusion.7, f32[128,20]{0,1:T(8,128)S(1)} %copy-done.25, f32[128,20]{0,1:T(8,128)S(1)} %copy-done.23, bf16[256,40,128]{2,0,1:T(8,128)(2,1)S(1)} %pad_maximum_fusion.9), kind=kOutput, calls=%fused_computation.3 | convolution fusion | flops 1027609600 | bytes 44584964 | tf_op jit(solution)/shard_map/jc,xcz->xjz/dot_general | solution.py:44
  1033.1 45.3 %all-reduce = (f32[]{:T(128)}, f32[]{:T(128)}, f32[]{:T(128)}) all-reduce(f32[]{:T(128)} %multiply_reduce_fusion.1, f32[]{:T(128)} %get-tuple-element.125, f32[]{:T(128)} %get-tuple-element.127), channel_id=1, replica_groups=mesh['gx'=4,'gy'=8] {'gx','gy'}, use_global_device_ids=true, to_apply=%region_9.10 | all-reduce | flops 3 | bytes 24 | tf_op jit(solution)/shard_map/psum | solution.py:169
  1080.3 17.3 %multiply_add_fusion = f32[256,128,128]{1,2,0:T(8,128)} fusion(f32[256,128,128]{1,2,0:T(8,128)} %copy.161, f32[256,128,128]{1,2,0:T(8,128)} %copy.155, f32[]{:T(128)S(6)} %div.21), kind=kLoop, calls=%fused_computation.8 | loop fusion | flops 8388608 | bytes 50331652 | tf_op jit(solution)/shard_map/add | solution.py:176
  1101.7 12.4 %fusion.2 = f32[256,128,128]{1,2,0:T(8,128)} fusion(f32[256,128,128]{1,2,0:T(8,128)} %bitcast_subtract_fusion.1, f32[256,128,128]{2,1,0:T(8,128)S(1)} %copy-done.2, f32[]{:T(128)S(6)} %div.21), kind=kLoop, calls=%fused_computation.5 | loop fusion | flops 8388608 | bytes 50331652 | tf_op jit(solution)/shard_map/sub | solution.py:176
  1114.1 17.4 %copy.162 = f32[256,128,128]{2,1,0:T(8,128)} copy(f32[256,128,128]{1,2,0:T(8,128)} %multiply_add_fusion) | data formatting | bytes 33554432
  1131.5 17.4 %copy.163 = f32[256,128,128]{2,1,0:T(8,128)} copy(f32[256,128,128]{1,2,0:T(8,128)} %fusion.2) | data formatting | bytes 33554432
  (336 shorter events, 368.8 us)
Async XLA Ops:
  7.2 268.2 %all-gather.4.cloned.1.call-start = ((), (), s32[]{:S(2)}) async-start(), calls=%async_computation | async-start | bytes 2621440 | tf_op jit(solution)/shard_map/all_gather | solution.py:109
  7.9 279.4 %all-gather.6.cloned.1.call-start = ((), (), s32[]{:S(2)}) async-start(), calls=%async_computation.1 | async-start | bytes 2359296 | tf_op jit(solution)/shard_map/all_gather | solution.py:110
  26.4 38.8 %collective-permute-start = (bf16[20,128,128]{1,2,0:T(8,128)(2,1)S(1)}, bf16[20,128,128]{1,2,0:T(8,128)(2,1)S(1)}, u32[]{:S(2)}, u32[]{:S(2)}) collective-permute-start(bf16[20,128,128]{1,2,0:T(8,128)(2,1)S(1)} %get-tuple-element.25), channel_id=1, source_target_pairs={{0,8},{8,16},{16,24},{1,9},{9,17},{17,25},{2,10},{10,18},{18,26},{... | collective-permute-start | bytes 1966088 | tf_op jit(solution)/shard_map/ppermute | solution.py:19
  31.3 39.1 %collective-permute-start.1 = (bf16[20,128,128]{1,2,0:T(8,128)(2,1)S(1)}, bf16[20,128,128]{1,2,0:T(8,128)(2,1)S(1)}, u32[]{:S(2)}, u32[]{:S(2)}) collective-permute-start(bf16[20,128,128]{1,2,0:T(8,128)(2,1)S(1)} %get-tuple-element.26), channel_id=1, source_target_pairs={{8,0},{16,8},{24,16},{9,1},{17,9},{25,17},{10,2},{18,10},{26,18},{... | collective-permute-start | bytes 1966088 | tf_op jit(solution)/shard_map/ppermute | solution.py:22
  174.3 36.4 %collective-permute-start.4 = (bf16[20,128,128]{2,1,0:T(8,128)(2,1)S(1)}, bf16[20,128,128]{2,1,0:T(8,128)(2,1)S(1)}, u32[]{:S(2)}, u32[]{:S(2)}) collective-permute-start(bf16[20,128,128]{2,1,0:T(8,128)(2,1)S(1)} %get-tuple-element.21), channel_id=1, source_target_pairs={{0,8},{8,16},{16,24},{1,9},{9,17},{17,25},{2,10},{10,18},{18,26},{... | collective-permute-start | bytes 1966088 | tf_op jit(solution)/shard_map/ppermute | solution.py:19
  245.5 43.8 %collective-permute-start.6 = (bf16[256,20,128]{2,0,1:T(8,128)(2,1)}, bf16[256,20,128]{2,0,1:T(8,128)(2,1)S(1)}, u32[]{:S(2)}, u32[]{:S(2)}) collective-permute-start(bf16[256,20,128]{2,0,1:T(8,128)(2,1)} %get-tuple-element.19), channel_id=1, source_target_pairs={{0,1},{1,2},{2,3},{3,4},{4,5},{5,6},{6,7},{8,9},{9,10},{10,11},{11... | collective-permute-start | bytes 3932168 | tf_op jit(solution)/shard_map/ppermute | solution.py:19
  249.2 43.2 %collective-permute-start.7 = (bf16[256,20,128]{2,0,1:T(8,128)(2,1)S(1)}, bf16[256,20,128]{2,0,1:T(8,128)(2,1)}, u32[]{:S(2)}, u32[]{:S(2)}) collective-permute-start(bf16[256,20,128]{2,0,1:T(8,128)(2,1)S(1)} %get-tuple-element.20), channel_id=1, source_target_pairs={{1,0},{2,1},{3,2},{4,3},{5,4},{6,5},{7,6},{9,8},{10,9},{11,10},{12... | collective-permute-start | bytes 3932168 | tf_op jit(solution)/shard_map/ppermute | solution.py:22
  331.7 90.7 %collective-permute-start.9 = (bf16[16,256,128]{2,0,1:T(8,128)(2,1)}, bf16[16,256,128]{2,0,1:T(8,128)(2,1)}, u32[]{:S(2)}, u32[]{:S(2)}) collective-permute-start(bf16[16,256,128]{2,0,1:T(8,128)(2,1)} %get-tuple-element.73), channel_id=1, source_target_pairs={{0,16},{8,24},{16,0},{24,8},{1,17},{9,25},{17,1},{25,9},{2,18},{10... | collective-permute-start | bytes 3145736 | tf_op jit(solution)/shard_map/ppermute | solution.py:64
  332.3 90.1 %collective-permute-start.8 = (bf16[16,256,128]{2,0,1:T(8,128)(2,1)S(1)}, bf16[16,256,128]{2,0,1:T(8,128)(2,1)}, u32[]{:S(2)}, u32[]{:S(2)}) collective-permute-start(bf16[16,256,128]{2,0,1:T(8,128)(2,1)S(1)} %get-tuple-element.74), channel_id=1, source_target_pairs={{0,8},{8,16},{16,24},{24,0},{1,9},{9,17},{17,25},{25,1},{2,10},{10... | collective-permute-start | bytes 3145736 | tf_op jit(solution)/shard_map/ppermute | solution.py:64
  339.9 141.5 %collective-permute-start.30 = (bf16[16,256,128]{2,0,1:T(8,128)(2,1)S(1)}, bf16[16,256,128]{2,0,1:T(8,128)(2,1)S(1)}, u32[]{:S(2)}, u32[]{:S(2)}) collective-permute-start(bf16[16,256,128]{2,0,1:T(8,128)(2,1)S(1)} %get-tuple-element.48), channel_id=1, source_target_pairs={{0,24},{8,0},{16,8},{24,16},{1,25},{9,1},{17,9},{25,17},{2,26},{10... | collective-permute-start | bytes 3145736 | tf_op jit(solution)/shard_map/ppermute | solution.py:64
  342.4 169.6 %collective-permute-start.29 = (bf16[16,256,128]{2,0,1:T(8,128)(2,1)S(1)}, bf16[16,256,128]{2,0,1:T(8,128)(2,1)S(1)}, u32[]{:S(2)}, u32[]{:S(2)}) collective-permute-start(bf16[16,256,128]{2,0,1:T(8,128)(2,1)S(1)} %get-tuple-element.49), channel_id=1, source_target_pairs={{0,16},{8,24},{16,0},{24,8},{1,17},{9,25},{17,1},{25,9},{2,18},{10... | collective-permute-start | bytes 3145736 | tf_op jit(solution)/shard_map/ppermute | solution.py:64
  356.3 155.8 %collective-permute-start.28 = (bf16[16,256,128]{2,0,1:T(8,128)(2,1)S(1)}, bf16[16,256,128]{2,0,1:T(8,128)(2,1)S(1)}, u32[]{:S(2)}, u32[]{:S(2)}) collective-permute-start(bf16[16,256,128]{2,0,1:T(8,128)(2,1)S(1)} %get-tuple-element.50), channel_id=1, source_target_pairs={{0,8},{8,16},{16,24},{24,0},{1,9},{9,17},{17,25},{25,1},{2,10},{10... | collective-permute-start | bytes 3145736 | tf_op jit(solution)/shard_map/ppermute | solution.py:64
  433.0 99.4 %collective-permute-start.12 = (bf16[16,128,128]{1,2,0:T(8,128)(2,1)S(1)}, bf16[16,128,128]{1,2,0:T(8,128)(2,1)S(1)}, u32[]{:S(2)}, u32[]{:S(2)}) collective-permute-start(bf16[16,128,128]{1,2,0:T(8,128)(2,1)S(1)} %get-tuple-element.68), channel_id=1, source_target_pairs={{0,2},{1,3},{2,4},{3,5},{4,6},{5,7},{6,0},{7,1},{8,10},{9,11},{10,... | collective-permute-start | bytes 1572872 | tf_op jit(solution)/shard_map/ppermute | solution.py:64
  439.0 90.0 %collective-permute-start.11 = (bf16[16,128,128]{1,2,0:T(8,128)(2,1)S(1)}, bf16[16,128,128]{1,2,0:T(8,128)(2,1)S(1)}, u32[]{:S(2)}, u32[]{:S(2)}) collective-permute-start(bf16[16,128,128]{1,2,0:T(8,128)(2,1)S(1)} %get-tuple-element.69), channel_id=1, source_target_pairs={{0,1},{1,2},{2,3},{3,4},{4,5},{5,6},{6,7},{7,0},{8,9},{9,10},{10,1... | collective-permute-start | bytes 1572872 | tf_op jit(solution)/shard_map/ppermute | solution.py:64
  520.1 34.7 %collective-permute-start.15 = (bf16[16,128,128]{1,2,0:T(8,128)(2,1)S(1)}, bf16[16,128,128]{1,2,0:T(8,128)(2,1)S(1)}, u32[]{:S(2)}, u32[]{:S(2)}) collective-permute-start(bf16[16,128,128]{1,2,0:T(8,128)(2,1)S(1)} %get-tuple-element.65), channel_id=1, source_target_pairs={{0,5},{1,6},{2,7},{3,0},{4,1},{5,2},{6,3},{7,4},{8,13},{9,14},{10,... | collective-permute-start | bytes 1572872 | tf_op jit(solution)/shard_map/ppermute | solution.py:64
  529.0 43.1 %collective-permute-start.16 = (bf16[16,128,128]{1,2,0:T(8,128)(2,1)S(1)}, bf16[16,128,128]{1,2,0:T(8,128)(2,1)S(1)}, u32[]{:S(2)}, u32[]{:S(2)}) collective-permute-start(bf16[16,128,128]{1,2,0:T(8,128)(2,1)S(1)} %get-tuple-element.64), channel_id=1, source_target_pairs={{0,6},{1,7},{2,0},{3,1},{4,2},{5,3},{6,4},{7,5},{8,14},{9,15},{10,... | collective-permute-start | bytes 1572872 | tf_op jit(solution)/shard_map/ppermute | solution.py:64
  532.4 44.8 %collective-permute-start.17 = (bf16[16,128,128]{1,2,0:T(8,128)(2,1)S(1)}, bf16[16,128,128]{1,2,0:T(8,128)(2,1)S(1)}, u32[]{:S(2)}, u32[]{:S(2)}) collective-permute-start(bf16[16,128,128]{1,2,0:T(8,128)(2,1)S(1)} %get-tuple-element.63), channel_id=1, source_target_pairs={{0,7},{1,0},{2,1},{3,2},{4,3},{5,4},{6,5},{7,6},{8,15},{9,8},{10,9... | collective-permute-start | bytes 1572872 | tf_op jit(solution)/shard_map/ppermute | solution.py:64
  554.6 58.9 %collective-permute-start.35 = (bf16[16,128,128]{1,2,0:T(8,128)(2,1)}, bf16[16,128,128]{1,2,0:T(8,128)(2,1)}, u32[]{:S(2)}, u32[]{:S(2)}) collective-permute-start(bf16[16,128,128]{1,2,0:T(8,128)(2,1)} %get-tuple-element.41), channel_id=1, source_target_pairs={{0,5},{1,6},{2,7},{3,0},{4,1},{5,2},{6,3},{7,4},{8,13},{9,14},{10,... | collective-permute-start | bytes 1572872 | tf_op jit(solution)/shard_map/ppermute | solution.py:64
  554.7 57.1 %collective-permute-start.34 = (bf16[16,128,128]{1,2,0:T(8,128)(2,1)}, bf16[16,128,128]{1,2,0:T(8,128)(2,1)}, u32[]{:S(2)}, u32[]{:S(2)}) collective-permute-start(bf16[16,128,128]{1,2,0:T(8,128)(2,1)} %get-tuple-element.42), channel_id=1, source_target_pairs={{0,4},{1,5},{2,6},{3,7},{4,0},{5,1},{6,2},{7,3},{8,12},{9,13},{10,... | collective-permute-start | bytes 1572872 | tf_op jit(solution)/shard_map/ppermute | solution.py:64
  554.8 55.8 %collective-permute-start.33 = (bf16[16,128,128]{1,2,0:T(8,128)(2,1)}, bf16[16,128,128]{1,2,0:T(8,128)(2,1)}, u32[]{:S(2)}, u32[]{:S(2)}) collective-permute-start(bf16[16,128,128]{1,2,0:T(8,128)(2,1)} %get-tuple-element.43), channel_id=1, source_target_pairs={{0,3},{1,4},{2,5},{3,6},{4,7},{5,0},{6,1},{7,2},{8,11},{9,12},{10,... | collective-permute-start | bytes 1572872 | tf_op jit(solution)/shard_map/ppermute | solution.py:64
  610.7 51.0 %collective-permute-start.22 = (bf16[16,128,128]{2,1,0:T(8,128)(2,1)}, bf16[16,128,128]{2,1,0:T(8,128)(2,1)}, u32[]{:S(2)}, u32[]{:S(2)}) collective-permute-start(bf16[16,128,128]{2,1,0:T(8,128)(2,1)} %get-tuple-element.57), channel_id=1, source_target_pairs={{0,5},{1,6},{2,7},{3,0},{4,1},{5,2},{6,3},{7,4},{8,13},{9,14},{10,... | collective-permute-start | bytes 1572872 | tf_op jit(solution)/shard_map/ppermute | solution.py:64
  611.8 47.1 %collective-permute-start.21 = (bf16[16,128,128]{2,1,0:T(8,128)(2,1)}, bf16[16,128,128]{2,1,0:T(8,128)(2,1)}, u32[]{:S(2)}, u32[]{:S(2)}) collective-permute-start(bf16[16,128,128]{2,1,0:T(8,128)(2,1)} %get-tuple-element.58), channel_id=1, source_target_pairs={{0,4},{1,5},{2,6},{3,7},{4,0},{5,1},{6,2},{7,3},{8,12},{9,13},{10,... | collective-permute-start | bytes 1572872 | tf_op jit(solution)/shard_map/ppermute | solution.py:64
  613.5 44.2 %collective-permute-start.20 = (bf16[16,128,128]{2,1,0:T(8,128)(2,1)}, bf16[16,128,128]{2,1,0:T(8,128)(2,1)}, u32[]{:S(2)}, u32[]{:S(2)}) collective-permute-start(bf16[16,128,128]{2,1,0:T(8,128)(2,1)} %get-tuple-element.59), channel_id=1, source_target_pairs={{0,3},{1,4},{2,5},{3,6},{4,7},{5,0},{6,1},{7,2},{8,11},{9,12},{10,... | collective-permute-start | bytes 1572872 | tf_op jit(solution)/shard_map/ppermute | solution.py:64
  657.7 51.1 %collective-permute-start.42 = (bf16[16,128,128]{2,1,0:T(8,128)(2,1)S(1)}, bf16[16,128,128]{2,1,0:T(8,128)(2,1)S(1)}, u32[]{:S(2)}, u32[]{:S(2)}) collective-permute-start(bf16[16,128,128]{2,1,0:T(8,128)(2,1)S(1)} %get-tuple-element.33), channel_id=1, source_target_pairs={{0,5},{1,6},{2,7},{3,0},{4,1},{5,2},{6,3},{7,4},{8,13},{9,14},{10,... | collective-permute-start | bytes 1572872 | tf_op jit(solution)/shard_map/ppermute | solution.py:64
  658.9 46.8 %collective-permute-start.41 = (bf16[16,128,128]{2,1,0:T(8,128)(2,1)S(1)}, bf16[16,128,128]{2,1,0:T(8,128)(2,1)S(1)}, u32[]{:S(2)}, u32[]{:S(2)}) collective-permute-start(bf16[16,128,128]{2,1,0:T(8,128)(2,1)S(1)} %get-tuple-element.34), channel_id=1, source_target_pairs={{0,4},{1,5},{2,6},{3,7},{4,0},{5,1},{6,2},{7,3},{8,12},{9,13},{10,... | collective-permute-start | bytes 1572872 | tf_op jit(solution)/shard_map/ppermute | solution.py:64
  661.6 43.9 %collective-permute-start.40 = (bf16[16,128,128]{2,1,0:T(8,128)(2,1)S(1)}, bf16[16,128,128]{2,1,0:T(8,128)(2,1)S(1)}, u32[]{:S(2)}, u32[]{:S(2)}) collective-permute-start(bf16[16,128,128]{2,1,0:T(8,128)(2,1)S(1)} %get-tuple-element.35), channel_id=1, source_target_pairs={{0,3},{1,4},{2,5},{3,6},{4,7},{5,0},{6,1},{7,2},{8,11},{9,12},{10,... | collective-permute-start | bytes 1572872 | tf_op jit(solution)/shard_map/ppermute | solution.py:64
  705.6 93.1 %collective-permute-start.27 = (bf16[16,256,128]{1,2,0:T(8,128)(2,1)S(1)}, bf16[16,256,128]{1,2,0:T(8,128)(2,1)S(1)}, u32[]{:S(2)}, u32[]{:S(2)}) collective-permute-start(bf16[16,256,128]{1,2,0:T(8,128)(2,1)S(1)} %get-tuple-element.51), channel_id=1, source_target_pairs={{0,24},{8,0},{16,8},{24,16},{1,25},{9,1},{17,9},{25,17},{2,26},{10... | collective-permute-start | bytes 3145736 | tf_op jit(solution)/shard_map/ppermute | solution.py:64
  705.7 91.9 %collective-permute-start.26 = (bf16[16,256,128]{1,2,0:T(8,128)(2,1)S(1)}, bf16[16,256,128]{1,2,0:T(8,128)(2,1)S(1)}, u32[]{:S(2)}, u32[]{:S(2)}) collective-permute-start(bf16[16,256,128]{1,2,0:T(8,128)(2,1)S(1)} %get-tuple-element.52), channel_id=1, source_target_pairs={{0,16},{8,24},{16,0},{24,8},{1,17},{9,25},{17,1},{25,9},{2,18},{10... | collective-permute-start | bytes 3145736 | tf_op jit(solution)/shard_map/ppermute | solution.py:64
  708.8 67.5 %collective-permute-start.25 = (bf16[16,256,128]{1,2,0:T(8,128)(2,1)S(1)}, bf16[16,256,128]{1,2,0:T(8,128)(2,1)S(1)}, u32[]{:S(2)}, u32[]{:S(2)}) collective-permute-start(bf16[16,256,128]{1,2,0:T(8,128)(2,1)S(1)} %get-tuple-element.53), channel_id=1, source_target_pairs={{0,8},{8,16},{16,24},{24,0},{1,9},{9,17},{17,25},{25,1},{2,10},{10... | collective-permute-start | bytes 3145736 | tf_op jit(solution)/shard_map/ppermute | solution.py:64
  801.2 69.5 %collective-permute-start.46 = (bf16[16,256,128]{1,2,0:T(8,128)(2,1)S(1)}, bf16[16,256,128]{1,2,0:T(8,128)(2,1)S(1)}, u32[]{:S(2)}, u32[]{:S(2)}) collective-permute-start(bf16[16,256,128]{1,2,0:T(8,128)(2,1)S(1)} %get-tuple-element.28), channel_id=1, source_target_pairs={{0,16},{8,24},{16,0},{24,8},{1,17},{9,25},{17,1},{25,9},{2,18},{10... | collective-permute-start | bytes 3145736 | tf_op jit(solution)/shard_map/ppermute | solution.py:64
  802.1 69.7 %collective-permute-start.47 = (bf16[16,256,128]{1,2,0:T(8,128)(2,1)S(1)}, bf16[16,256,128]{1,2,0:T(8,128)(2,1)S(1)}, u32[]{:S(2)}, u32[]{:S(2)}) collective-permute-start(bf16[16,256,128]{1,2,0:T(8,128)(2,1)S(1)} %get-tuple-element.27), channel_id=1, source_target_pairs={{0,24},{8,0},{16,8},{24,16},{1,25},{9,1},{17,9},{25,17},{2,26},{10... | collective-permute-start | bytes 3145736 | tf_op jit(solution)/shard_map/ppermute | solution.py:64
  893.6 51.6 %collective-permute-start.48 = (bf16[20,128,128]{2,1,0:T(8,128)(2,1)S(1)}, bf16[20,128,128]{2,1,0:T(8,128)(2,1)S(1)}, u32[]{:S(2)}, u32[]{:S(2)}) collective-permute-start(bf16[20,128,128]{2,1,0:T(8,128)(2,1)S(1)} %get-tuple-element.17), channel_id=1, source_target_pairs={{0,8},{8,16},{16,24},{1,9},{9,17},{17,25},{2,10},{10,18},{18,26},{... | collective-permute-start | bytes 1966088 | tf_op jit(solution)/shard_map/ppermute | solution.py:19
  (72 other events, 1614.5 us)
Sparse Core Ops, SparseCore 0:
  9.6 59.0 all-gather.3
  70.6 30.1 all-gather.5
where the time goes:
time: 1160 us
  waiting for transfers between devices  341 us (29%)
  matrix products  298 us (26%)
  local copies, waits for them, and re-layouts  201 us (17%)
  starting transfers between devices  157 us (14%)
  other arithmetic  85.1 us (7%)
  blocking collectives  56 us (5%)
  between operations  17.8 us (2%)
    ppermute x40, waiting for transfers between devices, swap(): arrived.append(lax.ppermute(pieces[step], axis_name, pairs))  335 us
    dot_general x9, matrix products, split_dot(): jnp.einsum(spec, matrix, block.astype(jnp.float32), precision=lax.Precisi...  187 us
    unnamed x163, local copies, waits for them, and re-layouts  118 us
    ppermute x40, starting transfers between devices, swap(): arrived.append(lax.ppermute(pieces[step], axis_name, pairs))  109 us
    psum x1, blocking collectives, shards(): descent = lax.psum(local_descent, ('gx', 'gy'))  45.3 us
    ppermute x6, starting transfers between devices, exchange(): lax.ppermute(lax.slice_in_dim(block, block.shape[dim] - width, None, axis...  39.9 us
    dot_general x2, matrix products, apply_blur(): jnp.einsum('xyc,zc->xyz', source, z_matrix, precision=lax.Precision.HIGH)  31.4 us
    concatenate x3, other arithmetic, blur_xy(): extended = jnp.concatenate([low, along_z, high], axis=0)  28.3 us
  transfers between devices with their start and end apart: 54, of which 20 were waited for; matrix products, arithmetic and copies ran while one was open for 33% of the time, Pallas kernels for 0%

commit v1 on v0

--- a/solution.py
+++ b/solution.py
@@ -1,6 +1,10 @@
+import functools
+
 import jax
 import jax.numpy as jnp
 from jax import lax
+from jax.experimental import pallas as pl
+from jax.experimental.pallas import tpu as pltpu
 from jax.sharding import PartitionSpec as P
 
 HALF = 16
@@ -87,29 +91,210 @@
     return blur_xy(along_z.astype(jnp.bfloat16), kernels, offsets)
 
 
-def shards(
-    observed,
-    confidence,
-    iterate,
-    kernel_bank,
-    tap_index,
-    offsets,
-    basis_x,
-    basis_y,
-    basis_z,
-    eigen_x,
-    eigen_y,
-    eigen_z,
+MESH_ID = pl.DeviceIdType.MESH
+PARTS = 4
+
+
+def transform_kernel(
+    parts, size_x, size_y,
+    section_ref, x_fwd, x_inv, y_fwd, y_inv, eigen_xy, eigen_z,
+    out_ref,
+    lines_x, lines_y, lines_back, send_a, send_b, send_c, modes,
+    fs, fr, gs, gr, hs, hr, bs, br, fl, gl, hl, bl,
 ):
-    kernels = kernels_of(kernel_bank, tap_index)
-    adjoint_kernels = kernels[:, ::-1]
-    weights = confidence.astype(jnp.float32)
-    misfit = observed.astype(jnp.float32) - apply_blur(iterate, kernels, offsets)
-    gradient = apply_blur(weights * misfit, adjoint_kernels, -offsets) - tikhonov * iterate
-    full_x = lax.all_gather(basis_x, "gx", axis=0, tiled=True)
-    full_y = lax.all_gather(basis_y, "gy", axis=0, tiled=True)
-
-    gradient_b = gradient.astype(jnp.bfloat16)
+    me_x = lax.axis_index("gx")
+    me_y = lax.axis_index("gy")
+    depth = lines_x.shape[0]
+    full = lines_x.shape[1]
+    block_y = lines_x.shape[2]
+    block_x = section_ref.shape[1]
+    share = lines_y.shape[1]
+    full_y = lines_y.shape[2]
+    part = depth // parts
+    slots = send_a.shape[0]
+
+    barrier = pltpu.get_barrier_semaphore()
+    for step in range(1, size_x):
+        pl.semaphore_signal(
+            barrier, inc=1, device_id=(lax.rem(me_x + step, size_x), me_y), device_id_type=MESH_ID
+        )
+    for step in range(1, size_y):
+        pl.semaphore_signal(
+            barrier, inc=1, device_id=(me_x, lax.rem(me_y + step, size_y)), device_id_type=MESH_ID
+        )
+    pl.semaphore_wait(barrier, size_x + size_y - 2)
+
+    def copies(kind, c):
+        out = []
+        here = pl.ds(c * part, part)
+        slot = c % slots
+        count = size_x if kind in "fb" else size_y
+        for step in range(count):
+            mine = step == 0
+            if kind in "fb":
+                peer = lax.rem(me_x + step, size_x)
+                target = (peer, me_y)
+            else:
+                peer = lax.rem(me_y + step, size_y)
+                target = (me_x, peer)
+            if kind == "f":
+                src = section_ref.at[pl.ds(peer * depth + c * part, part)]
+                dst = lines_x.at[here, pl.ds(me_x * block_x, block_x)]
+                sems = fs, fr, fl
+            elif kind == "g":
+                src = send_a.at[slot, :, pl.ds(peer * share, share)]
+                dst = lines_y.at[here, :, pl.ds(me_y * block_y, block_y)]
+                sems = gs, gr, gl
+            elif kind == "h":
+                src = send_b.at[slot, :, :, pl.ds(peer * block_y, block_y)]
+                dst = lines_back.at[here, pl.ds(me_y * share, share)]
+                sems = hs, hr, hl
+            else:
+                src = send_c.at[slot, :, pl.ds(peer * block_x, block_x)]
+                dst = out_ref.at[pl.ds(me_x * depth + c * part, part)]
+                sems = bs, br, bl
+            if mine:
+                out.append(pltpu.make_async_copy(src, dst, sems[2].at[c]))
+            else:
+                out.append(
+                    pltpu.make_async_remote_copy(
+                        src, dst, sems[0].at[c, step], sems[1].at[c, step],
+                        device_id=target, device_id_type=MESH_ID,
+                    )
+                )
+        return out
+
+    every = {kind: [copies(kind, c) for c in range(parts)] for kind in "fghb"}
+
+    def start(kind, c):
+        group = every[kind][c]
+        for copy in group[1:] + group[:1]:
+            copy.start()
+
+    def landed(kind, c):
+        group = every[kind][c]
+        if kind != "b":
+            group[0].wait()
+        for copy in group[1:]:
+            copy.wait_recv()
+
+    def sent(kind, c):
+        group = every[kind][c]
+        if kind == "b":
+            group[0].wait()
+        for copy in group[1:]:
+            copy.wait_send()
+
+    def along_x(matrix, lines, out, c):
+        def pair(i, carry):
+            k = c * part + 2 * i
+            both = jnp.concatenate([lines[k], lines[k + 1]], axis=1)
+            for b in range(0, full, 256):
+                found = jnp.dot(
+                    matrix[pl.ds(b, 256), :], both, preferred_element_type=jnp.float32
+                ).astype(jnp.bfloat16)
+                out[c % slots, 2 * i, pl.ds(b, 256)] = found[:, :block_y]
+                out[c % slots, 2 * i + 1, pl.ds(b, 256)] = found[:, block_y:]
+            return carry
+
+        lax.fori_loop(0, part // 2, pair, 0)
+
+    def along_y(c):
+        def pair(i, carry):
+            k = c * part + 2 * i
+            rows = jnp.concatenate([lines_y[k], lines_y[k + 1]], axis=0)
+            for b in range(0, full_y, 256):
+                found = jnp.dot(rows, y_fwd[:, pl.ds(b, 256)], preferred_element_type=jnp.float32)
+                weight = eigen_xy[:, pl.ds(b, 256)]
+                modes[pl.ds(0, share), pl.ds(b, 256)] = (
+                    found[:share] / (weight * eigen_z[k] + tikhonov)
+                ).astype(jnp.bfloat16)
+                modes[pl.ds(share, share), pl.ds(b, 256)] = (
+                    found[share:] / (weight * eigen_z[k + 1] + tikhonov)
+                ).astype(jnp.bfloat16)
+            for b in range(0, full_y, 256):
+                found = jnp.dot(
+                    modes[...], y_inv[:, pl.ds(b, 256)], preferred_element_type=jnp.float32
+                ).astype(jnp.bfloat16)
+                send_b[c % slots, 2 * i, :, pl.ds(b, 256)] = found[:share]
+                send_b[c % slots, 2 * i + 1, :, pl.ds(b, 256)] = found[share:]
+            return carry
+
+        lax.fori_loop(0, part // 2, pair, 0)
+
+    ahead = min(2, parts)
+    for c in range(ahead):
+        start("f", c)
+    for step in range(parts + 2):
+        c = step
+        if c < parts:
+            landed("f", c)
+            if c + ahead < parts:
+                start("f", c + ahead)
+            if c >= slots:
+                sent("g", c - slots)
+            along_x(x_fwd, lines_x, send_a, c)
+            start("g", c)
+        c = step - 1
+        if 0 <= c < parts:
+            landed("g", c)
+            if c >= slots:
+                sent("h", c - slots)
+            along_y(c)
+            start("h", c)
+        c = step - 2
+        if 0 <= c < parts:
+            landed("h", c)
+            if c >= slots:
+                sent("b", c - slots)
+            along_x(x_inv, lines_back, send_c, c)
+            start("b", c)
+    for c in range(parts):
+        landed("b", c)
+        sent("f", c)
+        if c >= parts - slots:
+            sent("g", c)
+            sent("h", c)
+            sent("b", c)
+
+
+def transform(section, x_fwd, x_inv, y_fwd, y_inv, eigen_xy, eigen_z, size_x, size_y):
+    modes_z, block_x, block_y = section.shape
+    depth = modes_z // size_x
+    full_x, full_y = x_fwd.shape[0], y_fwd.shape[0]
+    share = full_x // size_y
+    parts = PARTS
+    part = depth // parts
+    slots = 2
+    vmem = pl.BlockSpec(memory_space=pltpu.VMEM)
+    sem = lambda n: pltpu.SemaphoreType.DMA((parts, n))
+    one = pltpu.SemaphoreType.DMA((parts,))
+    bf = jnp.bfloat16
+    return pl.pallas_call(
+        functools.partial(transform_kernel, parts, size_x, size_y),
+        out_shape=jax.ShapeDtypeStruct(section.shape, bf),
+        in_specs=[pl.BlockSpec(memory_space=pl.ANY)] + [vmem] * 5
+        + [pl.BlockSpec(memory_space=pltpu.SMEM)],
+        out_specs=pl.BlockSpec(memory_space=pl.ANY),
+        scratch_shapes=[
+            pltpu.VMEM((depth, full_x, block_y), bf),
+            pltpu.VMEM((depth, share, full_y), bf),
+            pltpu.VMEM((depth, full_x, block_y), bf),
+            pltpu.VMEM((slots, part, full_x, block_y), bf),
+            pltpu.VMEM((slots, part, share, full_y), bf),
+            pltpu.VMEM((slots, part, full_x, block_y), bf),
+            pltpu.VMEM((2 * share, full_y), bf),
+            sem(size_x), sem(size_x), sem(size_y), sem(size_y),
+            sem(size_y), sem(size_y), sem(size_x), sem(size_x),
+            one, one, one, one,
+        ],
+        compiler_params=pltpu.CompilerParams(
+            collective_id=0, has_side_effects=True, vmem_limit_bytes=60 * 2**20
+        ),
+    )(section, x_fwd, x_inv, y_fwd, y_inv, eigen_xy, eigen_z)
+
+
+def modes_by_permutes(gradient_b, full_x, full_y, basis_z, eigen_x, eigen_y, eigen_z):
     gx_size = lax.axis_size("gx")
     depth = basis_z.shape[0]
     share_z = depth // gx_size
@@ -159,6 +344,67 @@
         .transpose(0, 2, 1, 3)
         .reshape(depth, depth)
     )
+    return section_six, basis_z
+
+
+def kernel_fits(block, size_x, size_y):
+    block_x, block_y, depth = block
+    return (
+        block_y == 128
+        and depth == 128
+        and block_x % 128 == 0
+        and depth // size_x % (2 * PARTS) == 0
+        and block_x * size_x // size_y == 128
+        and block_y * size_y % 256 == 0
+    )
+
+
+def modes_by_kernel(gradient_b, full_x, full_y, basis_z, eigen_x, eigen_y, eigen_z):
+    size_x, size_y = lax.axis_size("gx"), lax.axis_size("gy")
+    section_one = jnp.einsum(
+        "zk,xyz->kxy", basis_z, gradient_b, preferred_element_type=jnp.float32
+    ).astype(jnp.bfloat16)
+    all_x = lax.all_gather(eigen_x, "gx", axis=0, tiled=True)
+    share_x = all_x.shape[0] // size_y
+    part_x = lax.dynamic_slice_in_dim(all_x, lax.axis_index("gy") * share_x, share_x)
+    share_z = eigen_z.shape[0] // size_x
+    part_z = lax.dynamic_slice_in_dim(eigen_z, lax.axis_index("gx") * share_z, share_z)
+    section_six = transform(
+        section_one, full_x.T, full_x, full_y, full_y.T,
+        part_x[:, None] * eigen_y[None, :], part_z, size_x, size_y,
+    )
+    return section_six, basis_z
+
+
+def shards(
+    observed,
+    confidence,
+    iterate,
+    kernel_bank,
+    tap_index,
+    offsets,
+    basis_x,
+    basis_y,
+    basis_z,
+    eigen_x,
+    eigen_y,
+    eigen_z,
+):
+    kernels = kernels_of(kernel_bank, tap_index)
+    adjoint_kernels = kernels[:, ::-1]
+    weights = confidence.astype(jnp.float32)
+    misfit = observed.astype(jnp.float32) - apply_blur(iterate, kernels, offsets)
+    gradient = apply_blur(weights * misfit, adjoint_kernels, -offsets) - tikhonov * iterate
+    full_x = lax.all_gather(basis_x, "gx", axis=0, tiled=True)
+    full_y = lax.all_gather(basis_y, "gy", axis=0, tiled=True)
+
+    gradient_b = gradient.astype(jnp.bfloat16)
+    fits = kernel_fits(gradient.shape, lax.axis_size("gx"), lax.axis_size("gy"))
+    find_modes = modes_by_kernel if fits else modes_by_permutes
+    section_six, basis_z = find_modes(
+        gradient_b, full_x, full_y, basis_z, eigen_x, eigen_y, eigen_z
+    )
+    depth = basis_z.shape[0]
     direction = jnp.einsum("kxy,zk->xyz", section_six, basis_z, preferred_element_type=jnp.float32)
     z_matrix = band_matrix(kernels[2], offsets[2], depth, depth, 0)
     z_modes = jnp.dot(z_matrix, basis_z.astype(jnp.float32), precision=highest)

time: 1160 us -> 1010 us (0.87)
  Pallas kernels: 0 us -> 361 us
  waiting for transfers between devices: 341 us -> 47.4 us
  starting transfers between devices: 157 us -> 33.4 us
  matrix products: 298 us -> 238 us
  local copies, waits for them, and re-layouts: 201 us -> 160 us
    pallas_call x0 -> x1, Pallas kernels: none -> 361 us  [transform(): pl.pallas_call(functools.partial(transform_kernel, parts, size_x, size_y)...]
    ppermute x40 -> x0, waiting for transfers between devices: 335 us -> none  [swap(): arrived.append(lax.ppermute(pieces[step], axis_name, pairs))]
    ppermute x40 -> x0, starting transfers between devices: 109 us -> none  [swap(): arrived.append(lax.ppermute(pieces[step], axis_name, pairs))]
    dot_general x8 -> x1, matrix products: 63.6 us -> 11.4 us  [modes_by_kernel(): jnp.einsum('zk,xyz->kxy', basis_z, gradient_b, preferred_element_type=jnp...]
    unnamed x163 -> x56, local copies, waits for them, and re-layouts: 118 us -> 84.4 us
    ppermute x6, waiting for transfers between devices: 0.02 us -> 31.5 us  [exchange(): lax.ppermute(lax.slice_in_dim(block, block.shape[dim] - width, None, axis...]
    split x8 -> x0, local copies, waits for them, and re-layouts: 22.7 us -> none  [swap(): pieces = jnp.split(block, count, axis=split)]
    sub x1, other arithmetic: 12.4 us -> 34.1 us  [shards(): return (iterate + step_size * direction, misfit - step_size * blurred)]
  transfers between devices with their start and end apart: 54 -> 14, of which waited for: 20 -> 4; matrix products, arithmetic and copies ran while one was open for 33% -> 28% of each run, Pallas kernels for 0% -> 0%
where the time goes in v1:
time: 1010 us; the launch traced here: 999 us
  Pallas kernels  361 us (36%)
  matrix products  238 us (24%)
  local copies, waits for them, and re-layouts  160 us (16%)
  other arithmetic  87 us (9%)
  blocking collectives  54.9 us (5%)
  waiting for transfers between devices  47.4 us (5%)
  starting transfers between devices  33.4 us (3%)
  between operations  17 us (2%)
    pallas_call x1, Pallas kernels, transform(): pl.pallas_call(functools.partial(transform_kernel, parts, size_x, size_y)...  361 us
    dot_general x9, matrix products, split_dot(): jnp.einsum(spec, matrix, block.astype(jnp.float32), precision=lax.Precisi...  179 us
    unnamed x56, local copies, waits for them, and re-layouts  84.4 us
    psum x1, blocking collectives, shards(): descent = lax.psum(local_descent, ('gx', 'gy'))  44.7 us
    sub x1, other arithmetic, shards(): return (iterate + step_size * direction, misfit - step_size * blurred)  34.1 us
    ppermute x6, waiting for transfers between devices, exchange(): lax.ppermute(lax.slice_in_dim(block, block.shape[dim] - width, None, axis...  31.5 us
    dot_general x2, matrix products, apply_blur(): jnp.einsum('xyc,zc->xyz', source, z_matrix, precision=lax.Precision.HIGH)  31.4 us
    concatenate x3, other arithmetic, blur_xy(): extended = jnp.concatenate([low, along_z, high], axis=0)  28.2 us
  transfers between devices with their start and end apart: 14, of which 4 were waited for; matrix products, arithmetic and copies ran while one was open for 28% of the time, Pallas kernels for 0%

profile of v1, /device:TPU:0, one launch (start us, length us, event | category | flops | bytes accessed | tf_op | source)
XLA Modules:
  0.0 998.7 jit_solution(14767576736108170844)
XLA Ops:
  11.3 11.0 %convert_bitcast_fusion.1 = bf16[256,128,128]{1,2,0:T(8,128)(2,1)S(1)} fusion(f32[256,128,128]{2,1,0:T(8,128)} %param.14, f32[128,128]{1,0:T(8,128)S(1)} %select_reduce_fusion.5), kind=kOutput, calls=%fused_computation.32 | convolution fusion | flops 3225419776 | bytes 25231360 | tf_op jit(solution)/shard_map/xyc,zc->xyz/dot_general | solution.py:90
  38.8 20.6 %collective-permute-done = bf16[20,128,128]{1,2,0:T(8,128)(2,1)S(1)} collective-permute-done((bf16[20,128,128]{1,2,0:T(8,128)(2,1)S(1)}, bf16[20,128,128]{1,2,0:T(8,128)(2,1)S(1)}, u32[]{:S(2)}, u32[]{:S(2)}) %collective-permute-start) | collective-permute-done | bytes 655392 | tf_op jit(solution)/shard_map/ppermute | solution.py:23
  59.4 11.0 %collective-permute-done.1 = bf16[20,128,128]{1,2,0:T(8,128)(2,1)S(1)} collective-permute-done((bf16[20,128,128]{1,2,0:T(8,128)(2,1)S(1)}, bf16[20,128,128]{1,2,0:T(8,128)(2,1)S(1)}, u32[]{:S(2)}, u32[]{:S(2)}) %collective-permute-start.1) | collective-permute-done | bytes 655392 | tf_op jit(solution)/shard_map/ppermute | solution.py:26
  70.5 10.1 %pad_maximum_fusion = bf16[296,128,128]{1,2,0:T(8,128)(2,1)} fusion(bf16[20,128,128]{1,2,0:T(8,128)(2,1)S(1)} %collective-permute-done.1, bf16[256,128,128]{1,2,0:T(8,128)(2,1)} %copy-done.4, bf16[20,128,128]{1,2,0:T(8,128)(2,1)S(1)} %collective-permute-done), kind=kLoop, calls=%fused_computation.15 | loop fusion | flops 9699328 | bytes 19398656 | tf_op jit(solution)/shard_map/concatenate | solution.py:78
  80.5 14.1 %copy.73 = bf16[296,128,128]{2,0,1:T(8,128)(2,1)} copy(bf16[296,128,128]{1,2,0:T(8,128)(2,1)} %pad_maximum_fusion) | data formatting | bytes 19398656 | tf_op jit(solution)/shard_map/concatenate | solution.py:78
  94.7 11.6 %convolution_convert_fusion.1 = bf16[256,128,128]{2,0,1:T(8,128)(2,1)S(1)} fusion(bf16[296,128,128]{2,0,1:T(8,128)(2,1)} %copy.73, f32[256,296]{0,1:T(8,128)S(1)} %select_reduce_fusion), kind=kOutput, calls=%fused_computation.37 | convolution fusion | flops 7453278208 | bytes 18391040 | tf_op jit(solution)/shard_map/ic,cyz->iyz/dot_general | solution.py:48
  115.1 17.4 %copy.95 = f32[256,128,128]{1,2,0:T(8,128)} copy(f32[256,128,128]{2,1,0:T(8,128)} %param.14) | data formatting | bytes 33554432 | tf_op args[2]
  133.8 12.0 %copy.71 = bf16[256,128,128]{1,2,0:T(8,128)(2,1)} copy(bf16[256,128,128]{2,1,0:T(8,128)(2,1)} %param.13) | data formatting | bytes 16777216 | tf_op args[1]
  145.8 11.4 %copy.72 = bf16[256,128,128]{1,2,0:T(8,128)(2,1)} copy(bf16[256,128,128]{2,1,0:T(8,128)(2,1)} %param.12) | data formatting | bytes 16777216 | tf_op args[0]
  157.8 10.2 %all-gather = f32[4,1,256]{2,1,0:T(1,128)S(1)} all-gather(f32[1,1,256]{2,1,0:T(1,128)S(1)} %bitcast.90), channel_id=1, replica_groups=mesh['gx'=4,'gy'=8] {'gx'}, dimensions={0}, use_global_device_ids=true | all-gather | bytes 5120 | tf_op jit(solution)/shard_map/all_gather | solution.py:367
  169.0 17.2 %fusion.11 = f32[256,128,128]{2,1,0:T(8,128)} fusion(bf16[256,128,128]{2,0,1:T(8,128)(2,1)} %copy-done.3, f32[128,168]{0,1:T(8,128)S(1)} %select_reduce_fusion.3), kind=kOutput, calls=%fused_computation.27 | convolution fusion | flops 3221225472 | bytes 25231360 | tf_op jit(solution)/shard_map/jc,xcz->xjz/dot_general | solution.py:48
  189.3 14.9 %bitcast_subtract_fusion.1 = f32[256,128,128]{1,2,0:T(8,128)} fusion(f32[256,128,128]{2,1,0:T(8,128)} %fusion.11, bf16[256,128,128]{1,2,0:T(8,128)(2,1)S(1)} %bitcast.86, bf16[256,40,128]{2,0,1:T(8,128)(2,1)} %pad_maximum_fusion.3, f32[128,20]{0,1:T(8,128)} %get-tuple-element.28, f32[128,20]{0,1:T(8,128)S(1)} %get-tuple-element.27), kind=kOutput, calls=%fused_computation.7 | convolution fusion | flops 1019220992 | bytes 44584960 | tf_op jit(solution)/shard_map/jc,xcz->xjz/dot_general | solution.py:48
  204.2 20.5 %fusion.15 = bf16[256,128,128]{2,1,0:T(8,128)(2,1)} fusion(f32[256,128,128]{1,2,0:T(8,128)} %bitcast_subtract_fusion.1, bf16[256,128,128]{1,2,0:T(8,128)(2,1)} %copy.71, f32[128,128]{1,0:T(8,128)S(1)} %copy-done.10), kind=kOutput, calls=%fused_computation.34 | convolution fusion | flops 3233808384 | bytes 33619968 | tf_op jit(solution)/shard_map/xyc,zc->xyz/dot_general | solution.py:90
  231.2 10.8 %collective-permute-done.4 = bf16[20,128,128]{2,1,0:T(8,128)(2,1)S(1)} collective-permute-done((bf16[20,128,128]{2,1,0:T(8,128)(2,1)S(1)}, bf16[20,128,128]{2,1,0:T(8,128)(2,1)S(1)}, u32[]{:S(2)}, u32[]{:S(2)}) %collective-permute-start.4) | collective-permute-done | bytes 655392 | tf_op jit(solution)/shard_map/ppermute | solution.py:23
  253.0 26.5 %fusion.16 = bf16[256,128,128]{2,0,1:T(8,128)(2,1)S(1)} fusion(bf16[296,128,128]{2,1,0:T(8,128)(2,1)S(1)} %pad_maximum_fusion.1, f32[256,296]{0,1:T(8,128)S(1)} %select_reduce_fusion.1), kind=kOutput, calls=%fused_computation.35 | convolution fusion | flops 7453278208 | bytes 18391040 | tf_op jit(solution)/shard_map/ic,cyz->iyz/dot_general | solution.py:48
  284.4 24.8 %fusion.9 = f32[256,128,128]{2,1,0:T(8,128)} fusion(bf16[256,128,128]{2,0,1:T(8,128)(2,1)S(1)} %fusion.16, f32[128,168]{0,1:T(8,128)S(1)} %select_reduce_fusion.2), kind=kOutput, calls=%fused_computation.25 | convolution fusion | flops 3221225472 | bytes 25231360 | tf_op jit(solution)/shard_map/jc,xcz->xjz/dot_general | solution.py:48
  320.1 22.8 %bitcast_subtract_fusion = f32[256,128,128]{1,2,0:T(8,128)} fusion(f32[256,128,128]{1,2,0:T(8,128)} %copy.95, f32[256,128,128]{2,1,0:T(8,128)} %fusion.9, bf16[256,40,128]{2,0,1:T(8,128)(2,1)S(1)} %pad_maximum_fusion.4, f32[128,20]{0,1:T(8,128)S(1)} %get-tuple-element.26, f32[128,20]{0,1:T(8,128)S(1)} %get-tuple-element.25), kind=kOutput, calls=%fused_computation.6 | convolution fusion | flops 1019220992 | bytes 52973568 | tf_op jit(solution)/shard_map/jc,xcz->xjz/dot_general | solution.py:48
  342.9 11.4 %fusion.13 = bf16[256,128,128]{2,1,0:T(8,128)(2,1)} fusion(f32[256,128,128]{1,2,0:T(8,128)} %bitcast_subtract_fusion, bf16[128,128]{1,0:T(8,128)(2,1)S(1)} %copy-done), kind=kOutput, calls=%fused_computation.30 | convolution fusion | flops 1077936128 | bytes 25198592 | tf_op jit(solution)/shard_map/zk,xyz->kxy/dot_general | solution.py:364
  354.3 11.8 %copy.84 = bf16[256,128,128]{1,0,2:T(8,128)(2,1)} copy(bf16[256,128,128]{2,1,0:T(8,128)(2,1)} %fusion.13) | data formatting | bytes 16777216 | tf_op jit(solution)/shard_map/zk,xyz->kxy/dot_general | solution.py:364
  366.1 361.1 %shard_map.131 = bf16[128,256,128]{2,1,0:T(8,128)(2,1)} custom-call(bf16[128,256,128]{2,1,0:T(8,128)(2,1)} %bitcast.84, bf16[1024,1024]{1,0:T(8,128)(2,1)} %copy.86.x_fwd, bf16[1024,1024]{1,0:T(8,128)(2,1)} %all-gather.4.cloned.1.call-done.x_inv, bf16[1024,1024]{1,0:T(8,128)(2,1)} %copy.87.y_fwd, bf16[1024,1024]{1,0:T(8,128)(2,1)} %bitcast.88, ...), custom_call_target="tpu_custom_call" | custom-call | tf_op jit(solution)/shard_map/pallas_call | solution.py:273
  727.2 12.7 %copy.88 = bf16[128,256,128]{0,2,1:T(8,128)(2,1)} copy(bf16[128,256,128]{2,1,0:T(8,128)(2,1)} %shard_map.131) | data formatting | bytes 16777216 | tf_op jit(solution)/shard_map/pallas_call | solution.py:273
  747.2 13.7 %collective-permute-start.8 = (bf16[20,128,128]{2,1,0:T(8,128)(2,1)S(1)}, bf16[20,128,128]{2,1,0:T(8,128)(2,1)S(1)}, u32[]{:S(2)}, u32[]{:S(2)}) collective-permute-start(bf16[20,128,128]{2,1,0:T(8,128)(2,1)S(1)} %get-tuple-element.15), channel_id=1, source_target_pairs={{0,8},{8,16},{16,24},{1,9},{9,17},{17,25},{2,10},{10,18},{18,26},{... | collective-permute-start | bytes 1966088 | tf_op jit(solution)/shard_map/ppermute | solution.py:23
  770.9 17.4 %copy.89 = f32[256,128,128]{1,2,0:T(8,128)} copy(f32[256,128,128]{2,1,0:T(8,128)} %get-tuple-element.44) | data formatting | bytes 33554432 | tf_op jit(solution)/shard_map/kxy,zk->xyz/dot_general | solution.py:408
  788.4 11.4 %pad_maximum_fusion.2 = bf16[296,128,128]{2,1,0:T(8,128)(2,1)} fusion(bf16[20,128,128]{2,1,0:T(8,128)(2,1)S(1)} %collective-permute-done.9, bf16[256,128,128]{2,1,0:T(8,128)(2,1)} %copy-done.5, bf16[20,128,128]{2,1,0:T(8,128)(2,1)S(1)} %collective-permute-done.8), kind=kLoop, calls=%fused_computation.17 | loop fusion | flops 9699328 | bytes 19398656 | tf_op jit(solution)/shard_map/concatenate | solution.py:78
  799.8 23.9 %fusion.19 = bf16[256,128,128]{2,0,1:T(8,128)(2,1)} fusion(bf16[296,128,128]{2,1,0:T(8,128)(2,1)} %pad_maximum_fusion.2, f32[256,296]{0,1:T(8,128)S(1)} %copy-done.9), kind=kOutput, calls=%fused_computation.36 | convolution fusion | flops 7453278208 | bytes 18391040 | tf_op jit(solution)/shard_map/ic,cyz->iyz/dot_general | solution.py:48
  828.8 9.0 multiply_reduce_fusion.1
  837.8 16.7 %fusion.7 = f32[256,128,128]{2,1,0:T(8,128)} fusion(bf16[256,128,128]{2,0,1:T(8,128)(2,1)} %fusion.19, f32[128,168]{0,1:T(8,128)S(1)} %select_reduce_fusion.3), kind=kOutput, calls=%fused_computation.23 | convolution fusion | flops 3221225472 | bytes 25231360 | tf_op jit(solution)/shard_map/jc,xcz->xjz/dot_general | solution.py:48
  854.8 21.0 %fusion.1 = (f32[]{:T(128)}, f32[256,128,128]{2,1,0:T(8,128)}) fusion(bf16[256,128,128]{1,2,0:T(8,128)(2,1)} %copy.71, f32[256,128,128]{2,1,0:T(8,128)} %fusion.7, f32[128,20]{0,1:T(8,128)S(1)} %copy-done.12, f32[128,20]{0,1:T(8,128)S(1)} %get-tuple-element.27, bf16[256,40,128]{2,0,1:T(8,128)(2,1)S(1)} %pad_maximum_fusion.5), kind=kOutput, calls=%fused_computation.3 | convolution fusion | flops 1027609600 | bytes 44584964 | tf_op jit(solution)/shard_map/jc,xcz->xjz/dot_general | solution.py:48
  875.8 44.7 %all-reduce = (f32[]{:T(128)}, f32[]{:T(128)}, f32[]{:T(128)}) all-reduce(f32[]{:T(128)} %multiply_reduce_fusion.1, f32[]{:T(128)} %get-tuple-element.41, f32[]{:T(128)} %get-tuple-element.43), channel_id=1, replica_groups=mesh['gx'=4,'gy'=8] {'gx','gy'}, use_global_device_ids=true, to_apply=%region_9.10 | all-reduce | flops 3 | bytes 24 | tf_op jit(solution)/shard_map/psum | solution.py:415
  922.4 34.1 %fusion.2 = (f32[256,128,128]{1,2,0:T(8,128)}, f32[256,128,128]{1,2,0:T(8,128)}) fusion(f32[256,128,128]{1,2,0:T(8,128)} %bitcast_subtract_fusion.1, f32[256,128,128]{2,1,0:T(8,128)} %get-tuple-element.42, f32[]{:T(128)S(6)} %div.13, f32[256,128,128]{1,2,0:T(8,128)} %copy.95, f32[256,128,128]{1,2,0:T(8,128)} %copy.89), kind=kLoop, calls=%fused_computation.5 | loop fusion | flops 16777216 | bytes 100663296 | tf_op jit(solution)/shard_map/sub | solution.py:422
  956.5 17.4 %copy.97 = f32[256,128,128]{2,1,0:T(8,128)} copy(f32[256,128,128]{1,2,0:T(8,128)} %get-tuple-element.45) | data formatting | bytes 33554432
  974.0 17.4 %copy.96 = f32[256,128,128]{2,1,0:T(8,128)} copy(f32[256,128,128]{1,2,0:T(8,128)} %get-tuple-element.46) | data formatting | bytes 33554432
  (120 shorter events, 91.1 us)
Async XLA Ops:
  7.2 26.7 %copy-start = (bf16[128,128]{1,0:T(8,128)(2,1)S(1)}, bf16[128,128]{1,0:T(8,128)(2,1)}, u32[]{:S(2)}) copy-start(bf16[128,128]{1,0:T(8,128)(2,1)} %param.20) | copy-start | bytes 98308
  7.2 302.0 %all-gather.4.cloned.1.call-start = ((), (), s32[]{:S(2)}) async-start(), calls=%async_computation | async-start | bytes 2621440 | tf_op jit(solution)/shard_map/all_gather | solution.py:398
  7.9 305.2 %all-gather.6.cloned.1.call-start = ((), (), s32[]{:S(2)}) async-start(), calls=%async_computation.1 | async-start | bytes 2359296 | tf_op jit(solution)/shard_map/all_gather | solution.py:399
  11.3 21.0 %copy-start.11 = (bf16[128,1024]{1,0:T(8,128)(2,1)S(1)}, bf16[128,1024]{1,0:T(8,128)(2,1)}, u32[]{:S(2)}) copy-start(bf16[128,1024]{1,0:T(8,128)(2,1)} %param.19) | copy-start | bytes 786436
  11.3 21.9 %copy-start.13 = (s32[3]{0:T(128)S(1)}, s32[3]{0:T(128)}, u32[]{:S(2)}) copy-start(s32[3]{0:T(128)} %param.17) | copy-start | bytes 40
  25.8 33.7 %collective-permute-start = (bf16[20,128,128]{1,2,0:T(8,128)(2,1)S(1)}, bf16[20,128,128]{1,2,0:T(8,128)(2,1)S(1)}, u32[]{:S(2)}, u32[]{:S(2)}) collective-permute-start(bf16[20,128,128]{1,2,0:T(8,128)(2,1)S(1)} %get-tuple-element.23), channel_id=1, source_target_pairs={{0,8},{8,16},{16,24},{1,9},{9,17},{17,25},{2,10},{10,18},{18,26},{... | collective-permute-start | bytes 1966088 | tf_op jit(solution)/shard_map/ppermute | solution.py:23
  30.7 39.7 %collective-permute-start.1 = (bf16[20,128,128]{1,2,0:T(8,128)(2,1)S(1)}, bf16[20,128,128]{1,2,0:T(8,128)(2,1)S(1)}, u32[]{:S(2)}, u32[]{:S(2)}) collective-permute-start(bf16[20,128,128]{1,2,0:T(8,128)(2,1)S(1)} %get-tuple-element.24), channel_id=1, source_target_pairs={{8,0},{16,8},{24,16},{9,1},{17,9},{25,17},{10,2},{18,10},{26,18},{... | collective-permute-start | bytes 1966088 | tf_op jit(solution)/shard_map/ppermute | solution.py:26
  38.8 55.9 %copy-start.8 = (f32[256,296]{0,1:T(8,128)}, f32[256,296]{0,1:T(8,128)S(1)}, u32[]{:S(2)}) copy-start(f32[256,296]{0,1:T(8,128)S(1)} %select_reduce_fusion) | copy-start | bytes 909316
  111.2 75.0 %collective-permute-start.2 = (bf16[256,20,128]{2,0,1:T(8,128)(2,1)}, bf16[256,20,128]{2,0,1:T(8,128)(2,1)S(1)}, u32[]{:S(2)}, u32[]{:S(2)}) collective-permute-start(bf16[256,20,128]{2,0,1:T(8,128)(2,1)} %get-tuple-element.21), channel_id=1, source_target_pairs={{0,1},{1,2},{2,3},{3,4},{4,5},{5,6},{6,7},{8,9},{9,10},{10,11},{11... | collective-permute-start | bytes 3932168 | tf_op jit(solution)/shard_map/ppermute | solution.py:23
  113.2 73.0 %collective-permute-start.3 = (bf16[256,20,128]{2,0,1:T(8,128)(2,1)}, bf16[256,20,128]{2,0,1:T(8,128)(2,1)}, u32[]{:S(2)}, u32[]{:S(2)}) collective-permute-start(bf16[256,20,128]{2,0,1:T(8,128)(2,1)} %get-tuple-element.22), channel_id=1, source_target_pairs={{1,0},{2,1},{3,2},{4,3},{5,4},{6,5},{7,6},{9,8},{10,9},{11,10},{12... | collective-permute-start | bytes 3932168 | tf_op jit(solution)/shard_map/ppermute | solution.py:26
  168.4 20.9 %slice-start.4 = ((s8[8388608]{0:T(1024)(128)(4,1)}), s8[4194304]{0:T(1024)(128)(4,1)S(1)}, s32[]{:S(2)}) async-start(s8[8388608]{0:T(1024)(128)(4,1)} %bitcast.85), calls=%async_computation.6 | async-start | bytes 8388608
  169.0 20.3 %slice-start.5 = ((s8[8388608]{0:T(1024)(128)(4,1)}), s8[4194304]{0:T(1024)(128)(4,1)S(1)}, s32[]{:S(2)}) async-start(s8[8388608]{0:T(1024)(128)(4,1)} %bitcast.85), calls=%async_computation.7 | async-start | bytes 8388608
  204.2 25.5 %copy-start.16 = (f32[1,33]{1,0:T(1,128)S(1)}, f32[1,33]{1,0:T(1,128)}, u32[]{:S(2)}) copy-start(f32[1,33]{1,0:T(1,128)} %slice.122) | copy-start | bytes 400
  204.2 25.9 %copy-start.7 = (s32[256,296]{0,1:T(8,128)S(1)}, s32[256,296]{0,1:T(8,128)}, u32[]{:S(2)}) copy-start(s32[256,296]{0,1:T(8,128)} %fusion.29) | copy-start | bytes 909316
  204.2 25.9 %copy-start.17 = (f32[1,33]{1,0:T(1,128)S(1)}, f32[1,33]{1,0:T(1,128)}, u32[]{:S(2)}) copy-start(f32[1,33]{1,0:T(1,128)} %slice.104) | copy-start | bytes 400
  226.1 15.9 %collective-permute-start.4 = (bf16[20,128,128]{2,1,0:T(8,128)(2,1)S(1)}, bf16[20,128,128]{2,1,0:T(8,128)(2,1)S(1)}, u32[]{:S(2)}, u32[]{:S(2)}) collective-permute-start(bf16[20,128,128]{2,1,0:T(8,128)(2,1)S(1)} %get-tuple-element.19), channel_id=1, source_target_pairs={{0,8},{8,16},{16,24},{1,9},{9,17},{17,25},{2,10},{10,18},{18,26},{... | collective-permute-start | bytes 1966088 | tf_op jit(solution)/shard_map/ppermute | solution.py:23
  227.7 18.4 %collective-permute-start.5 = (bf16[20,128,128]{2,1,0:T(8,128)(2,1)S(1)}, bf16[20,128,128]{2,1,0:T(8,128)(2,1)S(1)}, u32[]{:S(2)}, u32[]{:S(2)}) collective-permute-start(bf16[20,128,128]{2,1,0:T(8,128)(2,1)S(1)} %get-tuple-element.20), channel_id=1, source_target_pairs={{8,0},{16,8},{24,16},{9,1},{17,9},{25,17},{10,2},{18,10},{26,18},{... | collective-permute-start | bytes 1966088 | tf_op jit(solution)/shard_map/ppermute | solution.py:26
  253.0 30.5 %copy-start.14 = (f32[1024]{0:T(1024)S(1)}, f32[1024]{0:T(1024)}, u32[]{:S(2)}) copy-start(f32[1024]{0:T(1024)} %param.22) | copy-start | bytes 12292
  280.8 36.3 %collective-permute-start.6 = (bf16[256,20,128]{2,0,1:T(8,128)(2,1)}, bf16[256,20,128]{2,0,1:T(8,128)(2,1)S(1)}, u32[]{:S(2)}, u32[]{:S(2)}) collective-permute-start(bf16[256,20,128]{2,0,1:T(8,128)(2,1)} %get-tuple-element.17), channel_id=1, source_target_pairs={{0,1},{1,2},{2,3},{3,4},{4,5},{5,6},{6,7},{8,9},{9,10},{10,11},{11... | collective-permute-start | bytes 3932168 | tf_op jit(solution)/shard_map/ppermute | solution.py:23
  282.1 36.1 %collective-permute-start.7 = (bf16[256,20,128]{2,0,1:T(8,128)(2,1)S(1)}, bf16[256,20,128]{2,0,1:T(8,128)(2,1)}, u32[]{:S(2)}, u32[]{:S(2)}) collective-permute-start(bf16[256,20,128]{2,0,1:T(8,128)(2,1)S(1)} %get-tuple-element.18), channel_id=1, source_target_pairs={{1,0},{2,1},{3,2},{4,3},{5,4},{6,5},{7,6},{9,8},{10,9},{11,10},{12... | collective-permute-start | bytes 3932168 | tf_op jit(solution)/shard_map/ppermute | solution.py:26
  739.9 22.3 %copy-start.2 = (bf16[128,256,128]{0,2,1:T(8,128)(2,1)S(1)}, bf16[128,256,128]{0,2,1:T(8,128)(2,1)}, u32[]{:S(2)}) copy-start(bf16[128,256,128]{0,2,1:T(8,128)(2,1)} %copy.88) | copy-start | bytes 25165828
  747.0 23.9 %copy-start.5 = (bf16[256,128,128]{2,1,0:T(8,128)(2,1)}, bf16[256,128,128]{2,1,0:T(8,128)(2,1)S(1)}, u32[]{:S(2)}) copy-start(bf16[256,128,128]{2,1,0:T(8,128)(2,1)S(1)} %convolution_convert_fusion) | copy-start | bytes 25165828
  747.2 41.2 %collective-permute-start.8 = (bf16[20,128,128]{2,1,0:T(8,128)(2,1)S(1)}, bf16[20,128,128]{2,1,0:T(8,128)(2,1)S(1)}, u32[]{:S(2)}, u32[]{:S(2)}) collective-permute-start(bf16[20,128,128]{2,1,0:T(8,128)(2,1)S(1)} %get-tuple-element.15), channel_id=1, source_target_pairs={{0,8},{8,16},{16,24},{1,9},{9,17},{17,25},{2,10},{10,18},{18,26},{... | collective-permute-start | bytes 1966088 | tf_op jit(solution)/shard_map/ppermute | solution.py:23
  760.9 27.5 %collective-permute-start.9 = (bf16[20,128,128]{2,1,0:T(8,128)(2,1)S(1)}, bf16[20,128,128]{2,1,0:T(8,128)(2,1)S(1)}, u32[]{:S(2)}, u32[]{:S(2)}) collective-permute-start(bf16[20,128,128]{2,1,0:T(8,128)(2,1)S(1)} %get-tuple-element.16), channel_id=1, source_target_pairs={{8,0},{16,8},{24,16},{9,1},{17,9},{25,17},{10,2},{18,10},{26,18},{... | collective-permute-start | bytes 1966088 | tf_op jit(solution)/shard_map/ppermute | solution.py:26
  788.4 40.3 %slice-start = ((s8[16777216]{0:T(1024)(128)(4,1)}), s8[4194304]{0:T(1024)(128)(4,1)S(1)}, s32[]{:S(2)}) async-start(s8[16777216]{0:T(1024)(128)(4,1)} %bitcast.82), calls=%async_computation.2 | async-start | bytes 8388608
  788.4 40.3 %slice-start.1 = ((s8[16777216]{0:T(1024)(128)(4,1)}), s8[4194304]{0:T(1024)(128)(4,1)S(1)}, s32[]{:S(2)}) async-start(s8[16777216]{0:T(1024)(128)(4,1)} %bitcast.82), calls=%async_computation.3 | async-start | bytes 8388608
  799.8 29.0 %slice-start.2 = ((s8[16777216]{0:T(1024)(128)(4,1)}), s8[4194304]{0:T(1024)(128)(4,1)S(1)}, s32[]{:S(2)}) async-start(s8[16777216]{0:T(1024)(128)(4,1)} %bitcast.82), calls=%async_computation.4 | async-start | bytes 8388608
  799.8 29.0 %slice-start.3 = ((s8[16777216]{0:T(1024)(128)(4,1)}), s8[4194304]{0:T(1024)(128)(4,1)S(1)}, s32[]{:S(2)}) async-start(s8[16777216]{0:T(1024)(128)(4,1)} %bitcast.82), calls=%async_computation.5 | async-start | bytes 8388608
  825.7 28.9 %collective-permute-start.10 = (bf16[256,20,128]{2,0,1:T(8,128)(2,1)S(1)}, bf16[256,20,128]{2,0,1:T(8,128)(2,1)S(1)}, u32[]{:S(2)}, u32[]{:S(2)}) collective-permute-start(bf16[256,20,128]{2,0,1:T(8,128)(2,1)S(1)} %get-tuple-element.13), channel_id=1, source_target_pairs={{0,1},{1,2},{2,3},{3,4},{4,5},{5,6},{6,7},{8,9},{9,10},{10,11},{11... | collective-permute-start | bytes 3932168 | tf_op jit(solution)/shard_map/ppermute | solution.py:23
  827.4 27.1 %collective-permute-start.11 = (bf16[256,20,128]{2,0,1:T(8,128)(2,1)S(1)}, bf16[256,20,128]{2,0,1:T(8,128)(2,1)S(1)}, u32[]{:S(2)}, u32[]{:S(2)}) collective-permute-start(bf16[256,20,128]{2,0,1:T(8,128)(2,1)S(1)} %get-tuple-element.14), channel_id=1, source_target_pairs={{1,0},{2,1},{3,2},{4,3},{5,4},{6,5},{7,6},{9,8},{10,9},{11,10},{12... | collective-permute-start | bytes 3932168 | tf_op jit(solution)/shard_map/ppermute | solution.py:26
  837.8 17.0 %copy-start.12 = (f32[128,20]{0,1:T(8,128)S(1)}, f32[128,20]{0,1:T(8,128)}, u32[]{:S(2)}) copy-start(f32[128,20]{0,1:T(8,128)} %get-tuple-element.28) | copy-start | bytes 30724
  974.0 17.4 %copy-start.1 = (bf16[128,128]{1,0:T(8,128)(2,1)S(1)}, bf16[128,128]{1,0:T(8,128)(2,1)}, u32[]{:S(2)}) copy-start(bf16[128,128]{1,0:T(8,128)(2,1)} %param.20) | copy-start | bytes 98308
  (7 other events, 57.5 us)
Sparse Core Ops, SparseCore 0:
  9.6 59.0 all-gather.3
  70.6 30.4 all-gather.5

commit v2 on v0

--- a/solution.py
+++ b/solution.py
@@ -1,6 +1,10 @@
+import functools
+
 import jax
 import jax.numpy as jnp
 from jax import lax
+from jax.experimental import pallas as pl
+from jax.experimental.pallas import tpu as pltpu
 from jax.sharding import PartitionSpec as P
 
 HALF = 16
@@ -176,9 +180,672 @@
     return (iterate + step_size * direction, misfit - step_size * blurred)
 
 
+MESH_ID = pl.DeviceIdType.MESH
+PARTS = 4
+
+
+def transform_kernel(
+    parts, size_x, size_y,
+    section_ref, x_fwd, x_inv, y_fwd, y_inv, eigen_xy, eigen_z,
+    out_ref,
+    lines_x, lines_y, lines_back, send_a, send_b, send_c, modes,
+    fs, fr, gs, gr, hs, hr, bs, br, fl, gl, hl, bl,
+):
+    me_x = lax.axis_index("gx")
+    me_y = lax.axis_index("gy")
+    depth = lines_x.shape[0]
+    full = lines_x.shape[1]
+    block_y = lines_x.shape[2]
+    block_x = section_ref.shape[1]
+    share = lines_y.shape[1]
+    full_y = lines_y.shape[2]
+    part = depth // parts
+    slots = send_a.shape[0]
+
+    barrier = pltpu.get_barrier_semaphore()
+    for step in range(1, size_x):
+        pl.semaphore_signal(
+            barrier, inc=1, device_id=(lax.rem(me_x + step, size_x), me_y), device_id_type=MESH_ID
+        )
+    for step in range(1, size_y):
+        pl.semaphore_signal(
+            barrier, inc=1, device_id=(me_x, lax.rem(me_y + step, size_y)), device_id_type=MESH_ID
+        )
+    pl.semaphore_wait(barrier, size_x + size_y - 2)
+
+    def copies(kind, c):
+        out = []
+        here = pl.ds(c * part, part)
+        slot = c % slots
+        count = size_x if kind in "fb" else size_y
+        for step in range(count):
+            mine = step == 0
+            if kind in "fb":
+                peer = lax.rem(me_x + step, size_x)
+                target = (peer, me_y)
+            else:
+                peer = lax.rem(me_y + step, size_y)
+                target = (me_x, peer)
+            if kind == "f":
+                src = section_ref.at[pl.ds(peer * depth + c * part, part)]
+                dst = lines_x.at[here, pl.ds(me_x * block_x, block_x)]
+                sems = fs, fr, fl
+            elif kind == "g":
+                src = send_a.at[slot, :, pl.ds(peer * share, share)]
+                dst = lines_y.at[here, :, pl.ds(me_y * block_y, block_y)]
+                sems = gs, gr, gl
+            elif kind == "h":
+                src = send_b.at[slot, :, :, pl.ds(peer * block_y, block_y)]
+                dst = lines_back.at[here, pl.ds(me_y * share, share)]
+                sems = hs, hr, hl
+            else:
+                src = send_c.at[slot, :, pl.ds(peer * block_x, block_x)]
+                dst = out_ref.at[pl.ds(me_x * depth + c * part, part)]
+                sems = bs, br, bl
+            if mine:
+                out.append(pltpu.make_async_copy(src, dst, sems[2].at[c]))
+            else:
+                out.append(
+                    pltpu.make_async_remote_copy(
+                        src, dst, sems[0].at[c, step], sems[1].at[c, step],
+                        device_id=target, device_id_type=MESH_ID,
+                    )
+                )
+        return out
+
+    every = {kind: [copies(kind, c) for c in range(parts)] for kind in "fghb"}
+
+    def start(kind, c):
+        group = every[kind][c]
+        for copy in group[1:] + group[:1]:
+            copy.start()
+
+    def landed(kind, c):
+        group = every[kind][c]
+        if kind != "b":
+            group[0].wait()
+        for copy in group[1:]:
+            copy.wait_recv()
+
+    def sent(kind, c):
+        group = every[kind][c]
+        if kind == "b":
+            group[0].wait()
+        for copy in group[1:]:
+            copy.wait_send()
+
+    def along_x(matrix, lines, out, c):
+        def pair(i, carry):
+            k = c * part + 2 * i
+            both = jnp.concatenate([lines[k], lines[k + 1]], axis=1)
+            for b in range(0, full, 256):
+                found = jnp.dot(
+                    matrix[pl.ds(b, 256), :], both, preferred_element_type=jnp.float32
+                ).astype(jnp.bfloat16)
+                out[c % slots, 2 * i, pl.ds(b, 256)] = found[:, :block_y]
+                out[c % slots, 2 * i + 1, pl.ds(b, 256)] = found[:, block_y:]
+            return carry
+
+        lax.fori_loop(0, part // 2, pair, 0)
+
+    def along_y(c):
+        def pair(i, carry):
+            k = c * part + 2 * i
+            rows = jnp.concatenate([lines_y[k], lines_y[k + 1]], axis=0)
+            for b in range(0, full_y, 256):
+                found = jnp.dot(rows, y_fwd[:, pl.ds(b, 256)], preferred_element_type=jnp.float32)
+                weight = eigen_xy[:, pl.ds(b, 256)]
+                modes[pl.ds(0, share), pl.ds(b, 256)] = (
+                    found[:share] / (weight * eigen_z[k] + tikhonov)
+                ).astype(jnp.bfloat16)
+                modes[pl.ds(share, share), pl.ds(b, 256)] = (
+                    found[share:] / (weight * eigen_z[k + 1] + tikhonov)
+                ).astype(jnp.bfloat16)
+            for b in range(0, full_y, 256):
+                found = jnp.dot(
+                    modes[...], y_inv[:, pl.ds(b, 256)], preferred_element_type=jnp.float32
+                ).astype(jnp.bfloat16)
+                send_b[c % slots, 2 * i, :, pl.ds(b, 256)] = found[:share]
+                send_b[c % slots, 2 * i + 1, :, pl.ds(b, 256)] = found[share:]
+            return carry
+
+        lax.fori_loop(0, part // 2, pair, 0)
+
+    ahead = min(2, parts)
+    for c in range(ahead):
+        start("f", c)
+    for step in range(parts + 2):
+        c = step
+        if c < parts:
+            landed("f", c)
+            if c + ahead < parts:
+                start("f", c + ahead)
+            if c >= slots:
+                sent("g", c - slots)
+            along_x(x_fwd, lines_x, send_a, c)
+            start("g", c)
+        c = step - 1
+        if 0 <= c < parts:
+            landed("g", c)
+            if c >= slots:
+                sent("h", c - slots)
+            along_y(c)
+            start("h", c)
+        c = step - 2
+        if 0 <= c < parts:
+            landed("h", c)
+            if c >= slots:
+                sent("b", c - slots)
+            along_x(x_inv, lines_back, send_c, c)
+            start("b", c)
+    for c in range(parts):
+        landed("b", c)
+        sent("f", c)
+        if c >= parts - slots:
+            sent("g", c)
+            sent("h", c)
+            sent("b", c)
+
+
+def transform(section, x_fwd, x_inv, y_fwd, y_inv, eigen_xy, eigen_z, size_x, size_y):
+    modes_z, block_x, block_y = section.shape
+    depth = modes_z // size_x
+    full_x, full_y = x_fwd.shape[0], y_fwd.shape[0]
+    share = full_x // size_y
+    parts = PARTS
+    part = depth // parts
+    slots = 2
+    vmem = pl.BlockSpec(memory_space=pltpu.VMEM)
+    sem = lambda n: pltpu.SemaphoreType.DMA((parts, n))
+    one = pltpu.SemaphoreType.DMA((parts,))
+    bf = jnp.bfloat16
+    return pl.pallas_call(
+        functools.partial(transform_kernel, parts, size_x, size_y),
+        out_shape=jax.ShapeDtypeStruct(section.shape, bf),
+        in_specs=[pl.BlockSpec(memory_space=pl.ANY)] + [vmem] * 5
+        + [pl.BlockSpec(memory_space=pltpu.SMEM)],
+        out_specs=pl.BlockSpec(memory_space=pl.ANY),
+        scratch_shapes=[
+            pltpu.VMEM((depth, full_x, block_y), bf),
+            pltpu.VMEM((depth, share, full_y), bf),
+            pltpu.VMEM((depth, full_x, block_y), bf),
+            pltpu.VMEM((slots, part, full_x, block_y), bf),
+            pltpu.VMEM((slots, part, share, full_y), bf),
+            pltpu.VMEM((slots, part, full_x, block_y), bf),
+            pltpu.VMEM((2 * share, full_y), bf),
+            sem(size_x), sem(size_x), sem(size_y), sem(size_y),
+            sem(size_y), sem(size_y), sem(size_x), sem(size_x),
+            one, one, one, one,
+        ],
+        compiler_params=pltpu.CompilerParams(
+            collective_id=0, has_side_effects=True, vmem_limit_bytes=60 * 2**20
+        ),
+    )(section, x_fwd, x_inv, y_fwd, y_inv, eigen_xy, eigen_z)
+
+
+BAND_ROWS = 16
+QUADS = 4
+RIM_ROWS = 32
+RIM_LANES = 32
+
+
+def to_modes_kernel(matrix, source, first, second, held):
+    rows, depth = source.shape[0], source.shape[2]
+    for x in range(0, rows, 2):
+        lines = source[pl.ds(x, 2)].reshape(2 * source.shape[1], depth).astype(jnp.bfloat16)
+        found = lax.dot_general(
+            matrix[...], lines, (((1,), (1,)), ((), ())), preferred_element_type=jnp.float32
+        )
+        held[:, x, :] = found[:, : source.shape[1]]
+        held[:, x + 1, :] = found[:, source.shape[1] :]
+    first[...] = held[:depth].reshape(first.shape).astype(first.dtype)
+    second[...] = held[depth:].reshape(second.shape).astype(second.dtype)
+
+
+def modes_block(rows, shape):
+    return pl.BlockSpec((shape[0], shape[1], rows, shape[3]), lambda i: (0, 0, i, 0))
+
+
+def space_block(rows, shape):
+    return pl.BlockSpec((rows, shape[1], shape[2]), lambda i: (i, 0, 0))
+
+
+def whole_block(shape):
+    return pl.BlockSpec(shape, lambda i: (0,) * len(shape))
+
+
+def to_modes(source, matrix):
+    block_x, block_y, depth = source.shape
+    shape = (QUADS, depth // QUADS, block_x, block_y)
+    out = jax.ShapeDtypeStruct(shape, jnp.bfloat16)
+    return pl.pallas_call(
+        to_modes_kernel,
+        grid=(block_x // BAND_ROWS,),
+        out_shape=[out, out],
+        in_specs=[whole_block(matrix.shape), space_block(BAND_ROWS, source.shape)],
+        out_specs=[modes_block(BAND_ROWS, shape)] * 2,
+        scratch_shapes=[pltpu.VMEM((2 * depth, BAND_ROWS, block_y), jnp.float32)],
+        compiler_params=pltpu.CompilerParams(vmem_limit_bytes=40 * 2**20),
+    )(matrix, source)
+
+
+def spread_kernel(size_x, size_y, parts, final, source, x_band, to_right, to_left, *rest):
+    if final:
+        y_band, plain, out, along, from_left, from_right = rest[:6]
+        rest = rest[6:]
+    else:
+        along, from_left, from_right = rest[:3]
+        rest = rest[3:]
+    low, high, right, left, xs, xr, ys, yr = rest
+    me_x = lax.axis_index("gx")
+    me_y = lax.axis_index("gy")
+    block_x = source.shape[2]
+    groups = source.shape[1]
+    part = groups // parts
+    has = (me_x > 0, me_x < size_x - 1, me_y > 0, me_y < size_y - 1)
+    peers = ((me_x - 1, me_y), (me_x + 1, me_y), (me_x, me_y - 1), (me_x, me_y + 1))
+
+    barrier = pltpu.get_barrier_semaphore()
+    for peer in (
+        (lax.rem(me_x + 1, size_x), me_y), (lax.rem(me_x + size_x - 1, size_x), me_y),
+        (me_x, lax.rem(me_y + 1, size_y)), (me_x, lax.rem(me_y + size_y - 1, size_y)),
+    ):
+        pl.semaphore_signal(barrier, inc=1, device_id=peer, device_id_type=MESH_ID)
+    pl.semaphore_wait(barrier, 4)
+
+    def x_copy(c, way):
+        here = pl.ds(c * part, part)
+        if way == 0:
+            src, dst, peer = source.at[:, here, pl.ds(0, RIM_ROWS)], high.at[:, here], peers[0]
+        else:
+            src = source.at[:, here, pl.ds(block_x - RIM_ROWS, RIM_ROWS)]
+            dst, peer = low.at[:, here], peers[1]
+        return pltpu.make_async_remote_copy(
+            src, dst, xs.at[c, way], xr.at[c, way], device_id=peer, device_id_type=MESH_ID
+        )
+
+    def y_copy(c, way):
+        here = pl.ds(c * part, part)
+        if way == 0:
+            src, dst, peer = left.at[here], from_right.at[here], peers[2]
+        else:
+            src, dst, peer = right.at[here], from_left.at[here], peers[3]
+        return pltpu.make_async_remote_copy(
+            src, dst, ys.at[c, way], yr.at[c, way], device_id=peer, device_id_type=MESH_ID
+        )
+
+    for c in range(parts):
+        for way in range(2):
+
+            @pl.when(has[way])
+            def _():
+                x_copy(c, way).start()
+
+    for there, ref in zip(has, (low, high, from_left, from_right)):
+
+        @pl.when(jnp.logical_not(there))
+        def _():
+            ref[...] = jnp.zeros_like(ref)
+
+    def blur_x(c):
+        def step(i, carry):
+            g = c * part + i
+            for q in range(0, QUADS, 2):
+                both = jnp.concatenate(
+                    [
+                        jnp.concatenate([low[p, g], source[p, g], high[p, g]], axis=0)
+                        for p in (q, q + 1)
+                    ],
+                    axis=1,
+                )
+                found = jnp.dot(
+                    x_band[...], both, preferred_element_type=jnp.float32
+                ).astype(jnp.bfloat16)
+                along[q, g] = found[:, : found.shape[1] // 2]
+                along[q + 1, g] = found[:, found.shape[1] // 2 :]
+            wide = jnp.concatenate([along[q, g] for q in range(QUADS)], axis=1)
+            right[g] = jnp.dot(
+                wide, to_right[...], preferred_element_type=jnp.float32
+            ).astype(jnp.bfloat16)
+            left[g] = jnp.dot(
+                wide, to_left[...], preferred_element_type=jnp.float32
+            ).astype(jnp.bfloat16)
+            return carry
+
+        lax.fori_loop(0, part, step, 0)
+
+    def blur_y(c):
+        def step(i, carry):
+            g = c * part + i
+            for q in range(QUADS):
+                wide = jnp.concatenate([along[q, g], from_left[g], from_right[g]], axis=1)
+                found = jnp.dot(wide, y_band[q], preferred_element_type=jnp.float32)
+                out[q, g] = (found - tikhonov * plain[q, g].astype(jnp.float32)).astype(out.dtype)
+            return carry
+
+        lax.fori_loop(0, part, step, 0)
+
+    def receive(copy, c):
+        for way in range(2):
+
+            @pl.when(has[(0, 2)[copy is y_copy] + 1 - way])
+            def _():
+                copy(c, way).wait_recv()
+
+    for c in range(parts):
+        receive(x_copy, c)
+        blur_x(c)
+        for way in range(2):
+
+            @pl.when(has[2 + way])
+            def _():
+                y_copy(c, way).start()
+
+        if final and c > 0:
+            receive(y_copy, c - 1)
+            blur_y(c - 1)
+    if final:
+        receive(y_copy, parts - 1)
+        blur_y(parts - 1)
+    else:
+        for c in range(parts):
+            receive(y_copy, c)
+    for c in range(parts):
+        for way in range(2):
+
+            @pl.when(has[way])
+            def _():
+                x_copy(c, way).wait_send()
+
+            @pl.when(has[2 + way])
+            def _():
+                y_copy(c, way).wait_send()
+
+
+def spread(source, x_band, selects, size_x, size_y, number, final=()):
+    quads, groups, block_x, block_y = source.shape
+    bf = jnp.bfloat16
+    whole = jax.ShapeDtypeStruct(source.shape, bf)
+    rims = jax.ShapeDtypeStruct((groups, block_x, block_y), bf)
+    vmem = pl.BlockSpec(memory_space=pltpu.VMEM)
+    parts = PARTS
+    outs = [whole] if final else [whole, rims, rims]
+    scratch = [pltpu.VMEM(s.shape, bf) for s in (whole, rims, rims)] if final else []
+    edge = pltpu.VMEM((quads, groups, RIM_ROWS, block_y), bf)
+    packed = pltpu.VMEM(rims.shape, bf)
+    sem = pltpu.SemaphoreType.DMA((parts, 2))
+    found = pl.pallas_call(
+        functools.partial(spread_kernel, size_x, size_y, parts, bool(final)),
+        out_shape=outs,
+        in_specs=[vmem] * (4 + len(final)),
+        out_specs=[vmem] * len(outs),
+        scratch_shapes=scratch + [edge, edge, packed, packed, sem, sem, sem, sem],
+        compiler_params=pltpu.CompilerParams(
+            collective_id=number, has_side_effects=True, vmem_limit_bytes=56 * 2**20
+        ),
+    )(source, x_band, *selects, *final)
+    return found
+
+
+def blur_y_rows(along, from_left, from_right, y_band, held):
+    quads, groups, rows, block_y = along.shape
+    count = groups * rows
+    sides = [from_left[...].reshape(count, block_y), from_right[...].reshape(count, block_y)]
+    for q in range(quads):
+        wide = jnp.concatenate([along[q].reshape(count, block_y)] + sides, axis=1)
+        found = jnp.dot(wide, y_band[q], preferred_element_type=jnp.float32)
+        held[pl.ds(q * groups, groups)] = found.reshape(groups, rows, block_y)
+
+
+def misfit_kernel(
+    along, from_left, from_right, observed, confidence, y_band, matrix,
+    misfit, weighted, held, turned_back,
+):
+    blur_y_rows(along, from_left, from_right, y_band, held)
+    for x in range(observed.shape[0]):
+        found = observed[x].astype(jnp.float32) - held[:, x, :].T
+        misfit[x] = found
+        lines = (confidence[x].astype(jnp.float32) * found).astype(jnp.bfloat16)
+        turned_back[:, x, :] = lax.dot_general(
+            matrix[...], lines, (((1,), (1,)), ((), ())), preferred_element_type=jnp.float32
+        )
+    weighted[...] = turned_back[...].reshape(weighted.shape).astype(weighted.dtype)
+
+
+def find_misfit(along, from_left, from_right, observed, confidence, y_band, matrix):
+    shape, space = along.shape, observed.shape
+    rims = pl.BlockSpec((shape[1], BAND_ROWS, shape[3]), lambda i: (0, i, 0))
+    held = pltpu.VMEM((space[2], BAND_ROWS, shape[3]), jnp.float32)
+    return pl.pallas_call(
+        misfit_kernel,
+        grid=(shape[2] // BAND_ROWS,),
+        out_shape=[
+            jax.ShapeDtypeStruct(space, jnp.float32),
+            jax.ShapeDtypeStruct(shape, jnp.bfloat16),
+        ],
+        in_specs=[
+            modes_block(BAND_ROWS, shape), rims, rims,
+            space_block(BAND_ROWS, space), space_block(BAND_ROWS, space),
+            whole_block(y_band.shape), whole_block(matrix.shape),
+        ],
+        out_specs=[space_block(BAND_ROWS, space), modes_block(BAND_ROWS, shape)],
+        scratch_shapes=[held, held],
+        compiler_params=pltpu.CompilerParams(vmem_limit_bytes=40 * 2**20),
+    )(along, from_left, from_right, observed, confidence, y_band, matrix)
+
+
+def folded(values):
+    return jnp.sum(values.reshape(-1, 8, values.shape[-1]), axis=0)
+
+
+def direction_kernel(
+    along, from_left, from_right, section_six, section_one, confidence, y_band, basis, blurring,
+    direction, blurred, sums, held, held_six,
+):
+    @pl.when(pl.program_id(0) == 0)
+    def _():
+        sums[...] = jnp.zeros_like(sums)
+
+    blur_y_rows(along, from_left, from_right, y_band, held)
+    six = section_six[...].astype(jnp.float32)
+    sums[0] += folded((six * section_one[...].astype(jnp.float32)).reshape(-1, six.shape[-1]))
+    held_six[...] = six.reshape(held_six.shape)
+    for x in range(confidence.shape[0]):
+        lines = held_six[:, x, :].T.astype(jnp.bfloat16)
+        found = jnp.dot(lines, basis[...], preferred_element_type=jnp.float32)
+        direction[x] = found
+        sums[2] += folded(found * found)
+        lines = held[:, x, :].T.astype(jnp.bfloat16)
+        found = jnp.dot(
+            jnp.concatenate([lines, lines], axis=1), blurring[...],
+            preferred_element_type=jnp.float32,
+        )
+        blurred[x] = found
+        sums[1] += folded(confidence[x].astype(jnp.float32) * found * found)
+
+
+def find_direction(
+    along, from_left, from_right, section_six, section_one, confidence, y_band, basis, blurring
+):
+    shape, space = along.shape, confidence.shape
+    rims = pl.BlockSpec((shape[1], BAND_ROWS, shape[3]), lambda i: (0, i, 0))
+    held = pltpu.VMEM((space[2], BAND_ROWS, shape[3]), jnp.float32)
+    sums = (3, 8, space[2])
+    return pl.pallas_call(
+        direction_kernel,
+        grid=(shape[2] // BAND_ROWS,),
+        out_shape=[
+            jax.ShapeDtypeStruct(space, jnp.float32),
+            jax.ShapeDtypeStruct(space, jnp.float32),
+            jax.ShapeDtypeStruct(sums, jnp.float32),
+        ],
+        in_specs=[
+            modes_block(BAND_ROWS, shape), rims, rims,
+            modes_block(BAND_ROWS, shape), modes_block(BAND_ROWS, shape),
+            space_block(BAND_ROWS, space),
+            whole_block(y_band.shape), whole_block(basis.shape), whole_block(blurring.shape),
+        ],
+        out_specs=[
+            space_block(BAND_ROWS, space), space_block(BAND_ROWS, space), whole_block(sums),
+        ],
+        scratch_shapes=[held, held],
+        compiler_params=pltpu.CompilerParams(vmem_limit_bytes=40 * 2**20),
+    )(
+        along, from_left, from_right, section_six, section_one, confidence, y_band, basis, blurring
+    )
+
+
+def total_kernel(size_x, size_y, values, total, from_x, from_y, held, sx, rx, sy, ry):
+    me_x = lax.axis_index("gx")
+    me_y = lax.axis_index("gy")
+    x_peers = [(lax.rem(me_x + s, size_x), me_y) for s in range(1, size_x)]
+    y_peers = [(me_x, lax.rem(me_y + s, size_y)) for s in range(1, size_y)]
+    barrier = pltpu.get_barrier_semaphore()
+    for peer in x_peers + y_peers:
+        pl.semaphore_signal(barrier, inc=1, device_id=peer, device_id_type=MESH_ID)
+    pl.semaphore_wait(barrier, size_x + size_y - 2)
+
+    def gather(source, landing, peers, sends, receives):
+        copies = [
+            pltpu.make_async_remote_copy(
+                source, landing.at[s], sends.at[s], receives.at[s],
+                device_id=peer, device_id_type=MESH_ID,
+            )
+            for s, peer in enumerate(peers)
+        ]
+        for copy in copies:
+            copy.start()
+        for copy in copies:
+            copy.wait()
+        return source[...] + jnp.sum(landing[...], axis=0)
+
+    held[...] = jnp.sum(values[...], axis=1)
+    held[...] = gather(held, from_x, x_peers, sx, rx)
+    total[...] = gather(held, from_y, y_peers, sy, ry)
+
+
+def total_sums(sums, size_x, size_y, number):
+    lanes = sums.shape[2]
+    padded = jnp.pad(sums, ((0, 5), (0, 0), (0, 0)))
+    vmem = pl.BlockSpec(memory_space=pltpu.VMEM)
+    sem = lambda n: pltpu.SemaphoreType.DMA((n - 1,))
+    f32 = jnp.float32
+    return pl.pallas_call(
+        functools.partial(total_kernel, size_x, size_y),
+        out_shape=jax.ShapeDtypeStruct((8, lanes), f32),
+        in_specs=[vmem],
+        out_specs=vmem,
+        scratch_shapes=[
+            pltpu.VMEM((size_x - 1, 8, lanes), f32),
+            pltpu.VMEM((size_y - 1, 8, lanes), f32),
+            pltpu.VMEM((8, lanes), f32),
+            sem(size_x), sem(size_x), sem(size_y), sem(size_y),
+        ],
+        compiler_params=pltpu.CompilerParams(collective_id=number, has_side_effects=True),
+    )(padded)
+
+
+def y_bands(kernel, offset, block_y):
+    rim = HALF + SHIFT
+    band = band_matrix(kernel, offset, block_y, block_y + 2 * rim, rim).T
+    lanes = QUADS * RIM_LANES
+    stacks = []
+    for q in range(QUADS):
+        before = q * RIM_LANES
+        pads = ((before, lanes - before - rim), (0, 0))
+        stacks.append(
+            jnp.concatenate(
+                [band[rim:-rim], jnp.pad(band[:rim], pads), jnp.pad(band[-rim:], pads)], axis=0
+            )
+        )
+    return jnp.stack(stacks).astype(jnp.bfloat16)
+
+
+def rim_selects(block_y):
+    rim = HALF + SHIFT
+    row = lax.broadcasted_iota(jnp.int32, (QUADS * block_y, QUADS * RIM_LANES), 0)
+    lane = lax.broadcasted_iota(jnp.int32, (QUADS * block_y, QUADS * RIM_LANES), 1)
+    same = row // block_y == lane // RIM_LANES
+    place = lane % RIM_LANES
+    within = jnp.logical_and(same, place < rim)
+    spot = row % block_y
+    right = jnp.logical_and(within, spot == block_y - rim + place)
+    left = jnp.logical_and(within, spot == place)
+    return right.astype(jnp.bfloat16), left.astype(jnp.bfloat16)
+
+
+def kernel_shards(
+    observed, confidence, iterate, kernel_bank, tap_index, offsets,
+    basis_x, basis_y, basis_z, eigen_x, eigen_y, eigen_z,
+):
+    size_x, size_y = lax.axis_size("gx"), lax.axis_size("gy")
+    block_x, block_y, depth = iterate.shape
+    bf = jnp.bfloat16
+    kernels = kernels_of(kernel_bank, tap_index)
+    adjoint = kernels[:, ::-1]
+    full_x = lax.all_gather(basis_x, "gx", axis=0, tiled=True)
+    full_y = lax.all_gather(basis_y, "gy", axis=0, tiled=True)
+    all_x = lax.all_gather(eigen_x, "gx", axis=0, tiled=True)
+    share_x = all_x.shape[0] // size_y
+    part_x = lax.dynamic_slice_in_dim(all_x, lax.axis_index("gy") * share_x, share_x)
+    share_z = depth // size_x
+    part_z = lax.dynamic_slice_in_dim(eigen_z, lax.axis_index("gx") * share_z, share_z)
+
+    wide_x = block_x + 2 * RIM_ROWS
+    x_band = band_matrix(kernels[0], offsets[0], block_x, wide_x, RIM_ROWS).astype(bf)
+    x_back = band_matrix(adjoint[0], -offsets[0], block_x, wide_x, RIM_ROWS).astype(bf)
+    y_band = y_bands(kernels[1], offsets[1], block_y)
+    y_back = y_bands(adjoint[1], -offsets[1], block_y)
+    z_band = band_matrix(kernels[2], offsets[2], depth, depth, 0)
+    selects = rim_selects(block_y)
+    basis_f = basis_z.astype(jnp.float32)
+    blurring = jnp.dot(z_band, basis_f, precision=highest)
+    entry = jnp.concatenate([z_band.astype(bf), basis_z.T], axis=0)
+
+    along_z, plain = to_modes(iterate, entry)
+    rims = spread(along_z, x_band, selects, size_x, size_y, 1)
+    misfit, weighted = find_misfit(
+        *rims, observed, confidence, y_band, blurring.T.astype(bf)
+    )
+    section_one = spread(
+        weighted, x_back, selects, size_x, size_y, 2, (y_back, plain)
+    )[0]
+    section_six = transform(
+        section_one.reshape(depth, block_x, block_y), full_x.T, full_x, full_y, full_y.T,
+        part_x[:, None] * eigen_y[None, :], part_z, size_x, size_y,
+    ).reshape(section_one.shape)
+    rims = spread(section_six, x_band, selects, size_x, size_y, 3)
+    coarse = blurring.T.astype(bf)
+    fine = (blurring.T - coarse.astype(jnp.float32)).astype(bf)
+    direction, blurred, sums = find_direction(
+        *rims, section_six, section_one, confidence, y_band, basis_z.T,
+        jnp.concatenate([coarse, fine], axis=0),
+    )
+    totals = jnp.sum(total_sums(sums, size_x, size_y, 4), axis=1)
+    step_size = totals[0] / (totals[1] + tikhonov * totals[2])
+    return (iterate + step_size * direction, misfit - step_size * blurred)
+
+
+def kernels_fit(block, size_x, size_y):
+    block_x, block_y, depth = block
+    return (
+        block_y == 128
+        and depth == 128
+        and block_x == 256
+        and depth // size_x == 32
+        and block_x * size_x // size_y == 128
+        and block_y * size_y % 256 == 0
+    )
+
+
+def step_shards(*arrays):
+    fits = kernels_fit(arrays[2].shape, lax.axis_size("gx"), lax.axis_size("gy"))
+    return (kernel_shards if fits else shards)(*arrays)
+
+
 def solution(mesh):
     return jax.shard_map(
-        shards,
+        step_shards,
         mesh=mesh,
         in_specs=(
             P("gx", "gy", None),

time: 1160 us -> 794 us (0.68)
  Pallas kernels: 0 us -> 684 us
  waiting for transfers between devices: 341 us -> 0.7 us
  matrix products: 298 us -> 0.24 us
  local copies, waits for them, and re-layouts: 201 us -> 36.5 us
  starting transfers between devices: 157 us -> 0.08 us
  other arithmetic: 85.1 us -> 40.6 us
  blocking collectives: 56 us -> 13 us
    pallas_call x0 -> x8, Pallas kernels: none -> 684 us  [the longest x1 377 us: transform(): pl.pallas_call(functools.partial(transform_kernel, parts, size_x, size_y)...]
    ppermute x52 -> x0, waiting for transfers between devices: 340 us -> none  [the longest x40 335 us: swap(): arrived.append(lax.ppermute(pieces[step], axis_name, pairs))]
    dot_general x22 -> x1, matrix products: 298 us -> 0.24 us  [kernel_shards(): blurring = jnp.dot(z_band, basis_f, precision=highest)]
    ppermute x52 -> x0, starting transfers between devices: 157 us -> none  [the longest x40 109 us: swap(): arrived.append(lax.ppermute(pieces[step], axis_name, pairs))]
    unnamed x163 -> x30, local copies, waits for them, and re-layouts: 118 us -> 22.7 us
    psum x1 -> x0, blocking collectives: 45.3 us -> none  [shards(): descent = lax.psum(local_descent, ('gx', 'gy'))]
    concatenate x10 -> x2, other arithmetic: 36.7 us -> 0.01 us  [the longest x1 0.01 us: kernel_shards(): jnp.concatenate([coarse, fine], axis=0)]
    concatenate x10 -> x0, local copies, waits for them, and re-layouts: 30 us -> none  [the longest x2 14.5 us: shards(): section_six = jnp.concatenate(found, axis=0)]
  transfers between devices with their start and end apart: 54 -> 2, of which waited for: 20 -> 0; matrix products, arithmetic and copies ran while one was open for 33% -> 3% of each run, Pallas kernels for 0% -> 23%
where the time goes in v2:
time: 794 us; the launch traced here: 793 us
  Pallas kernels  684 us (86%)
  other arithmetic  40.6 us (5%)
  local copies, waits for them, and re-layouts  36.5 us (5%)
  between operations  17.6 us (2%)
  blocking collectives  13 us (2%)
    pallas_call x1, Pallas kernels, transform(): pl.pallas_call(functools.partial(transform_kernel, parts, size_x, size_y)...  377 us
    pallas_call x3, Pallas kernels, spread(): pl.pallas_call(functools.partial(spread_kernel, size_x, size_y, parts, bo...  174 us
    pallas_call x1, Pallas kernels, total_sums(): pl.pallas_call(functools.partial(total_kernel, size_x, size_y), out_shape...  37.3 us
    pallas_call x1, Pallas kernels, find_direction(): pl.pallas_call(direction_kernel, grid=(shape[2] // BAND_ROWS,), out_shape...  35.7 us
    pallas_call x1, Pallas kernels, find_misfit(): pl.pallas_call(misfit_kernel, grid=(shape[2] // BAND_ROWS,), out_shape=[j...  33.2 us
    pallas_call x1, Pallas kernels, to_modes(): pl.pallas_call(to_modes_kernel, grid=(block_x // BAND_ROWS,), out_shape=[...  26.8 us
    unnamed x30, local copies, waits for them, and re-layouts  22.7 us
    add x1, other arithmetic, kernel_shards(): return (iterate + step_size * direction, misfit - step_size * blurred)  17.8 us
  transfers between devices with their start and end apart: 2, of which 0 were waited for; matrix products, arithmetic and copies ran while one was open for 3% of the time, Pallas kernels for 23%

profile of v2, /device:TPU:0, one launch (start us, length us, event | category | flops | bytes accessed | tf_op | source)
XLA Modules:
  0.0 792.7 jit_solution(8549281494139794184)
XLA Ops:
  7.9 1.8 copy.31
  9.8 1.4 fusion.46
  13.3 0.9 select_reduce_fusion.5
  14.4 0.9 copy.28
  16.3 1.1 select_reduce_fusion
  18.3 1.1 select_reduce_fusion.1
  20.2 1.3 dynamic_slice.7.eigen_z
  21.5 13.0 %all-gather = f32[4,1,256]{2,1,0:T(1,128)S(1)} all-gather(f32[1,1,256]{2,1,0:T(1,128)} %bitcast.55), channel_id=1, replica_groups=mesh['gx'=4,'gy'=8] {'gx'}, dimensions={0}, use_global_device_ids=true | all-gather | bytes 5120 | tf_op jit(solution)/shard_map/all_gather | solution.py:788
  34.6 26.8 %shard_map.131 = (bf16[4,32,256,128]{3,2,1,0:T(8,128)(2,1)S(1)}, bf16[4,32,256,128]{3,2,1,0:T(8,128)(2,1)}) custom-call(bf16[256,128]{1,0:T(8,128)(2,1)S(1)} %pad_maximum_fusion.10.matrix, f32[256,128,128]{2,1,0:T(8,128)} %source.1), custom_call_target="tpu_custom_call" | custom-call | tf_op jit(solution)/shard_map/pallas_call | solution.py:421
  61.4 3.4 copy-done.1
  64.9 1.3 fusion.6
  66.2 39.1 %shard_map.132 = (bf16[4,32,256,128]{3,2,1,0:T(8,128)(2,1)}, bf16[32,256,128]{2,1,0:T(8,128)(2,1)}, bf16[32,256,128]{2,1,0:T(8,128)(2,1)}) custom-call(bf16[4,32,256,128]{3,2,1,0:T(8,128)(2,1)} %copy-done.1, bf16[256,320]{1,0:T(8,128)(2,1)} %copy.29.x_band, bf16[512,128]{1,0:T(8,128)(2,1)} %get-tuple-element.49.to_right, ...), custom_call_target="tpu_custom_call" | custom-call | tf_op jit(solution)/shard_map/pallas_call | solution.py:577
  107.2 1.6 copy-done.3
  108.8 1.6 copy-done.4
  110.4 33.2 %shard_map.133 = (f32[256,128,128]{2,1,0:T(8,128)}, bf16[4,32,256,128]{3,2,1,0:T(8,128)(2,1)S(1)}) custom-call(bf16[4,32,256,128]{3,2,1,0:T(8,128)(2,1)} %get-tuple-element.16.along, bf16[32,256,128]{2,1,0:T(8,128)(2,1)S(1)} %copy-done.3, bf16[32,256,128]{2,1,0:T(8,128)(2,1)S(1)} %copy-done.4, bf16[256,128,128]{2,1,0:T(8,128)(2,1)} %observed.1, ...), custom_call_target="tpu_custom_call" | custom-call | tf_op jit(solution)/shard_map/pallas_call | solution.py:619
  143.5 3.3 copy-done
  147.7 85.0 %shard_map.134.section_one = bf16[4,32,256,128]{3,2,1,0:T(8,128)(2,1)} custom-call(bf16[4,32,256,128]{3,2,1,0:T(8,128)(2,1)} %copy-done, bf16[256,320]{1,0:T(8,128)(2,1)} %copy.30.x_band, bf16[512,128]{1,0:T(8,128)(2,1)} %get-tuple-element.49.to_right, bf16[512,128]{1,0:T(8,128)(2,1)} %get-tuple-element.48.to_left, ...), custom_call_target="tpu_custom_call" | custom-call | tf_op jit(solution)/shard_map/pallas_call | solution.py:577
  232.7 0.9 broadcast_multiply_fusion.eigen_xy
  233.6 3.9 copy.32.x_fwd
  237.6 3.9 copy.33.y_fwd
  241.5 376.9 %shard_map.135 = bf16[128,256,128]{2,1,0:T(8,128)(2,1)} custom-call(bf16[128,256,128]{2,1,0:T(8,128)(2,1)} %bitcast.43, bf16[1024,1024]{1,0:T(8,128)(2,1)} %copy.32.x_fwd, bf16[1024,1024]{1,0:T(8,128)(2,1)} %all-gather.4.cloned.1.call-done.x_inv, bf16[1024,1024]{1,0:T(8,128)(2,1)} %copy.33.y_fwd, bf16[1024,1024]{1,0:T(8,128)(2,1)} %bitcast.49, ...), custom_call_target="tpu_custom_call" | custom-call | tf_op jit(solution)/shard_map/pallas_call | solution.py:362
  618.4 50.0 %shard_map.136 = (bf16[4,32,256,128]{3,2,1,0:T(8,128)(2,1)}, bf16[32,256,128]{2,1,0:T(8,128)(2,1)}, bf16[32,256,128]{2,1,0:T(8,128)(2,1)}) custom-call(bf16[4,32,256,128]{3,2,1,0:T(8,128)(2,1)} %bitcast.44, bf16[256,320]{1,0:T(8,128)(2,1)} %copy.29.x_band, bf16[512,128]{1,0:T(8,128)(2,1)} %get-tuple-element.49.to_right, ...), custom_call_target="tpu_custom_call" | custom-call | tf_op jit(solution)/shard_map/pallas_call | solution.py:577
  668.4 3.4 copy-done.2
  671.8 1.6 copy-done.5
  673.4 1.6 copy-done.6
  675.0 35.7 %shard_map.137 = (f32[256,128,128]{2,1,0:T(8,128)}, f32[256,128,128]{2,1,0:T(8,128)}, f32[3,8,128]{2,1,0:T(8,128)S(1)}) custom-call(bf16[4,32,256,128]{3,2,1,0:T(8,128)(2,1)S(1)} %copy-done.2, bf16[32,256,128]{2,1,0:T(8,128)(2,1)S(1)} %copy-done.5, bf16[32,256,128]{2,1,0:T(8,128)(2,1)S(1)} %copy-done.6, bf16[4,32,256,128]{3,2,1,0:T(8,128)(2,1)} %bitcast.45, ...), custom_call_target="tpu_custom_call" | custom-call | tf_op jit(solution)/shard_map/pallas_call | solution.py:674
  711.3 37.3 %shard_map.138 = f32[8,128]{1,0:T(8,128)} custom-call(f32[8,8,128]{2,1,0:T(8,128)} %pad.86.values), custom_call_target="tpu_custom_call" | custom-call | tf_op jit(solution)/shard_map/pallas_call | solution.py:733
  751.9 17.8 %multiply_add_fusion = f32[256,128,128]{2,1,0:T(8,128)} fusion(f32[256,128,128]{2,1,0:T(8,128)} %source.1, f32[256,128,128]{2,1,0:T(8,128)} %get-tuple-element.25, f32[]{:T(128)} %bitcast.26), kind=kLoop, calls=%fused_computation.1 | loop fusion | flops 8388608 | bytes 50331652 | tf_op jit(solution)/shard_map/add | solution.py:826
  769.8 1.3 slice-done.1
  771.0 1.2 slice-done.2
  772.2 1.2 slice-done.3
  773.4 12.4 %multiply_subtract_fusion = f32[256,128,128]{2,1,0:T(8,128)} fusion(f32[256,128,128]{2,1,0:T(8,128)S(1)} %bitcast.47, f32[256,128,128]{2,1,0:T(8,128)} %get-tuple-element.27, f32[]{:T(128)} %bitcast.26), kind=kLoop, calls=%fused_computation | loop fusion | flops 8388608 | bytes 50331652 | tf_op jit(solution)/shard_map/sub | solution.py:826
  (60 shorter events, 9.3 us)
Async XLA Ops:
  7.2 226.5 %all-gather.4.cloned.1.call-start = ((), (), s32[]{:S(2)}) async-start(), calls=%async_computation | async-start | bytes 2621440 | tf_op jit(solution)/shard_map/all_gather | solution.py:786
  7.9 229.7 %all-gather.6.cloned.1.call-start = ((), (), s32[]{:S(2)}) async-start(), calls=%async_computation.1 | async-start | bytes 2359296 | tf_op jit(solution)/shard_map/all_gather | solution.py:787
  61.4 3.4 copy-start.1
  64.8 41.9 %copy-start.9 = (pred[128]{0:T(512)(128)(4,1)S(1)}, pred[128]{0:T(512)(128)(4,1)}, u32[]{:S(2)}) copy-start(pred[128]{0:T(512)(128)(4,1)} %constant.90.clone.1) | copy-start | bytes 388
  64.8 42.1 %copy-start.7 = (bf16[128,128]{1,0:T(8,128)(2,1)S(1)}, bf16[128,128]{1,0:T(8,128)(2,1)}, u32[]{:S(2)}) copy-start(bf16[128,128]{1,0:T(8,128)(2,1)} %param.20) | copy-start | bytes 98308
  107.2 1.6 copy-start.3
  108.8 1.6 copy-start.4
  143.5 3.3 copy-start
  147.7 85.1 %copy-start.8 = (f32[1024]{0:T(1024)S(1)}, f32[1024]{0:T(1024)}, u32[]{:S(2)}) copy-start(f32[1024]{0:T(1024)} %param.22) | copy-start | bytes 12292
  668.4 3.4 copy-start.2
  671.8 1.6 copy-start.5
  673.4 1.6 copy-start.6
  751.9 17.9 %slice-start = ((s8[16777216]{0:T(1024)(128)(4,1)}), s8[4194304]{0:T(1024)(128)(4,1)S(1)}, s32[]{:S(2)}) async-start(s8[16777216]{0:T(1024)(128)(4,1)} %bitcast.46), calls=%async_computation.2 | async-start | bytes 8388608
  751.9 19.1 %slice-start.1 = ((s8[16777216]{0:T(1024)(128)(4,1)}), s8[4194304]{0:T(1024)(128)(4,1)S(1)}, s32[]{:S(2)}) async-start(s8[16777216]{0:T(1024)(128)(4,1)} %bitcast.46), calls=%async_computation.3 | async-start | bytes 8388608
  751.9 20.3 %slice-start.2 = ((s8[16777216]{0:T(1024)(128)(4,1)}), s8[4194304]{0:T(1024)(128)(4,1)S(1)}, s32[]{:S(2)}) async-start(s8[16777216]{0:T(1024)(128)(4,1)} %bitcast.46), calls=%async_computation.4 | async-start | bytes 8388608
  751.9 21.5 %slice-start.3 = ((s8[16777216]{0:T(1024)(128)(4,1)}), s8[4194304]{0:T(1024)(128)(4,1)S(1)}, s32[]{:S(2)}) async-start(s8[16777216]{0:T(1024)(128)(4,1)} %bitcast.46), calls=%async_computation.5 | async-start | bytes 8388608
Sparse Core Ops, SparseCore 0:
  9.6 48.6 all-gather.3
  60.1 29.7 all-gather.5

commit v3 on v2

--- a/solution.py
+++ b/solution.py
@@ -186,21 +186,22 @@
 
 def transform_kernel(
     parts, size_x, size_y,
-    section_ref, x_fwd, x_inv, y_fwd, y_inv, eigen_xy, eigen_z,
-    out_ref,
-    lines_x, lines_y, lines_back, send_a, send_b, send_c, modes,
-    fs, fr, gs, gr, hs, hr, bs, br, fl, gl, hl, bl,
+    weighted, plain, x_back, x_band, y_band, rim_select, x_fwd, x_inv, y_fwd, eigen_xy, eigen_z,
+    section_one, section_six, spread_out, left_out, right_out,
+    lines_x, lines_y, lines_back, send_a, send_b, send_c, modes, along, low, high, rims,
+    from_left, from_right,
+    fs, fr, gs, gr, hs, hr, bs, br, fl, gl, hl, bl, xs, xr, ys, yr, us, ur, vs, vr, loads,
 ):
     me_x = lax.axis_index("gx")
     me_y = lax.axis_index("gy")
-    depth = lines_x.shape[0]
-    full = lines_x.shape[1]
+    depth, full = lines_x.shape[0], lines_x.shape[1]
     block_y = lines_x.shape[2]
-    block_x = section_ref.shape[1]
-    share = lines_y.shape[1]
-    full_y = lines_y.shape[2]
+    block_x = section_one.shape[2]
+    share, full_y = lines_y.shape[1], lines_y.shape[2]
     part = depth // parts
     slots = send_a.shape[0]
+    halves = block_x // share
+    bf = jnp.bfloat16
 
     barrier = pltpu.get_barrier_semaphore()
     for step in range(1, size_x):
@@ -213,13 +214,70 @@
         )
     pl.semaphore_wait(barrier, size_x + size_y - 2)
 
+    has = (me_x > 0, me_x < size_x - 1, me_y > 0, me_y < size_y - 1)
+    peers = ((me_x - 1, me_y), (me_x + 1, me_y), (me_x, me_y - 1), (me_x, me_y + 1))
+
+    def remote(src, dst, send, receive, peer):
+        return pltpu.make_async_remote_copy(
+            src, dst, send, receive, device_id=peer, device_id_type=MESH_ID
+        )
+
+    def x_halo(source, sends, receives):
+        def copy(c, way):
+            here = pl.ds(c * part, part)
+            if way == 0:
+                src, dst = source.at[here, :, pl.ds(0, RIM_ROWS)], high.at[here]
+            else:
+                src = source.at[here, :, pl.ds(block_x - RIM_ROWS, RIM_ROWS)]
+                dst = low.at[here]
+            return remote(src, dst, sends.at[c, way], receives.at[c, way], peers[way])
+
+        return copy, 0
+
+    def y_halo(landing, sends, receives):
+        def copy(c, way):
+            src = rims.at[c % slots, 1 - way]
+            dst = landing[1 - way].at[pl.ds(c * part, part)]
+            return remote(src, dst, sends.at[c, way], receives.at[c, way], peers[2 + way])
+
+        return copy, 2
+
+    def halo_start(kind, c):
+        copy, base = kind
+        for way in range(2):
+
+            @pl.when(has[base + way])
+            def _():
+                copy(c, way).start()
+
+    def halo_landed(kind, c):
+        copy, base = kind
+        for way in range(2):
+
+            @pl.when(has[base + 1 - way])
+            def _():
+                copy(c, way).wait_recv()
+
+    def halo_sent(kind, c):
+        copy, base = kind
+        for way in range(2):
+
+            @pl.when(has[base + way])
+            def _():
+                copy(c, way).wait_send()
+
+    def local(source, target, kind, c):
+        return pltpu.make_async_copy(source, target, loads.at[kind, c])
+
+    def whole(ref, c):
+        return ref.at[pl.ds(c * part, part)]
+
     def copies(kind, c):
         out = []
         here = pl.ds(c * part, part)
         slot = c % slots
         count = size_x if kind in "fb" else size_y
         for step in range(count):
-            mine = step == 0
             if kind in "fb":
                 peer = lax.rem(me_x + step, size_x)
                 target = (peer, me_y)
@@ -227,11 +285,13 @@
                 peer = lax.rem(me_y + step, size_y)
                 target = (me_x, peer)
             if kind == "f":
-                src = section_ref.at[pl.ds(peer * depth + c * part, part)]
+                src = section_one.at[here, peer]
                 dst = lines_x.at[here, pl.ds(me_x * block_x, block_x)]
                 sems = fs, fr, fl
             elif kind == "g":
-                src = send_a.at[slot, :, pl.ds(peer * share, share)]
+                src = send_a.at[
+                    slot, :, peer // halves, pl.ds(lax.rem(peer, halves) * share, share)
+                ]
                 dst = lines_y.at[here, :, pl.ds(me_y * block_y, block_y)]
                 sems = gs, gr, gl
             elif kind == "h":
@@ -239,18 +299,13 @@
                 dst = lines_back.at[here, pl.ds(me_y * share, share)]
                 sems = hs, hr, hl
             else:
-                src = send_c.at[slot, :, pl.ds(peer * block_x, block_x)]
-                dst = out_ref.at[pl.ds(me_x * depth + c * part, part)]
+                src = send_c.at[slot, :, peer]
+                dst = section_six.at[here, me_x]
                 sems = bs, br, bl
-            if mine:
+            if step == 0:
                 out.append(pltpu.make_async_copy(src, dst, sems[2].at[c]))
             else:
-                out.append(
-                    pltpu.make_async_remote_copy(
-                        src, dst, sems[0].at[c, step], sems[1].at[c, step],
-                        device_id=target, device_id_type=MESH_ID,
-                    )
-                )
+                out.append(remote(src, dst, sems[0].at[c, step], sems[1].at[c, step], target))
         return out
 
     every = {kind: [copies(kind, c) for c in range(parts)] for kind in "fghb"}
@@ -278,12 +333,13 @@
         def pair(i, carry):
             k = c * part + 2 * i
             both = jnp.concatenate([lines[k], lines[k + 1]], axis=1)
-            for b in range(0, full, 256):
+            for b in range(full // block_x):
                 found = jnp.dot(
-                    matrix[pl.ds(b, 256), :], both, preferred_element_type=jnp.float32
-                ).astype(jnp.bfloat16)
-                out[c % slots, 2 * i, pl.ds(b, 256)] = found[:, :block_y]
-                out[c % slots, 2 * i + 1, pl.ds(b, 256)] = found[:, block_y:]
+                    matrix[pl.ds(b * block_x, block_x), :], both,
+                    preferred_element_type=jnp.float32,
+                ).astype(bf)
+                out[c % slots, 2 * i, b] = found[:, :block_y]
+                out[c % slots, 2 * i + 1, b] = found[:, block_y:]
             return carry
 
         lax.fori_loop(0, part // 2, pair, 0)
@@ -297,23 +353,96 @@
                 weight = eigen_xy[:, pl.ds(b, 256)]
                 modes[pl.ds(0, share), pl.ds(b, 256)] = (
                     found[:share] / (weight * eigen_z[k] + tikhonov)
-                ).astype(jnp.bfloat16)
+                ).astype(bf)
                 modes[pl.ds(share, share), pl.ds(b, 256)] = (
                     found[share:] / (weight * eigen_z[k + 1] + tikhonov)
-                ).astype(jnp.bfloat16)
+                ).astype(bf)
             for b in range(0, full_y, 256):
-                found = jnp.dot(
-                    modes[...], y_inv[:, pl.ds(b, 256)], preferred_element_type=jnp.float32
-                ).astype(jnp.bfloat16)
+                found = lax.dot_general(
+                    modes[...], y_fwd[pl.ds(b, 256), :], (((1,), (1,)), ((), ())),
+                    preferred_element_type=jnp.float32,
+                ).astype(bf)
                 send_b[c % slots, 2 * i, :, pl.ds(b, 256)] = found[:share]
                 send_b[c % slots, 2 * i + 1, :, pl.ds(b, 256)] = found[share:]
             return carry
 
         lax.fori_loop(0, part // 2, pair, 0)
 
-    ahead = min(2, parts)
-    for c in range(ahead):
-        start("f", c)
+    def blur_x(source, band, c):
+        def step(i, carry):
+            blur_x_lines(
+                [source[c % slots, i, q] for q in range(QUADS)],
+                low.at[c * part + i], high.at[c * part + i], band,
+                along.at[c % slots, i], rims.at[c % slots, 0, i], rims.at[c % slots, 1, i],
+                rim_select,
+            )
+            return carry
+
+        lax.fori_loop(0, part, step, 0)
+
+    def blur_y(c):
+        some = part // 2
+
+        def step(i, carry):
+            here = pl.ds(i * some, some)
+            there = pl.ds(c * part + i * some, some)
+            rows = some * block_x
+            sides = [r[there].reshape(rows, block_y) for r in (from_left, from_right)]
+            for q in range(QUADS):
+                wide = jnp.concatenate(
+                    [along[c % slots, here, q].reshape(rows, block_y)] + sides, axis=1
+                )
+                found = jnp.dot(wide, y_band[q], preferred_element_type=jnp.float32)
+                term = send_c[c % slots, here, q].reshape(rows, block_y).astype(jnp.float32)
+                send_c[c % slots, here, q] = (
+                    (found - tikhonov * term).astype(bf).reshape(some, block_x, block_y)
+                )
+            return carry
+
+        lax.fori_loop(0, 2, step, 0)
+
+    x_first = x_halo(weighted, xs, xr)
+    y_first = y_halo((from_left, from_right), ys, yr)
+    load_u = [local(whole(weighted, c), send_a.at[c % slots], 0, c) for c in range(parts)]
+    load_p = [local(whole(plain, c), send_c.at[c % slots], 1, c) for c in range(parts)]
+    store_one = [local(send_c.at[c % slots], whole(section_one, c), 2, c) for c in range(parts)]
+    for c in range(parts):
+        halo_start(x_first, c)
+    for c in range(slots):
+        load_u[c].start()
+        load_p[c].start()
+    for there, ref in zip(has, (low, high, from_left, from_right)):
+
+        @pl.when(jnp.logical_not(there))
+        def _():
+            ref[...] = jnp.zeros_like(ref)
+
+    ahead = 2
+    for c in range(parts + 1):
+        if c < parts:
+            load_u[c].wait()
+            halo_landed(x_first, c)
+            if c >= slots:
+                halo_sent(y_first, c - slots)
+            blur_x(send_a, x_back, c)
+            halo_start(y_first, c)
+            if c + slots < parts:
+                load_u[c + slots].start()
+        if c > 0:
+            halo_landed(y_first, c - 1)
+            load_p[c - 1].wait()
+            blur_y(c - 1)
+            store_one[c - 1].start()
+            store_one[c - 1].wait()
+            if c - 1 < ahead:
+                start("f", c - 1)
+            if c - 1 + slots < parts:
+                load_p[c - 1 + slots].start()
+    for c in range(parts):
+        halo_sent(x_first, c)
+        if c >= parts - slots:
+            halo_sent(y_first, c)
+
     for step in range(parts + 2):
         c = step
         if c < parts:
@@ -339,48 +468,120 @@
             along_x(x_inv, lines_back, send_c, c)
             start("b", c)
     for c in range(parts):
-        landed("b", c)
         sent("f", c)
         if c >= parts - slots:
             sent("g", c)
             sent("h", c)
-            sent("b", c)
-
-
-def transform(section, x_fwd, x_inv, y_fwd, y_inv, eigen_xy, eigen_z, size_x, size_y):
-    modes_z, block_x, block_y = section.shape
-    depth = modes_z // size_x
+
+    x_last = x_halo(section_six, us, ur)
+    y_last = y_halo((left_out, right_out), vs, vr)
+    load_s = [local(whole(section_six, c), send_a.at[c % slots], 3, c) for c in range(parts)]
+    store_a = [local(along.at[c % slots], whole(spread_out, c), 4, c) for c in range(parts)]
+    empty = [
+        pltpu.make_async_copy(ref, out, loads.at[5, n])
+        for n, (ref, out) in enumerate(((from_left, left_out), (from_right, right_out)))
+    ]
+    for there, copy in zip(has[2:], empty):
+
+        @pl.when(jnp.logical_not(there))
+        def _():
+            copy.start()
+
+    for c in range(parts + 1):
+        if c < parts:
+            if c >= parts - slots:
+                sent("b", c)
+            landed("b", c)
+            halo_start(x_last, c)
+            load_s[c].start()
+        if c > 0:
+            d = c - 1
+            load_s[d].wait()
+            halo_landed(x_last, d)
+            if d >= slots:
+                halo_sent(y_last, d - slots)
+                store_a[d - slots].wait()
+            blur_x(send_a, x_band, d)
+            halo_start(y_last, d)
+            store_a[d].start()
+    for c in range(parts):
+        halo_landed(y_last, c)
+        halo_sent(x_last, c)
+        if c >= parts - slots:
+            halo_sent(y_last, c)
+            store_a[c].wait()
+    for there, copy in zip(has[2:], empty):
+
+        @pl.when(jnp.logical_not(there))
+        def _():
+            copy.wait()
+
+
+def transform(
+    weighted, plain, x_back, x_band, y_back, rim_select, x_fwd, x_inv, y_fwd, eigen_xy, eigen_z,
+    size_x, size_y,
+):
+    depth, quads, block_x, block_y = weighted.shape
     full_x, full_y = x_fwd.shape[0], y_fwd.shape[0]
     share = full_x // size_y
     parts = PARTS
     part = depth // parts
     slots = 2
     vmem = pl.BlockSpec(memory_space=pltpu.VMEM)
+    hbm = pl.BlockSpec(memory_space=pl.ANY)
     sem = lambda n: pltpu.SemaphoreType.DMA((parts, n))
     one = pltpu.SemaphoreType.DMA((parts,))
     bf = jnp.bfloat16
+    modes = jax.ShapeDtypeStruct(weighted.shape, bf)
+    side = jax.ShapeDtypeStruct((depth, block_x, block_y), bf)
+    chunk = pltpu.VMEM((slots, part, quads, block_x, block_y), bf)
+    edge = pltpu.VMEM((depth, quads, RIM_ROWS, block_y), bf)
     return pl.pallas_call(
         functools.partial(transform_kernel, parts, size_x, size_y),
-        out_shape=jax.ShapeDtypeStruct(section.shape, bf),
-        in_specs=[pl.BlockSpec(memory_space=pl.ANY)] + [vmem] * 5
-        + [pl.BlockSpec(memory_space=pltpu.SMEM)],
-        out_specs=pl.BlockSpec(memory_space=pl.ANY),
+        out_shape=[modes, modes, modes, side, side],
+        in_specs=[hbm, hbm] + [vmem] * 8 + [pl.BlockSpec(memory_space=pltpu.SMEM)],
+        out_specs=[hbm] * 5,
         scratch_shapes=[
             pltpu.VMEM((depth, full_x, block_y), bf),
             pltpu.VMEM((depth, share, full_y), bf),
             pltpu.VMEM((depth, full_x, block_y), bf),
-            pltpu.VMEM((slots, part, full_x, block_y), bf),
+            chunk,
             pltpu.VMEM((slots, part, share, full_y), bf),
-            pltpu.VMEM((slots, part, full_x, block_y), bf),
+            chunk,
             pltpu.VMEM((2 * share, full_y), bf),
+            chunk,
+            edge, edge,
+            pltpu.VMEM((slots, 2, part, block_x, block_y), bf),
+            pltpu.VMEM(side.shape, bf), pltpu.VMEM(side.shape, bf),
             sem(size_x), sem(size_x), sem(size_y), sem(size_y),
             sem(size_y), sem(size_y), sem(size_x), sem(size_x),
             one, one, one, one,
+            sem(2), sem(2), sem(2), sem(2), sem(2), sem(2), sem(2), sem(2),
+            pltpu.SemaphoreType.DMA((6, parts)),
         ],
         compiler_params=pltpu.CompilerParams(
-            collective_id=0, has_side_effects=True, vmem_limit_bytes=60 * 2**20
+            collective_id=0, has_side_effects=True, vmem_limit_bytes=62 * 2**20
         ),
-    )(section, x_fwd, x_inv, y_fwd, y_inv, eigen_xy, eigen_z)
+    )(
+        weighted, plain, x_back, x_band, y_back, rim_select, x_fwd, x_inv, y_fwd, eigen_xy, eigen_z
+    )
+
+
+def blur_x_lines(lines, low, high, band, along, to_right, to_left, rim_select):
+    half = lines[0].shape[1]
+    for q in range(0, QUADS, 2):
+        both = jnp.concatenate(
+            [jnp.concatenate([low[p], lines[p], high[p]], axis=0) for p in (q, q + 1)], axis=1
+        )
+        found = jnp.dot(band[...], both, preferred_element_type=jnp.float32).astype(jnp.bfloat16)
+        along[q] = found[:, :half]
+        along[q + 1] = found[:, half:]
+    wide = jnp.concatenate([along[q] for q in range(QUADS)], axis=1)
+    found = jnp.dot(
+        wide, rim_select[...], preferred_element_type=jnp.float32
+    ).astype(jnp.bfloat16)
+    to_left[...] = found[:, half:]
+    to_right[...] = found[:, :half]
 
 
 BAND_ROWS = 16
@@ -398,8 +599,10 @@
         )
         held[:, x, :] = found[:, : source.shape[1]]
         held[:, x + 1, :] = found[:, source.shape[1] :]
-    first[...] = held[:depth].reshape(first.shape).astype(first.dtype)
-    second[...] = held[depth:].reshape(second.shape).astype(second.dtype)
+    groups = first.shape[0]
+    for q in range(QUADS):
+        first[:, q] = held[pl.ds(q * groups, groups)].astype(first.dtype)
+        second[:, q] = held[pl.ds(depth + q * groups, groups)].astype(second.dtype)
 
 
 def modes_block(rows, shape):
@@ -416,7 +619,7 @@
 
 def to_modes(source, matrix):
     block_x, block_y, depth = source.shape
-    shape = (QUADS, depth // QUADS, block_x, block_y)
+    shape = (depth // QUADS, QUADS, block_x, block_y)
     out = jax.ShapeDtypeStruct(shape, jnp.bfloat16)
     return pl.pallas_call(
         to_modes_kernel,
@@ -429,18 +632,14 @@
     )(matrix, source)
 
 
-def spread_kernel(size_x, size_y, parts, final, source, x_band, to_right, to_left, *rest):
-    if final:
-        y_band, plain, out, along, from_left, from_right = rest[:6]
-        rest = rest[6:]
-    else:
-        along, from_left, from_right = rest[:3]
-        rest = rest[3:]
-    low, high, right, left, xs, xr, ys, yr = rest
+def spread_kernel(
+    size_x, size_y, parts, source, x_band, rim_select, along, from_left, from_right,
+    low, high, right, left, xs, xr, ys, yr,
+):
     me_x = lax.axis_index("gx")
     me_y = lax.axis_index("gy")
     block_x = source.shape[2]
-    groups = source.shape[1]
+    groups = source.shape[0]
     part = groups // parts
     has = (me_x > 0, me_x < size_x - 1, me_y > 0, me_y < size_y - 1)
     peers = ((me_x - 1, me_y), (me_x + 1, me_y), (me_x, me_y - 1), (me_x, me_y + 1))
@@ -456,22 +655,23 @@
     def x_copy(c, way):
         here = pl.ds(c * part, part)
         if way == 0:
-            src, dst, peer = source.at[:, here, pl.ds(0, RIM_ROWS)], high.at[:, here], peers[0]
+            src, dst = source.at[here, :, pl.ds(0, RIM_ROWS)], high.at[here]
         else:
-            src = source.at[:, here, pl.ds(block_x - RIM_ROWS, RIM_ROWS)]
-            dst, peer = low.at[:, here], peers[1]
+            src = source.at[here, :, pl.ds(block_x - RIM_ROWS, RIM_ROWS)]
+            dst = low.at[here]
         return pltpu.make_async_remote_copy(
-            src, dst, xs.at[c, way], xr.at[c, way], device_id=peer, device_id_type=MESH_ID
+            src, dst, xs.at[c, way], xr.at[c, way], device_id=peers[way], device_id_type=MESH_ID
         )
 
     def y_copy(c, way):
         here = pl.ds(c * part, part)
         if way == 0:
-            src, dst, peer = left.at[here], from_right.at[here], peers[2]
+            src, dst = left.at[here], from_right.at[here]
         else:
-            src, dst, peer = right.at[here], from_left.at[here], peers[3]
+            src, dst = right.at[here], from_left.at[here]
         return pltpu.make_async_remote_copy(
-            src, dst, ys.at[c, way], yr.at[c, way], device_id=peer, device_id_type=MESH_ID
+            src, dst, ys.at[c, way], yr.at[c, way], device_id=peers[2 + way],
+            device_id_type=MESH_ID,
         )
 
     for c in range(parts):
@@ -490,50 +690,21 @@
     def blur_x(c):
         def step(i, carry):
             g = c * part + i
-            for q in range(0, QUADS, 2):
-                both = jnp.concatenate(
-                    [
-                        jnp.concatenate([low[p, g], source[p, g], high[p, g]], axis=0)
-                        for p in (q, q + 1)
-                    ],
-                    axis=1,
-                )
-                found = jnp.dot(
-                    x_band[...], both, preferred_element_type=jnp.float32
-                ).astype(jnp.bfloat16)
-                along[q, g] = found[:, : found.shape[1] // 2]
-                along[q + 1, g] = found[:, found.shape[1] // 2 :]
-            wide = jnp.concatenate([along[q, g] for q in range(QUADS)], axis=1)
-            right[g] = jnp.dot(
-                wide, to_right[...], preferred_element_type=jnp.float32
-            ).astype(jnp.bfloat16)
-            left[g] = jnp.dot(
-                wide, to_left[...], preferred_element_type=jnp.float32
-            ).astype(jnp.bfloat16)
+            blur_x_lines(
+                [source[g, q] for q in range(QUADS)], low.at[g], high.at[g], x_band,
+                along.at[g], right.at[g], left.at[g], rim_select,
+            )
             return carry
 
         lax.fori_loop(0, part, step, 0)
 
-    def blur_y(c):
-        def step(i, carry):
-            g = c * part + i
-            for q in range(QUADS):
-                wide = jnp.concatenate([along[q, g], from_left[g], from_right[g]], axis=1)
-                found = jnp.dot(wide, y_band[q], preferred_element_type=jnp.float32)
-                out[q, g] = (found - tikhonov * plain[q, g].astype(jnp.float32)).astype(out.dtype)
-            return carry
-
-        lax.fori_loop(0, part, step, 0)
-
-    def receive(copy, c):
+    for c in range(parts):
         for way in range(2):
 
-            @pl.when(has[(0, 2)[copy is y_copy] + 1 - way])
+            @pl.when(has[1 - way])
             def _():
-                copy(c, way).wait_recv()
-
-    for c in range(parts):
-        receive(x_copy, c)
+                x_copy(c, way).wait_recv()
+
         blur_x(c)
         for way in range(2):
 
@@ -541,17 +712,12 @@
             def _():
                 y_copy(c, way).start()
 
-        if final and c > 0:
-            receive(y_copy, c - 1)
-            blur_y(c - 1)
-    if final:
-        receive(y_copy, parts - 1)
-        blur_y(parts - 1)
-    else:
-        for c in range(parts):
-            receive(y_copy, c)
     for c in range(parts):
         for way in range(2):
+
+            @pl.when(has[3 - way])
+            def _():
+                y_copy(c, way).wait_recv()
 
             @pl.when(has[way])
             def _():
@@ -562,37 +728,33 @@
                 y_copy(c, way).wait_send()
 
 
-def spread(source, x_band, selects, size_x, size_y, number, final=()):
-    quads, groups, block_x, block_y = source.shape
+def spread(source, x_band, rim_select, size_x, size_y, number):
+    groups, quads, block_x, block_y = source.shape
     bf = jnp.bfloat16
     whole = jax.ShapeDtypeStruct(source.shape, bf)
     rims = jax.ShapeDtypeStruct((groups, block_x, block_y), bf)
     vmem = pl.BlockSpec(memory_space=pltpu.VMEM)
-    parts = PARTS
-    outs = [whole] if final else [whole, rims, rims]
-    scratch = [pltpu.VMEM(s.shape, bf) for s in (whole, rims, rims)] if final else []
-    edge = pltpu.VMEM((quads, groups, RIM_ROWS, block_y), bf)
+    edge = pltpu.VMEM((groups, quads, RIM_ROWS, block_y), bf)
     packed = pltpu.VMEM(rims.shape, bf)
-    sem = pltpu.SemaphoreType.DMA((parts, 2))
-    found = pl.pallas_call(
-        functools.partial(spread_kernel, size_x, size_y, parts, bool(final)),
-        out_shape=outs,
-        in_specs=[vmem] * (4 + len(final)),
-        out_specs=[vmem] * len(outs),
-        scratch_shapes=scratch + [edge, edge, packed, packed, sem, sem, sem, sem],
+    sem = pltpu.SemaphoreType.DMA((PARTS, 2))
+    return pl.pallas_call(
+        functools.partial(spread_kernel, size_x, size_y, PARTS),
+        out_shape=[whole, rims, rims],
+        in_specs=[vmem] * 3,
+        out_specs=[vmem] * 3,
+        scratch_shapes=[edge, edge, packed, packed, sem, sem, sem, sem],
         compiler_params=pltpu.CompilerParams(
             collective_id=number, has_side_effects=True, vmem_limit_bytes=56 * 2**20
         ),
-    )(source, x_band, *selects, *final)
-    return found
+    )(source, x_band, rim_select)
 
 
 def blur_y_rows(along, from_left, from_right, y_band, held):
-    quads, groups, rows, block_y = along.shape
+    groups, quads, rows, block_y = along.shape
     count = groups * rows
     sides = [from_left[...].reshape(count, block_y), from_right[...].reshape(count, block_y)]
     for q in range(quads):
-        wide = jnp.concatenate([along[q].reshape(count, block_y)] + sides, axis=1)
+        wide = jnp.concatenate([along[:, q].reshape(count, block_y)] + sides, axis=1)
         found = jnp.dot(wide, y_band[q], preferred_element_type=jnp.float32)
         held[pl.ds(q * groups, groups)] = found.reshape(groups, rows, block_y)
 
@@ -609,12 +771,14 @@
         turned_back[:, x, :] = lax.dot_general(
             matrix[...], lines, (((1,), (1,)), ((), ())), preferred_element_type=jnp.float32
         )
-    weighted[...] = turned_back[...].reshape(weighted.shape).astype(weighted.dtype)
+    groups = weighted.shape[0]
+    for q in range(QUADS):
+        weighted[:, q] = turned_back[pl.ds(q * groups, groups)].astype(weighted.dtype)
 
 
 def find_misfit(along, from_left, from_right, observed, confidence, y_band, matrix):
     shape, space = along.shape, observed.shape
-    rims = pl.BlockSpec((shape[1], BAND_ROWS, shape[3]), lambda i: (0, i, 0))
+    rims = pl.BlockSpec((shape[0], BAND_ROWS, shape[3]), lambda i: (0, i, 0))
     held = pltpu.VMEM((space[2], BAND_ROWS, shape[3]), jnp.float32)
     return pl.pallas_call(
         misfit_kernel,
@@ -649,7 +813,9 @@
     blur_y_rows(along, from_left, from_right, y_band, held)
     six = section_six[...].astype(jnp.float32)
     sums[0] += folded((six * section_one[...].astype(jnp.float32)).reshape(-1, six.shape[-1]))
-    held_six[...] = six.reshape(held_six.shape)
+    groups = six.shape[0]
+    for q in range(QUADS):
+        held_six[pl.ds(q * groups, groups)] = six[:, q]
     for x in range(confidence.shape[0]):
         lines = held_six[:, x, :].T.astype(jnp.bfloat16)
         found = jnp.dot(lines, basis[...], preferred_element_type=jnp.float32)
@@ -668,7 +834,7 @@
     along, from_left, from_right, section_six, section_one, confidence, y_band, basis, blurring
 ):
     shape, space = along.shape, confidence.shape
-    rims = pl.BlockSpec((shape[1], BAND_ROWS, shape[3]), lambda i: (0, i, 0))
+    rims = pl.BlockSpec((shape[0], BAND_ROWS, shape[3]), lambda i: (0, i, 0))
     held = pltpu.VMEM((space[2], BAND_ROWS, shape[3]), jnp.float32)
     sums = (3, 8, space[2])
     return pl.pallas_call(
@@ -771,7 +937,7 @@
     spot = row % block_y
     right = jnp.logical_and(within, spot == block_y - rim + place)
     left = jnp.logical_and(within, spot == place)
-    return right.astype(jnp.bfloat16), left.astype(jnp.bfloat16)
+    return jnp.concatenate([right, left], axis=1).astype(jnp.bfloat16)
 
 
 def kernel_shards(
@@ -797,31 +963,27 @@
     y_band = y_bands(kernels[1], offsets[1], block_y)
     y_back = y_bands(adjoint[1], -offsets[1], block_y)
     z_band = band_matrix(kernels[2], offsets[2], depth, depth, 0)
-    selects = rim_selects(block_y)
+    rim_select = rim_selects(block_y)
     basis_f = basis_z.astype(jnp.float32)
     blurring = jnp.dot(z_band, basis_f, precision=highest)
     entry = jnp.concatenate([z_band.astype(bf), basis_z.T], axis=0)
 
     along_z, plain = to_modes(iterate, entry)
-    rims = spread(along_z, x_band, selects, size_x, size_y, 1)
+    rims = spread(along_z, x_band, rim_select, size_x, size_y, 1)
     misfit, weighted = find_misfit(
         *rims, observed, confidence, y_band, blurring.T.astype(bf)
     )
-    section_one = spread(
-        weighted, x_back, selects, size_x, size_y, 2, (y_back, plain)
-    )[0]
-    section_six = transform(
-        section_one.reshape(depth, block_x, block_y), full_x.T, full_x, full_y, full_y.T,
+    section_one, section_six, *rims = transform(
+        weighted, plain, x_back, x_band, y_back, rim_select, full_x.T, full_x, full_y,
         part_x[:, None] * eigen_y[None, :], part_z, size_x, size_y,
-    ).reshape(section_one.shape)
-    rims = spread(section_six, x_band, selects, size_x, size_y, 3)
+    )
     coarse = blurring.T.astype(bf)
     fine = (blurring.T - coarse.astype(jnp.float32)).astype(bf)
     direction, blurred, sums = find_direction(
         *rims, section_six, section_one, confidence, y_band, basis_z.T,
         jnp.concatenate([coarse, fine], axis=0),
     )
-    totals = jnp.sum(total_sums(sums, size_x, size_y, 4), axis=1)
+    totals = jnp.sum(total_sums(sums, size_x, size_y, 2), axis=1)
     step_size = totals[0] / (totals[1] + tikhonov * totals[2])
     return (iterate + step_size * direction, misfit - step_size * blurred)
 

time: 794 us -> 731 us (0.921)
  Pallas kernels: 684 us -> 627 us
    pallas_call x3 -> x1, Pallas kernels: 174 us -> 38.6 us  [spread(): pl.pallas_call(functools.partial(spread_kernel, size_x, size_y, PARTS), o...]
    pallas_call x1, Pallas kernels: 377 us -> 452 us  [transform(): pl.pallas_call(functools.partial(transform_kernel, parts, size_x, size_y)...]
    unnamed x30 -> x29, local copies, waits for them, and re-layouts: 22.7 us -> 21 us
  transfers between devices with their start and end apart: 2 -> 2, of which waited for: 0 -> 0; matrix products, arithmetic and copies ran while one was open for 3% -> 3% of each run, Pallas kernels for 23% -> 14%
where the time goes in v3:
time: 731 us; the launch traced here: 730 us
  Pallas kernels  627 us (86%)
  other arithmetic  40.6 us (6%)
  local copies, waits for them, and re-layouts  30.7 us (4%)
  between operations  17.5 us (2%)
  blocking collectives  12.9 us (2%)
    pallas_call x1, Pallas kernels, transform(): pl.pallas_call(functools.partial(transform_kernel, parts, size_x, size_y)...  452 us
    pallas_call x1, Pallas kernels, total_sums(): pl.pallas_call(functools.partial(total_kernel, size_x, size_y), out_shape...  39.6 us
    pallas_call x1, Pallas kernels, spread(): pl.pallas_call(functools.partial(spread_kernel, size_x, size_y, PARTS), o...  38.6 us
    pallas_call x1, Pallas kernels, find_direction(): pl.pallas_call(direction_kernel, grid=(shape[2] // BAND_ROWS,), out_shape...  36.6 us
    pallas_call x1, Pallas kernels, find_misfit(): pl.pallas_call(misfit_kernel, grid=(shape[2] // BAND_ROWS,), out_shape=[j...  33.2 us
    pallas_call x1, Pallas kernels, to_modes(): pl.pallas_call(to_modes_kernel, grid=(block_x // BAND_ROWS,), out_shape=[...  27 us
    unnamed x29, local copies, waits for them, and re-layouts  21 us
    add x1, other arithmetic, kernel_shards(): return (iterate + step_size * direction, misfit - step_size * blurred)  17.8 us
  transfers between devices with their start and end apart: 2, of which 0 were waited for; matrix products, arithmetic and copies ran while one was open for 3% of the time, Pallas kernels for 14%

profile of v3, /device:TPU:0, one launch (start us, length us, event | category | flops | bytes accessed | tf_op | source)
XLA Modules:
  0.0 730.3 jit_solution(5082985788379188912)
XLA Ops:
  8.7 1.4 fusion.44
  12.0 0.9 select_reduce_fusion.5
  13.2 0.9 copy.22
  15.1 1.1 select_reduce_fusion
  16.2 0.8 copy.24.x_back
  17.0 1.1 select_reduce_fusion.1
  18.1 0.8 copy.23.x_band
  19.0 1.3 dynamic_slice.7.eigen_z
  20.2 12.9 %all-gather = f32[4,1,256]{2,1,0:T(1,128)S(1)} all-gather(f32[1,1,256]{2,1,0:T(1,128)} %bitcast.48), channel_id=1, replica_groups=mesh['gx'=4,'gy'=8] {'gx'}, dimensions={0}, use_global_device_ids=true | all-gather | bytes 5120 | tf_op jit(solution)/shard_map/all_gather | solution.py:954
  33.2 27.0 %shard_map.131 = (bf16[32,4,256,128]{3,2,1,0:T(8,128)(2,1)S(1)}, bf16[32,4,256,128]{3,2,1,0:T(8,128)(2,1)}) custom-call(bf16[256,128]{1,0:T(8,128)(2,1)S(1)} %pad_maximum_fusion.10.matrix, f32[256,128,128]{2,1,0:T(8,128)} %source.1), custom_call_target="tpu_custom_call" | custom-call | tf_op jit(solution)/shard_map/pallas_call | solution.py:624
  60.2 3.4 copy-done.1
  64.3 0.8 add_convert_fusion.rim_select
  65.1 38.6 %shard_map.132 = (bf16[32,4,256,128]{3,2,1,0:T(8,128)(2,1)}, bf16[32,256,128]{2,1,0:T(8,128)(2,1)}, bf16[32,256,128]{2,1,0:T(8,128)(2,1)}) custom-call(bf16[32,4,256,128]{3,2,1,0:T(8,128)(2,1)} %copy-done.1, bf16[256,320]{1,0:T(8,128)(2,1)} %copy.23.x_band, bf16[512,256]{1,0:T(8,128)(2,1)} %add_convert_fusion.rim_select), custom_call_target="tpu_custom_call" | custom-call | tf_op jit(solution)/shard_map/pallas_call | solution.py:740
  105.6 1.6 copy-done.3
  107.2 1.6 copy-done.4
  108.8 33.2 %shard_map.133 = (f32[256,128,128]{2,1,0:T(8,128)}, bf16[32,4,256,128]{3,2,1,0:T(8,128)(2,1)S(1)}) custom-call(bf16[32,4,256,128]{3,2,1,0:T(8,128)(2,1)} %get-tuple-element.18.along, bf16[32,256,128]{2,1,0:T(8,128)(2,1)S(1)} %copy-done.3, bf16[32,256,128]{2,1,0:T(8,128)(2,1)S(1)} %copy-done.4, bf16[256,128,128]{2,1,0:T(8,128)(2,1)} %observed.1, ...), custom_call_target="tpu_custom_call" | custom-call | tf_op jit(solution)/shard_map/pallas_call | solution.py:783
  141.9 3.3 copy-done
  145.3 0.8 pad_maximum_fusion.1.y_band
  146.1 0.9 broadcast_multiply_fusion.eigen_xy
  147.0 3.9 copy.25.x_fwd
  150.9 451.8 %shard_map.134 = (bf16[32,4,256,128]{3,2,1,0:T(8,128)(2,1)}, bf16[32,4,256,128]{3,2,1,0:T(8,128)(2,1)}, bf16[32,4,256,128]{3,2,1,0:T(8,128)(2,1)}, bf16[32,256,128]{2,1,0:T(8,128)(2,1)}, bf16[32,256,128]{2,1,0:T(8,128)(2,1)}) custom-call(bf16[32,4,256,128]{3,2,1,0:T(8,128)(2,1)} %copy-done, bf16[32,4,256,128]{3,2,1,0:T(8,128)(2,1)} %get-tuple-element.22.plain, ...), custom_call_target="tpu_custom_call" | custom-call | tf_op jit(solution)/shard_map/pallas_call | solution.py:539
  602.7 3.4 copy-done.2
  606.1 1.6 copy-done.5
  607.7 1.6 copy-done.6
  609.3 36.6 %shard_map.135 = (f32[256,128,128]{2,1,0:T(8,128)}, f32[256,128,128]{2,1,0:T(8,128)}, f32[3,8,128]{2,1,0:T(8,128)S(1)}) custom-call(bf16[32,4,256,128]{3,2,1,0:T(8,128)(2,1)S(1)} %copy-done.2, bf16[32,256,128]{2,1,0:T(8,128)(2,1)S(1)} %copy-done.5, bf16[32,256,128]{2,1,0:T(8,128)(2,1)S(1)} %copy-done.6, ...), custom_call_target="tpu_custom_call" | custom-call | tf_op jit(solution)/shard_map/pallas_call | solution.py:840
  646.5 39.6 %shard_map.136 = f32[8,128]{1,0:T(8,128)} custom-call(f32[8,8,128]{2,1,0:T(8,128)} %pad.86.values), custom_call_target="tpu_custom_call" | custom-call | tf_op jit(solution)/shard_map/pallas_call | solution.py:899
  686.1 0.8 reduce_sum.79
  689.5 17.8 %multiply_add_fusion = f32[256,128,128]{2,1,0:T(8,128)} fusion(f32[256,128,128]{2,1,0:T(8,128)} %source.1, f32[256,128,128]{2,1,0:T(8,128)} %get-tuple-element.29, f32[]{:T(128)} %bitcast.23), kind=kLoop, calls=%fused_computation.1 | loop fusion | flops 8388608 | bytes 50331652 | tf_op jit(solution)/shard_map/add | solution.py:988
  707.3 1.3 slice-done.1
  708.6 1.2 slice-done.2
  709.8 1.2 slice-done.3
  711.0 12.4 %multiply_subtract_fusion = f32[256,128,128]{2,1,0:T(8,128)} fusion(f32[256,128,128]{2,1,0:T(8,128)S(1)} %bitcast.41, f32[256,128,128]{2,1,0:T(8,128)} %get-tuple-element.31, f32[]{:T(128)} %bitcast.23), kind=kLoop, calls=%fused_computation | loop fusion | flops 8388608 | bytes 50331652 | tf_op jit(solution)/shard_map/sub | solution.py:988
  (57 shorter events, 7.3 us)
Async XLA Ops:
  7.2 139.8 %all-gather.4.cloned.1.call-start = ((), (), s32[]{:S(2)}) async-start(), calls=%async_computation | async-start | bytes 2621440 | tf_op jit(solution)/shard_map/all_gather | solution.py:952
  7.9 143.0 %all-gather.6.cloned.1.call-start = ((), (), s32[]{:S(2)}) async-start(), calls=%async_computation.1 | async-start | bytes 2359296 | tf_op jit(solution)/shard_map/all_gather | solution.py:953
  60.2 3.4 copy-start.1
  63.6 41.5 %copy-start.9 = (pred[128]{0:T(512)(128)(4,1)S(1)}, pred[128]{0:T(512)(128)(4,1)}, u32[]{:S(2)}) copy-start(pred[128]{0:T(512)(128)(4,1)} %constant.90.clone.1) | copy-start | bytes 388
  63.6 41.7 %copy-start.7 = (bf16[128,128]{1,0:T(8,128)(2,1)S(1)}, bf16[128,128]{1,0:T(8,128)(2,1)}, u32[]{:S(2)}) copy-start(bf16[128,128]{1,0:T(8,128)(2,1)} %param.20) | copy-start | bytes 98308
  105.6 1.6 copy-start.3
  107.2 1.6 copy-start.4
  108.8 37.3 %copy-start.8 = (f32[1024]{0:T(1024)S(1)}, f32[1024]{0:T(1024)}, u32[]{:S(2)}) copy-start(f32[1024]{0:T(1024)} %param.22) | copy-start | bytes 12292
  141.9 3.3 copy-start
  602.7 3.4 copy-start.2
  606.1 1.6 copy-start.5
  607.7 1.6 copy-start.6
  689.5 17.9 %slice-start = ((s8[16777216]{0:T(1024)(128)(4,1)}), s8[4194304]{0:T(1024)(128)(4,1)S(1)}, s32[]{:S(2)}) async-start(s8[16777216]{0:T(1024)(128)(4,1)} %bitcast.40), calls=%async_computation.2 | async-start | bytes 8388608
  689.5 19.1 %slice-start.1 = ((s8[16777216]{0:T(1024)(128)(4,1)}), s8[4194304]{0:T(1024)(128)(4,1)S(1)}, s32[]{:S(2)}) async-start(s8[16777216]{0:T(1024)(128)(4,1)} %bitcast.40), calls=%async_computation.3 | async-start | bytes 8388608
  689.5 20.3 %slice-start.2 = ((s8[16777216]{0:T(1024)(128)(4,1)}), s8[4194304]{0:T(1024)(128)(4,1)S(1)}, s32[]{:S(2)}) async-start(s8[16777216]{0:T(1024)(128)(4,1)} %bitcast.40), calls=%async_computation.4 | async-start | bytes 8388608
  689.5 21.5 %slice-start.3 = ((s8[16777216]{0:T(1024)(128)(4,1)}), s8[4194304]{0:T(1024)(128)(4,1)S(1)}, s32[]{:S(2)}) async-start(s8[16777216]{0:T(1024)(128)(4,1)} %bitcast.40), calls=%async_computation.5 | async-start | bytes 8388608
Sparse Core Ops, SparseCore 0:
  9.6 48.6 all-gather.3
  60.1 30.3 all-gather.5

commit v4 on v3

--- a/solution.py
+++ b/solution.py
@@ -181,16 +181,16 @@
 
 
 MESH_ID = pl.DeviceIdType.MESH
-PARTS = 4
+PARTS = 8
 
 
 def transform_kernel(
     parts, size_x, size_y,
-    weighted, plain, x_back, x_band, y_band, rim_select, x_fwd, x_inv, y_fwd, eigen_xy, eigen_z,
+    weighted, plain, x_back, x_band, y_band, rim_select, x_inv, y_fwd, rows_x, rows_y, eigen_z,
     section_one, section_six, spread_out, left_out, right_out,
     lines_x, lines_y, lines_back, send_a, send_b, send_c, modes, along, low, high, rims,
-    from_left, from_right,
-    fs, fr, gs, gr, hs, hr, bs, br, fl, gl, hl, bl, xs, xr, ys, yr, us, ur, vs, vr, loads,
+    from_left, from_right, x_fwd, eigen_xy, all_x,
+    fs, fr, gs, gr, hs, hr, bs, br, fl, gl, hl, bl, xs, xr, ys, yr, us, ur, vs, vr, loads, es, er,
 ):
     me_x = lax.axis_index("gx")
     me_y = lax.axis_index("gy")
@@ -417,6 +417,17 @@
         def _():
             ref[...] = jnp.zeros_like(ref)
 
+    eigen_copies = [
+        remote(rows_x, all_x.at[me_x], es.at[step], er.at[step],
+               (lax.rem(me_x + step, size_x), me_y))
+        for step in range(1, size_x)
+    ]
+    for copy in eigen_copies:
+        copy.start()
+    all_x[me_x] = rows_x[...]
+    for b in range(0, full, block_y):
+        x_fwd[pl.ds(b, block_y), :] = x_inv[:, pl.ds(b, block_y)].astype(jnp.float32).T.astype(bf)
+
     ahead = 2
     for c in range(parts + 1):
         if c < parts:
@@ -443,6 +454,12 @@
         if c >= parts - slots:
             halo_sent(y_first, c)
 
+    for copy in eigen_copies:
+        copy.wait()
+    row = all_x[me_y // halves, lax.rem(me_y, halves)][:1]
+    column = jnp.broadcast_to(row, (share, share)).T
+    for b in range(0, full_y, share):
+        eigen_xy[:, pl.ds(b, share)] = column * rows_y[:1, pl.ds(b, share)]
     for step in range(parts + 2):
         c = step
         if c < parts:
@@ -518,11 +535,11 @@
 
 
 def transform(
-    weighted, plain, x_back, x_band, y_back, rim_select, x_fwd, x_inv, y_fwd, eigen_xy, eigen_z,
+    weighted, plain, x_back, x_band, y_back, rim_select, x_inv, y_fwd, rows_x, rows_y, eigen_z,
     size_x, size_y,
 ):
     depth, quads, block_x, block_y = weighted.shape
-    full_x, full_y = x_fwd.shape[0], y_fwd.shape[0]
+    full_x, full_y = x_inv.shape[0], y_fwd.shape[0]
     share = full_x // size_y
     parts = PARTS
     part = depth // parts
@@ -553,30 +570,34 @@
             edge, edge,
             pltpu.VMEM((slots, 2, part, block_x, block_y), bf),
             pltpu.VMEM(side.shape, bf), pltpu.VMEM(side.shape, bf),
+            pltpu.VMEM((full_x, full_x), bf),
+            pltpu.VMEM((share, full_y), jnp.float32),
+            pltpu.VMEM((size_x,) + rows_x.shape, jnp.float32),
             sem(size_x), sem(size_x), sem(size_y), sem(size_y),
             sem(size_y), sem(size_y), sem(size_x), sem(size_x),
             one, one, one, one,
             sem(2), sem(2), sem(2), sem(2), sem(2), sem(2), sem(2), sem(2),
             pltpu.SemaphoreType.DMA((6, parts)),
+            pltpu.SemaphoreType.DMA((size_x,)), pltpu.SemaphoreType.DMA((size_x,)),
         ],
         compiler_params=pltpu.CompilerParams(
             collective_id=0, has_side_effects=True, vmem_limit_bytes=62 * 2**20
         ),
     )(
-        weighted, plain, x_back, x_band, y_back, rim_select, x_fwd, x_inv, y_fwd, eigen_xy, eigen_z
+        weighted, plain, x_back, x_band, y_back, rim_select, x_inv, y_fwd, rows_x, rows_y, eigen_z
     )
 
 
 def blur_x_lines(lines, low, high, band, along, to_right, to_left, rim_select):
     half = lines[0].shape[1]
-    for q in range(0, QUADS, 2):
+    for q in range(0, len(lines), 2):
         both = jnp.concatenate(
             [jnp.concatenate([low[p], lines[p], high[p]], axis=0) for p in (q, q + 1)], axis=1
         )
         found = jnp.dot(band[...], both, preferred_element_type=jnp.float32).astype(jnp.bfloat16)
         along[q] = found[:, :half]
         along[q + 1] = found[:, half:]
-    wide = jnp.concatenate([along[q] for q in range(QUADS)], axis=1)
+    wide = jnp.concatenate([along[q] for q in range(len(lines))], axis=1)
     found = jnp.dot(
         wide, rim_select[...], preferred_element_type=jnp.float32
     ).astype(jnp.bfloat16)
@@ -587,7 +608,7 @@
 BAND_ROWS = 16
 QUADS = 4
 RIM_ROWS = 32
-RIM_LANES = 32
+SIXES = 6
 
 
 def to_modes_kernel(matrix, source, first, second, held):
@@ -599,9 +620,13 @@
         )
         held[:, x, :] = found[:, : source.shape[1]]
         held[:, x + 1, :] = found[:, source.shape[1] :]
-    groups = first.shape[0]
+    full = depth // SIXES
+    first[:full] = held[: full * SIXES].reshape((full,) + first.shape[1:]).astype(first.dtype)
+    left = depth - full * SIXES
+    first[full, :left] = held[full * SIXES : depth].astype(first.dtype)
+    first[full, left:] = jnp.zeros((SIXES - left,) + first.shape[2:], first.dtype)
+    groups = second.shape[0]
     for q in range(QUADS):
-        first[:, q] = held[pl.ds(q * groups, groups)].astype(first.dtype)
         second[:, q] = held[pl.ds(depth + q * groups, groups)].astype(second.dtype)
 
 
@@ -619,16 +644,17 @@
 
 def to_modes(source, matrix):
     block_x, block_y, depth = source.shape
-    shape = (depth // QUADS, QUADS, block_x, block_y)
-    out = jax.ShapeDtypeStruct(shape, jnp.bfloat16)
+    shapes = [
+        (depth // SIXES + 1, SIXES, block_x, block_y), (depth // QUADS, QUADS, block_x, block_y)
+    ]
     return pl.pallas_call(
         to_modes_kernel,
         grid=(block_x // BAND_ROWS,),
-        out_shape=[out, out],
+        out_shape=[jax.ShapeDtypeStruct(shape, jnp.bfloat16) for shape in shapes],
         in_specs=[whole_block(matrix.shape), space_block(BAND_ROWS, source.shape)],
-        out_specs=[modes_block(BAND_ROWS, shape)] * 2,
+        out_specs=[modes_block(BAND_ROWS, shape) for shape in shapes],
         scratch_shapes=[pltpu.VMEM((2 * depth, BAND_ROWS, block_y), jnp.float32)],
-        compiler_params=pltpu.CompilerParams(vmem_limit_bytes=40 * 2**20),
+        compiler_params=pltpu.CompilerParams(vmem_limit_bytes=60 * 2**20),
     )(matrix, source)
 
 
@@ -691,7 +717,7 @@
         def step(i, carry):
             g = c * part + i
             blur_x_lines(
-                [source[g, q] for q in range(QUADS)], low.at[g], high.at[g], x_band,
+                [source[g, q] for q in range(source.shape[1])], low.at[g], high.at[g], x_band,
                 along.at[g], right.at[g], left.at[g], rim_select,
             )
             return carry
@@ -736,9 +762,9 @@
     vmem = pl.BlockSpec(memory_space=pltpu.VMEM)
     edge = pltpu.VMEM((groups, quads, RIM_ROWS, block_y), bf)
     packed = pltpu.VMEM(rims.shape, bf)
-    sem = pltpu.SemaphoreType.DMA((PARTS, 2))
+    sem = pltpu.SemaphoreType.DMA((groups // 2, 2))
     return pl.pallas_call(
-        functools.partial(spread_kernel, size_x, size_y, PARTS),
+        functools.partial(spread_kernel, size_x, size_y, groups // 2),
         out_shape=[whole, rims, rims],
         in_specs=[vmem] * 3,
         out_specs=[vmem] * 3,
@@ -749,23 +775,28 @@
     )(source, x_band, rim_select)
 
 
-def blur_y_rows(along, from_left, from_right, y_band, held):
+def blur_y_rows(along, from_left, from_right, y_band, put):
     groups, quads, rows, block_y = along.shape
     count = groups * rows
     sides = [from_left[...].reshape(count, block_y), from_right[...].reshape(count, block_y)]
     for q in range(quads):
         wide = jnp.concatenate([along[:, q].reshape(count, block_y)] + sides, axis=1)
         found = jnp.dot(wide, y_band[q], preferred_element_type=jnp.float32)
-        held[pl.ds(q * groups, groups)] = found.reshape(groups, rows, block_y)
+        put(q, found.reshape(groups, rows, block_y))
 
 
 def misfit_kernel(
     along, from_left, from_right, observed, confidence, y_band, matrix,
     misfit, weighted, held, turned_back,
 ):
-    blur_y_rows(along, from_left, from_right, y_band, held)
+    def put(s, found):
+        for r in range(found.shape[0]):
+            held[r * SIXES + s] = found[r]
+
+    blur_y_rows(along, from_left, from_right, y_band, put)
+    depth = observed.shape[2]
     for x in range(observed.shape[0]):
-        found = observed[x].astype(jnp.float32) - held[:, x, :].T
+        found = observed[x].astype(jnp.float32) - held[:depth, x, :].T
         misfit[x] = found
         lines = (confidence[x].astype(jnp.float32) * found).astype(jnp.bfloat16)
         turned_back[:, x, :] = lax.dot_general(
@@ -778,23 +809,25 @@
 
 def find_misfit(along, from_left, from_right, observed, confidence, y_band, matrix):
     shape, space = along.shape, observed.shape
+    modes = (space[2] // QUADS, QUADS, shape[2], shape[3])
     rims = pl.BlockSpec((shape[0], BAND_ROWS, shape[3]), lambda i: (0, i, 0))
-    held = pltpu.VMEM((space[2], BAND_ROWS, shape[3]), jnp.float32)
+    held = pltpu.VMEM((shape[0] * SIXES, BAND_ROWS, shape[3]), jnp.float32)
+    turned = pltpu.VMEM((space[2], BAND_ROWS, shape[3]), jnp.float32)
     return pl.pallas_call(
         misfit_kernel,
         grid=(shape[2] // BAND_ROWS,),
         out_shape=[
             jax.ShapeDtypeStruct(space, jnp.float32),
-            jax.ShapeDtypeStruct(shape, jnp.bfloat16),
+            jax.ShapeDtypeStruct(modes, jnp.bfloat16),
         ],
         in_specs=[
             modes_block(BAND_ROWS, shape), rims, rims,
             space_block(BAND_ROWS, space), space_block(BAND_ROWS, space),
             whole_block(y_band.shape), whole_block(matrix.shape),
         ],
-        out_specs=[space_block(BAND_ROWS, space), modes_block(BAND_ROWS, shape)],
-        scratch_shapes=[held, held],
-        compiler_params=pltpu.CompilerParams(vmem_limit_bytes=40 * 2**20),
+        out_specs=[space_block(BAND_ROWS, space), modes_block(BAND_ROWS, modes)],
+        scratch_shapes=[held, turned],
+        compiler_params=pltpu.CompilerParams(vmem_limit_bytes=60 * 2**20),
     )(along, from_left, from_right, observed, confidence, y_band, matrix)
 
 
@@ -810,7 +843,10 @@
     def _():
         sums[...] = jnp.zeros_like(sums)
 
-    blur_y_rows(along, from_left, from_right, y_band, held)
+    def put(q, found):
+        held[pl.ds(q * found.shape[0], found.shape[0])] = found
+
+    blur_y_rows(along, from_left, from_right, y_band, put)
     six = section_six[...].astype(jnp.float32)
     sums[0] += folded((six * section_one[...].astype(jnp.float32)).reshape(-1, six.shape[-1]))
     groups = six.shape[0]
@@ -855,7 +891,7 @@
             space_block(BAND_ROWS, space), space_block(BAND_ROWS, space), whole_block(sums),
         ],
         scratch_shapes=[held, held],
-        compiler_params=pltpu.CompilerParams(vmem_limit_bytes=40 * 2**20),
+        compiler_params=pltpu.CompilerParams(vmem_limit_bytes=60 * 2**20),
     )(
         along, from_left, from_right, section_six, section_one, confidence, y_band, basis, blurring
     )
@@ -911,14 +947,13 @@
     )(padded)
 
 
-def y_bands(kernel, offset, block_y):
+def y_bands(kernel, offset, block_y, count):
     rim = HALF + SHIFT
     band = band_matrix(kernel, offset, block_y, block_y + 2 * rim, rim).T
-    lanes = QUADS * RIM_LANES
     stacks = []
-    for q in range(QUADS):
-        before = q * RIM_LANES
-        pads = ((before, lanes - before - rim), (0, 0))
+    for q in range(count):
+        before = q * (block_y // count)
+        pads = ((before, block_y - before - rim), (0, 0))
         stacks.append(
             jnp.concatenate(
                 [band[rim:-rim], jnp.pad(band[:rim], pads), jnp.pad(band[-rim:], pads)], axis=0
@@ -927,12 +962,13 @@
     return jnp.stack(stacks).astype(jnp.bfloat16)
 
 
-def rim_selects(block_y):
+def rim_selects(block_y, count):
     rim = HALF + SHIFT
-    row = lax.broadcasted_iota(jnp.int32, (QUADS * block_y, QUADS * RIM_LANES), 0)
-    lane = lax.broadcasted_iota(jnp.int32, (QUADS * block_y, QUADS * RIM_LANES), 1)
-    same = row // block_y == lane // RIM_LANES
-    place = lane % RIM_LANES
+    row = lax.broadcasted_iota(jnp.int32, (count * block_y, block_y), 0)
+    lane = lax.broadcasted_iota(jnp.int32, (count * block_y, block_y), 1)
+    width = block_y // count
+    same = row // block_y == lane // width
+    place = lane % width
     within = jnp.logical_and(same, place < rim)
     spot = row % block_y
     right = jnp.logical_and(within, spot == block_y - rim + place)
@@ -951,31 +987,32 @@
     adjoint = kernels[:, ::-1]
     full_x = lax.all_gather(basis_x, "gx", axis=0, tiled=True)
     full_y = lax.all_gather(basis_y, "gy", axis=0, tiled=True)
-    all_x = lax.all_gather(eigen_x, "gx", axis=0, tiled=True)
-    share_x = all_x.shape[0] // size_y
-    part_x = lax.dynamic_slice_in_dim(all_x, lax.axis_index("gy") * share_x, share_x)
+    share_x = block_x * size_x // size_y
+    rows_x = jnp.broadcast_to(eigen_x.reshape(-1, 1, share_x), (block_x // share_x, 8, share_x))
+    rows_y = jnp.broadcast_to(eigen_y[None, :], (8, eigen_y.shape[0]))
     share_z = depth // size_x
     part_z = lax.dynamic_slice_in_dim(eigen_z, lax.axis_index("gx") * share_z, share_z)
 
     wide_x = block_x + 2 * RIM_ROWS
     x_band = band_matrix(kernels[0], offsets[0], block_x, wide_x, RIM_ROWS).astype(bf)
     x_back = band_matrix(adjoint[0], -offsets[0], block_x, wide_x, RIM_ROWS).astype(bf)
-    y_band = y_bands(kernels[1], offsets[1], block_y)
-    y_back = y_bands(adjoint[1], -offsets[1], block_y)
+    y_first = y_bands(kernels[1], offsets[1], block_y, SIXES)
+    y_band = y_bands(kernels[1], offsets[1], block_y, QUADS)
+    y_back = y_bands(adjoint[1], -offsets[1], block_y, QUADS)
     z_band = band_matrix(kernels[2], offsets[2], depth, depth, 0)
-    rim_select = rim_selects(block_y)
+    rim_select = rim_selects(block_y, QUADS)
     basis_f = basis_z.astype(jnp.float32)
     blurring = jnp.dot(z_band, basis_f, precision=highest)
     entry = jnp.concatenate([z_band.astype(bf), basis_z.T], axis=0)
 
     along_z, plain = to_modes(iterate, entry)
-    rims = spread(along_z, x_band, rim_select, size_x, size_y, 1)
+    rims = spread(along_z, x_band, rim_selects(block_y, SIXES), size_x, size_y, 1)
     misfit, weighted = find_misfit(
-        *rims, observed, confidence, y_band, blurring.T.astype(bf)
+        *rims, observed, confidence, y_first, blurring.T.astype(bf)
     )
     section_one, section_six, *rims = transform(
-        weighted, plain, x_back, x_band, y_back, rim_select, full_x.T, full_x, full_y,
-        part_x[:, None] * eigen_y[None, :], part_z, size_x, size_y,
+        weighted, plain, x_back, x_band, y_back, rim_select, full_x, full_y,
+        rows_x, rows_y, part_z, size_x, size_y,
     )
     coarse = blurring.T.astype(bf)
     fine = (blurring.T - coarse.astype(jnp.float32)).astype(bf)

time: 731 us -> 697 us (0.953)
  local copies, waits for them, and re-layouts: 30.7 us -> 12.3 us
  blocking collectives: 12.9 us -> 0 us
  Pallas kernels: 627 us -> 615 us
    unnamed x29 -> x23, local copies, waits for them, and re-layouts: 21 us -> 4.57 us
    all_gather x1 -> x0, blocking collectives: 12.9 us -> none  [kernel_shards(): all_x = lax.all_gather(eigen_x, 'gx', axis=0, tiled=True)]
    pallas_call x1, Pallas kernels: 39.6 us -> 31.3 us  [total_sums(): pl.pallas_call(functools.partial(total_kernel, size_x, size_y), out_shape...]
  transfers between devices with their start and end apart: 2 -> 2, of which waited for: 0 -> 0; matrix products, arithmetic and copies ran while one was open for 3% -> 3% of each run, Pallas kernels for 14% -> 15%
where the time goes in v4:
time: 697 us; the launch traced here: 691 us
  Pallas kernels  615 us (88%)
  other arithmetic  43.7 us (6%)
  between operations  18 us (3%)
  local copies, waits for them, and re-layouts  12.3 us (2%)
    pallas_call x1, Pallas kernels, transform(): pl.pallas_call(functools.partial(transform_kernel, parts, size_x, size_y)...  445 us
    pallas_call x1, Pallas kernels, spread(): pl.pallas_call(functools.partial(spread_kernel, size_x, size_y, groups //...  39.7 us
    pallas_call x1, Pallas kernels, find_direction(): pl.pallas_call(direction_kernel, grid=(shape[2] // BAND_ROWS,), out_shape...  37.6 us
    pallas_call x1, Pallas kernels, find_misfit(): pl.pallas_call(misfit_kernel, grid=(shape[2] // BAND_ROWS,), out_shape=[j...  34.4 us
    pallas_call x1, Pallas kernels, total_sums(): pl.pallas_call(functools.partial(total_kernel, size_x, size_y), out_shape...  31.3 us
    pallas_call x1, Pallas kernels, to_modes(): pl.pallas_call(to_modes_kernel, grid=(block_x // BAND_ROWS,), out_shape=[...  27.1 us
    add x1, other arithmetic, kernel_shards(): return (iterate + step_size * direction, misfit - step_size * blurred)  17.8 us
  transfers between devices with their start and end apart: 2, of which 0 were waited for; matrix products, arithmetic and copies ran while one was open for 3% of the time, Pallas kernels for 15%

profile of v4, /device:TPU:0, one launch (start us, length us, event | category | flops | bytes accessed | tf_op | source)
XLA Modules:
  0.0 691.0 jit_solution(1804477977212591028)
XLA Ops:
  7.2 0.7 all-gather.3.cloned.1.call-update
  7.9 0.7 all-gather.5.cloned.1.call-update
  8.7 1.4 fusion.73
  12.1 0.7 fusion.4
  12.9 0.9 select_reduce_fusion.5
  14.0 0.9 copy.18
  14.9 0.7 add_subtract_fusion
  15.9 1.1 select_reduce_fusion
  17.1 0.8 copy.20.x_back
  17.9 1.1 select_reduce_fusion.1
  19.0 0.8 copy.19.x_band
  19.8 1.3 dynamic_slice.3.eigen_z
  21.7 0.9 fusion
  22.7 0.9 add_convert_fusion.rim_select
  23.5 27.1 %shard_map.131 = (bf16[22,6,256,128]{3,2,1,0:T(8,128)(2,1)}, bf16[32,4,256,128]{3,2,1,0:T(8,128)(2,1)}) custom-call(bf16[256,128]{1,0:T(8,128)(2,1)} %pad_maximum_fusion.14.matrix, f32[256,128,128]{2,1,0:T(8,128)} %source.1), custom_call_target="tpu_custom_call" | custom-call | tf_op jit(solution)/shard_map/pallas_call | solution.py:650
  50.6 39.7 %shard_map.132 = (bf16[22,6,256,128]{3,2,1,0:T(8,128)(2,1)}, bf16[22,256,128]{2,1,0:T(8,128)(2,1)}, bf16[22,256,128]{2,1,0:T(8,128)(2,1)}) custom-call(bf16[22,6,256,128]{3,2,1,0:T(8,128)(2,1)} %get-tuple-element.17.source, bf16[256,320]{1,0:T(8,128)(2,1)} %copy.19.x_band, bf16[768,256]{1,0:T(8,128)(2,1)} %add_convert_fusion.rim_select), custom_call_target="tpu_custom_call" | custom-call | tf_op jit(solution)/shard_map/pallas_call | solution.py:766
  91.4 0.8 subtract_convert_fusion
  92.2 34.4 %shard_map.133 = (f32[256,128,128]{2,1,0:T(8,128)}, bf16[32,4,256,128]{3,2,1,0:T(8,128)(2,1)}) custom-call(bf16[22,6,256,128]{3,2,1,0:T(8,128)(2,1)} %get-tuple-element.18.along, bf16[22,256,128]{2,1,0:T(8,128)(2,1)} %get-tuple-element.19.from_left, bf16[22,256,128]{2,1,0:T(8,128)(2,1)} %get-tuple-element.20.from_right, bf16[256,128,128]{2,1,0:T(8,128)(2,1)} %observed.1, ...), custom_call_target="tpu_custom_call" | custom-call | tf_op jit(solution)/shard_map/pallas_call | solution.py:816
  128.0 0.8 add_convert_fusion.1.rim_select
  128.8 0.8 pad_maximum_fusion.y_band
  129.6 0.8 pad_maximum_fusion.1.y_band
  131.6 444.6 %shard_map.134 = (bf16[32,4,256,128]{3,2,1,0:T(8,128)(2,1)}, bf16[32,4,256,128]{3,2,1,0:T(8,128)(2,1)}, bf16[32,4,256,128]{3,2,1,0:T(8,128)(2,1)}, bf16[32,256,128]{2,1,0:T(8,128)(2,1)}, bf16[32,256,128]{2,1,0:T(8,128)(2,1)}) custom-call(bf16[32,4,256,128]{3,2,1,0:T(8,128)(2,1)} %get-tuple-element.21.weighted, ...), custom_call_target="tpu_custom_call" | custom-call | tf_op jit(solution)/shard_map/pallas_call | solution.py:556
  576.2 37.6 %shard_map.135 = (f32[256,128,128]{2,1,0:T(8,128)}, f32[256,128,128]{2,1,0:T(8,128)}, f32[3,8,128]{2,1,0:T(8,128)}) custom-call(bf16[32,4,256,128]{3,2,1,0:T(8,128)(2,1)} %get-tuple-element.23.along, bf16[32,256,128]{2,1,0:T(8,128)(2,1)} %get-tuple-element.24.from_left, bf16[32,256,128]{2,1,0:T(8,128)(2,1)} %get-tuple-element.25.from_right, ...), custom_call_target="tpu_custom_call" | custom-call | tf_op jit(solution)/shard_map/pallas_call | solution.py:876
  613.8 1.3 pad.142.values
  615.1 31.3 %shard_map.136 = f32[8,128]{1,0:T(8,128)} custom-call(f32[8,8,128]{2,1,0:T(8,128)} %pad.142.values), custom_call_target="tpu_custom_call" | custom-call | tf_op jit(solution)/shard_map/pallas_call | solution.py:935
  646.4 0.8 reduce_sum.83
  647.2 0.7 fusion.72
  649.8 17.8 %multiply_add_fusion = f32[256,128,128]{2,1,0:T(8,128)} fusion(f32[256,128,128]{2,1,0:T(8,128)} %source.1, f32[256,128,128]{2,1,0:T(8,128)} %get-tuple-element.29, f32[]{:T(128)} %bitcast.26), kind=kLoop, calls=%fused_computation.1 | loop fusion | flops 8388608 | bytes 50331652 | tf_op jit(solution)/shard_map/add | solution.py:1025
  667.7 1.3 slice-done.1
  668.9 1.2 slice-done.2
  670.1 1.2 slice-done.3
  671.3 12.4 %multiply_subtract_fusion = f32[256,128,128]{2,1,0:T(8,128)} fusion(f32[256,128,128]{2,1,0:T(8,128)S(1)} %bitcast.58, f32[256,128,128]{2,1,0:T(8,128)} %get-tuple-element.31, f32[]{:T(128)} %bitcast.26), kind=kLoop, calls=%fused_computation | loop fusion | flops 8388608 | bytes 50331652 | tf_op jit(solution)/shard_map/sub | solution.py:1025
  (63 shorter events, 5.6 us)
Async XLA Ops:
  7.2 123.2 %all-gather.3.cloned.1.call-start = ((), (), s32[]{:S(2)}) async-start(), calls=%async_computation | async-start | bytes 2621440 | tf_op jit(solution)/shard_map/all_gather | solution.py:988
  7.9 122.5 %all-gather.5.cloned.1.call-start = ((), (), s32[]{:S(2)}) async-start(), calls=%async_computation.1 | async-start | bytes 2359296 | tf_op jit(solution)/shard_map/all_gather | solution.py:989
  14.9 35.7 %copy-start.2 = (bf16[128,128]{0,1:T(8,128)(2,1)}, bf16[128,128]{0,1:T(8,128)(2,1)S(1)}, u32[]{:S(2)}) copy-start(bf16[128,128]{0,1:T(8,128)(2,1)S(1)} %copy.18) | copy-start | bytes 98308
  50.6 40.5 %copy-start.6 = (pred[128]{0:T(512)(128)(4,1)S(1)}, pred[128]{0:T(512)(128)(4,1)}, u32[]{:S(2)}) copy-start(pred[128]{0:T(512)(128)(4,1)} %constant.120.clone.1) | copy-start | bytes 388
  50.6 40.7 %copy-start.3 = (bf16[128,128]{1,0:T(8,128)(2,1)S(1)}, bf16[128,128]{1,0:T(8,128)(2,1)}, u32[]{:S(2)}) copy-start(bf16[128,128]{1,0:T(8,128)(2,1)} %param.20) | copy-start | bytes 98308
  91.4 0.9 copy-start
  92.2 34.5 %copy-start.1 = (bf16[128,128]{1,0:T(8,128)(2,1)S(1)}, bf16[128,128]{1,0:T(8,128)(2,1)}, u32[]{:S(2)}) copy-start(bf16[128,128]{1,0:T(8,128)(2,1)} %get-tuple-element.35.matrix) | copy-start | bytes 98308
  92.2 38.2 %copy-start.5 = (f32[256]{0:T(256)S(1)}, f32[256]{0:T(256)}, u32[]{:S(2)}) copy-start(f32[256]{0:T(256)} %param.21) | copy-start | bytes 3076
  92.2 38.8 %copy-start.4 = (f32[1024]{0:T(1024)S(1)}, f32[1024]{0:T(1024)}, u32[]{:S(2)}) copy-start(f32[1024]{0:T(1024)} %param.22) | copy-start | bytes 12292
  649.8 17.9 %slice-start = ((s8[16777216]{0:T(1024)(128)(4,1)}), s8[4194304]{0:T(1024)(128)(4,1)S(1)}, s32[]{:S(2)}) async-start(s8[16777216]{0:T(1024)(128)(4,1)} %bitcast.57), calls=%async_computation.2 | async-start | bytes 8388608
  649.8 19.1 %slice-start.1 = ((s8[16777216]{0:T(1024)(128)(4,1)}), s8[4194304]{0:T(1024)(128)(4,1)S(1)}, s32[]{:S(2)}) async-start(s8[16777216]{0:T(1024)(128)(4,1)} %bitcast.57), calls=%async_computation.3 | async-start | bytes 8388608
  649.8 20.3 %slice-start.2 = ((s8[16777216]{0:T(1024)(128)(4,1)}), s8[4194304]{0:T(1024)(128)(4,1)S(1)}, s32[]{:S(2)}) async-start(s8[16777216]{0:T(1024)(128)(4,1)} %bitcast.57), calls=%async_computation.4 | async-start | bytes 8388608
  649.8 21.5 %slice-start.3 = ((s8[16777216]{0:T(1024)(128)(4,1)}), s8[4194304]{0:T(1024)(128)(4,1)S(1)}, s32[]{:S(2)}) async-start(s8[16777216]{0:T(1024)(128)(4,1)} %bitcast.57), calls=%async_computation.5 | async-start | bytes 8388608
Sparse Core Ops, SparseCore 0:
  9.6 48.5 all-gather.2
  60.1 35.1 all-gather.4

commit v5 on v4

--- a/solution.py
+++ b/solution.py
@@ -186,9 +186,11 @@
 
 def transform_kernel(
     parts, size_x, size_y,
-    weighted, plain, x_back, x_band, y_band, rim_select, x_inv, y_fwd, rows_x, rows_y, eigen_z,
+    weighted, plain, first_rest, last_rest,
+    x_back, x_band, y_band, rim_select, x_inv, y_fwd, rows_x, rows_y, eigen_z,
     section_one, section_six, spread_out, left_out, right_out,
-    lines_x, lines_y, lines_back, send_a, send_b, send_c, modes, along, low, high, rims,
+    lines_x, lines_y, lines_back, send_a, send_b, send_c, modes, along, low, high, low_rest, high_rest,
+    found_rest, rims,
     from_left, from_right, x_fwd, eigen_xy, all_x,
     fs, fr, gs, gr, hs, hr, bs, br, fl, gl, hl, bl, xs, xr, ys, yr, us, ur, vs, vr, loads, es, er,
 ):
@@ -222,49 +224,56 @@
             src, dst, send, receive, device_id=peer, device_id_type=MESH_ID
         )
 
-    def x_halo(source, sends, receives):
-        def copy(c, way):
+    def x_halo(source, rests, sends, receives):
+        def copies_of(c, way):
             here = pl.ds(c * part, part)
             if way == 0:
-                src, dst = source.at[here, :, pl.ds(0, RIM_ROWS)], high.at[here]
+                near = source.at[here, :, pl.ds(0, NEAR)], high.at[here]
+                rest = rests[0].at[here], high_rest.at[here]
             else:
-                src = source.at[here, :, pl.ds(block_x - RIM_ROWS, RIM_ROWS)]
-                dst = low.at[here]
-            return remote(src, dst, sends.at[c, way], receives.at[c, way], peers[way])
-
-        return copy, 0
+                near = source.at[here, :, pl.ds(block_x - NEAR, NEAR)], low.at[here]
+                rest = rests[1].at[here], low_rest.at[here]
+            return [
+                remote(*pair, sends.at[c, 2 * way + n], receives.at[c, 2 * way + n], peers[way])
+                for n, pair in enumerate((near, rest))
+            ]
+
+        return copies_of, 0
 
     def y_halo(landing, sends, receives):
-        def copy(c, way):
+        def copies_of(c, way):
             src = rims.at[c % slots, 1 - way]
             dst = landing[1 - way].at[pl.ds(c * part, part)]
-            return remote(src, dst, sends.at[c, way], receives.at[c, way], peers[2 + way])
-
-        return copy, 2
+            return [remote(src, dst, sends.at[c, way], receives.at[c, way], peers[2 + way])]
+
+        return copies_of, 2
 
     def halo_start(kind, c):
-        copy, base = kind
+        copies_of, base = kind
         for way in range(2):
 
             @pl.when(has[base + way])
             def _():
-                copy(c, way).start()
+                for copy in copies_of(c, way):
+                    copy.start()
 
     def halo_landed(kind, c):
-        copy, base = kind
+        copies_of, base = kind
         for way in range(2):
 
             @pl.when(has[base + 1 - way])
             def _():
-                copy(c, way).wait_recv()
+                for copy in copies_of(c, way):
+                    copy.wait_recv()
 
     def halo_sent(kind, c):
-        copy, base = kind
+        copies_of, base = kind
         for way in range(2):
 
             @pl.when(has[base + way])
             def _():
-                copy(c, way).wait_send()
+                for copy in copies_of(c, way):
+                    copy.wait_send()
 
     def local(source, target, kind, c):
         return pltpu.make_async_copy(source, target, loads.at[kind, c])
@@ -352,10 +361,10 @@
                 found = jnp.dot(rows, y_fwd[:, pl.ds(b, 256)], preferred_element_type=jnp.float32)
                 weight = eigen_xy[:, pl.ds(b, 256)]
                 modes[pl.ds(0, share), pl.ds(b, 256)] = (
-                    found[:share] / (weight * eigen_z[k] + tikhonov)
+                    found[:share] / (weight * eigen_z[me_x * depth + k] + tikhonov)
                 ).astype(bf)
                 modes[pl.ds(share, share), pl.ds(b, 256)] = (
-                    found[share:] / (weight * eigen_z[k + 1] + tikhonov)
+                    found[share:] / (weight * eigen_z[me_x * depth + k + 1] + tikhonov)
                 ).astype(bf)
             for b in range(0, full_y, 256):
                 found = lax.dot_general(
@@ -369,13 +378,45 @@
         lax.fori_loop(0, part // 2, pair, 0)
 
     def blur_x(source, band, c):
+        slot = c % slots
+
         def step(i, carry):
-            blur_x_lines(
-                [source[c % slots, i, q] for q in range(QUADS)],
-                low.at[c * part + i], high.at[c * part + i], band,
-                along.at[c % slots, i], rims.at[c % slots, 0, i], rims.at[c % slots, 1, i],
-                rim_select,
-            )
+            for q in range(QUADS):
+                both = jnp.concatenate(
+                    [
+                        jnp.concatenate(
+                            [
+                                low[c * part + p, q], low_rest[c * part + p], source[slot, p, q],
+                                high[c * part + p, q], high_rest[c * part + p],
+                            ],
+                            axis=0,
+                        )
+                        for p in (2 * i, 2 * i + 1)
+                    ],
+                    axis=1,
+                )
+                found = jnp.dot(band[q], both, preferred_element_type=jnp.float32).astype(bf)
+                along[slot, 2 * i, q] = found[:, :block_y]
+                along[slot, 2 * i + 1, q] = found[:, block_y:]
+            for p in (2 * i, 2 * i + 1):
+                pack_rims(
+                    [along[slot, p, q] for q in range(QUADS)],
+                    rims.at[slot, 0, p], rims.at[slot, 1, p], rim_select,
+                )
+            return carry
+
+        lax.fori_loop(0, part // 2, step, 0)
+
+    def pack_rest(source, c):
+        def step(i, carry):
+            for n, row, skip in ((0, NEAR, 0), (1, block_x - 2 * NEAR, NEAR - REST)):
+                lines = [
+                    source[c % slots, i, q, pl.ds(row, NEAR)].astype(jnp.float32)[
+                        skip : skip + REST
+                    ]
+                    for q in range(QUADS)
+                ]
+                found_rest[n, c * part + i] = jnp.concatenate(lines, axis=0).astype(bf)
             return carry
 
         lax.fori_loop(0, part, step, 0)
@@ -401,7 +442,7 @@
 
         lax.fori_loop(0, 2, step, 0)
 
-    x_first = x_halo(weighted, xs, xr)
+    x_first = x_halo(weighted, (first_rest, last_rest), xs, xr)
     y_first = y_halo((from_left, from_right), ys, yr)
     load_u = [local(whole(weighted, c), send_a.at[c % slots], 0, c) for c in range(parts)]
     load_p = [local(whole(plain, c), send_c.at[c % slots], 1, c) for c in range(parts)]
@@ -411,7 +452,9 @@
     for c in range(slots):
         load_u[c].start()
         load_p[c].start()
-    for there, ref in zip(has, (low, high, from_left, from_right)):
+    for there, ref in zip(
+        has + has[:2], (low, high, from_left, from_right, low_rest, high_rest)
+    ):
 
         @pl.when(jnp.logical_not(there))
         def _():
@@ -490,7 +533,7 @@
             sent("g", c)
             sent("h", c)
 
-    x_last = x_halo(section_six, us, ur)
+    x_last = x_halo(section_six, (found_rest.at[0], found_rest.at[1]), us, ur)
     y_last = y_halo((left_out, right_out), vs, vr)
     load_s = [local(whole(section_six, c), send_a.at[c % slots], 3, c) for c in range(parts)]
     store_a = [local(along.at[c % slots], whole(spread_out, c), 4, c) for c in range(parts)]
@@ -509,11 +552,12 @@
             if c >= parts - slots:
                 sent("b", c)
             landed("b", c)
+            load_s[c].start()
+            load_s[c].wait()
+            pack_rest(send_a, c)
             halo_start(x_last, c)
-            load_s[c].start()
         if c > 0:
             d = c - 1
-            load_s[d].wait()
             halo_landed(x_last, d)
             if d >= slots:
                 halo_sent(y_last, d - slots)
@@ -535,7 +579,8 @@
 
 
 def transform(
-    weighted, plain, x_back, x_band, y_back, rim_select, x_inv, y_fwd, rows_x, rows_y, eigen_z,
+    weighted, plain, first_rest, last_rest,
+    x_back, x_band, y_back, rim_select, x_inv, y_fwd, rows_x, rows_y, eigen_z,
     size_x, size_y,
 ):
     depth, quads, block_x, block_y = weighted.shape
@@ -552,11 +597,12 @@
     modes = jax.ShapeDtypeStruct(weighted.shape, bf)
     side = jax.ShapeDtypeStruct((depth, block_x, block_y), bf)
     chunk = pltpu.VMEM((slots, part, quads, block_x, block_y), bf)
-    edge = pltpu.VMEM((depth, quads, RIM_ROWS, block_y), bf)
+    edge = pltpu.VMEM((depth, quads, NEAR, block_y), bf)
+    rest = pltpu.VMEM((depth, quads * REST, block_y), bf)
     return pl.pallas_call(
         functools.partial(transform_kernel, parts, size_x, size_y),
         out_shape=[modes, modes, modes, side, side],
-        in_specs=[hbm, hbm] + [vmem] * 8 + [pl.BlockSpec(memory_space=pltpu.SMEM)],
+        in_specs=[hbm] * 4 + [vmem] * 8 + [pl.BlockSpec(memory_space=pltpu.SMEM)],
         out_specs=[hbm] * 5,
         scratch_shapes=[
             pltpu.VMEM((depth, full_x, block_y), bf),
@@ -567,7 +613,8 @@
             chunk,
             pltpu.VMEM((2 * share, full_y), bf),
             chunk,
-            edge, edge,
+            edge, edge, rest, rest,
+            pltpu.VMEM((2, depth, quads * REST, block_y), bf),
             pltpu.VMEM((slots, 2, part, block_x, block_y), bf),
             pltpu.VMEM(side.shape, bf), pltpu.VMEM(side.shape, bf),
             pltpu.VMEM((full_x, full_x), bf),
@@ -576,7 +623,7 @@
             sem(size_x), sem(size_x), sem(size_y), sem(size_y),
             sem(size_y), sem(size_y), sem(size_x), sem(size_x),
             one, one, one, one,
-            sem(2), sem(2), sem(2), sem(2), sem(2), sem(2), sem(2), sem(2),
+            sem(4), sem(4), sem(2), sem(2), sem(4), sem(4), sem(2), sem(2),
             pltpu.SemaphoreType.DMA((6, parts)),
             pltpu.SemaphoreType.DMA((size_x,)), pltpu.SemaphoreType.DMA((size_x,)),
         ],
@@ -584,7 +631,8 @@
             collective_id=0, has_side_effects=True, vmem_limit_bytes=62 * 2**20
         ),
     )(
-        weighted, plain, x_back, x_band, y_back, rim_select, x_inv, y_fwd, rows_x, rows_y, eigen_z
+        weighted, plain, first_rest, last_rest,
+        x_back, x_band, y_back, rim_select, x_inv, y_fwd, rows_x, rows_y, eigen_z,
     )
 
 
@@ -597,9 +645,13 @@
         found = jnp.dot(band[...], both, preferred_element_type=jnp.float32).astype(jnp.bfloat16)
         along[q] = found[:, :half]
         along[q + 1] = found[:, half:]
-    wide = jnp.concatenate([along[q] for q in range(len(lines))], axis=1)
+    pack_rims([along[q] for q in range(len(lines))], to_right, to_left, rim_select)
+
+
+def pack_rims(lines, to_right, to_left, rim_select):
+    half = lines[0].shape[1]
     found = jnp.dot(
-        wide, rim_select[...], preferred_element_type=jnp.float32
+        jnp.concatenate(lines, axis=1), rim_select[...], preferred_element_type=jnp.float32
     ).astype(jnp.bfloat16)
     to_left[...] = found[:, half:]
     to_right[...] = found[:, :half]
@@ -608,6 +660,8 @@
 BAND_ROWS = 16
 QUADS = 4
 RIM_ROWS = 32
+NEAR = 16
+REST = HALF + SHIFT - NEAR
 SIXES = 6
 
 
@@ -787,7 +841,7 @@
 
 def misfit_kernel(
     along, from_left, from_right, observed, confidence, y_band, matrix,
-    misfit, weighted, held, turned_back,
+    misfit, weighted, first_rest, last_rest, held, turned_back,
 ):
     def put(s, found):
         for r in range(found.shape[0]):
@@ -806,10 +860,25 @@
     for q in range(QUADS):
         weighted[:, q] = turned_back[pl.ds(q * groups, groups)].astype(weighted.dtype)
 
+    def rest(row):
+        return jnp.concatenate(
+            [turned_back[pl.ds(q * groups, groups), pl.ds(row, REST)] for q in range(QUADS)],
+            axis=1,
+        ).astype(weighted.dtype)
+
+    @pl.when(pl.program_id(0) == 1)
+    def _():
+        first_rest[...] = rest(0)
+
+    @pl.when(pl.program_id(0) == pl.num_programs(0) - 2)
+    def _():
+        last_rest[...] = rest(BAND_ROWS - REST)
+
 
 def find_misfit(along, from_left, from_right, observed, confidence, y_band, matrix):
     shape, space = along.shape, observed.shape
     modes = (space[2] // QUADS, QUADS, shape[2], shape[3])
+    rest = (modes[0], QUADS * REST, shape[3])
     rims = pl.BlockSpec((shape[0], BAND_ROWS, shape[3]), lambda i: (0, i, 0))
     held = pltpu.VMEM((shape[0] * SIXES, BAND_ROWS, shape[3]), jnp.float32)
     turned = pltpu.VMEM((space[2], BAND_ROWS, shape[3]), jnp.float32)
@@ -819,13 +888,18 @@
         out_shape=[
             jax.ShapeDtypeStruct(space, jnp.float32),
             jax.ShapeDtypeStruct(modes, jnp.bfloat16),
+            jax.ShapeDtypeStruct(rest, jnp.bfloat16),
+            jax.ShapeDtypeStruct(rest, jnp.bfloat16),
         ],
         in_specs=[
             modes_block(BAND_ROWS, shape), rims, rims,
             space_block(BAND_ROWS, space), space_block(BAND_ROWS, space),
             whole_block(y_band.shape), whole_block(matrix.shape),
         ],
-        out_specs=[space_block(BAND_ROWS, space), modes_block(BAND_ROWS, modes)],
+        out_specs=[
+            space_block(BAND_ROWS, space), modes_block(BAND_ROWS, modes),
+            whole_block(rest), whole_block(rest),
+        ],
         scratch_shapes=[held, turned],
         compiler_params=pltpu.CompilerParams(vmem_limit_bytes=60 * 2**20),
     )(along, from_left, from_right, observed, confidence, y_band, matrix)
@@ -872,7 +946,7 @@
     shape, space = along.shape, confidence.shape
     rims = pl.BlockSpec((shape[0], BAND_ROWS, shape[3]), lambda i: (0, i, 0))
     held = pltpu.VMEM((space[2], BAND_ROWS, shape[3]), jnp.float32)
-    sums = (3, 8, space[2])
+    sums = (8, 8, space[2])
     return pl.pallas_call(
         direction_kernel,
         grid=(shape[2] // BAND_ROWS,),
@@ -928,7 +1002,6 @@
 
 def total_sums(sums, size_x, size_y, number):
     lanes = sums.shape[2]
-    padded = jnp.pad(sums, ((0, 5), (0, 0), (0, 0)))
     vmem = pl.BlockSpec(memory_space=pltpu.VMEM)
     sem = lambda n: pltpu.SemaphoreType.DMA((n - 1,))
     f32 = jnp.float32
@@ -944,7 +1017,25 @@
             sem(size_x), sem(size_x), sem(size_y), sem(size_y),
         ],
         compiler_params=pltpu.CompilerParams(collective_id=number, has_side_effects=True),
-    )(padded)
+    )(sums)
+
+
+def x_bands(kernel, offset, block_x):
+    rim = HALF + SHIFT
+    band = band_matrix(kernel, offset, block_x, block_x + 2 * rim, rim)
+    stacks = []
+    for q in range(QUADS):
+        pads = ((0, 0), (q * REST, (QUADS - 1 - q) * REST))
+        stacks.append(
+            jnp.concatenate(
+                [
+                    band[:, REST:rim], jnp.pad(band[:, :REST], pads), band[:, rim:-rim],
+                    band[:, -rim:-REST], jnp.pad(band[:, -REST:], pads),
+                ],
+                axis=1,
+            )
+        )
+    return jnp.stack(stacks).astype(jnp.bfloat16)
 
 
 def y_bands(kernel, offset, block_y, count):
@@ -990,12 +1081,10 @@
     share_x = block_x * size_x // size_y
     rows_x = jnp.broadcast_to(eigen_x.reshape(-1, 1, share_x), (block_x // share_x, 8, share_x))
     rows_y = jnp.broadcast_to(eigen_y[None, :], (8, eigen_y.shape[0]))
-    share_z = depth // size_x
-    part_z = lax.dynamic_slice_in_dim(eigen_z, lax.axis_index("gx") * share_z, share_z)
-
     wide_x = block_x + 2 * RIM_ROWS
     x_band = band_matrix(kernels[0], offsets[0], block_x, wide_x, RIM_ROWS).astype(bf)
-    x_back = band_matrix(adjoint[0], -offsets[0], block_x, wide_x, RIM_ROWS).astype(bf)
+    x_bands_back = x_bands(adjoint[0], -offsets[0], block_x)
+    x_bands_on = x_bands(kernels[0], offsets[0], block_x)
     y_first = y_bands(kernels[1], offsets[1], block_y, SIXES)
     y_band = y_bands(kernels[1], offsets[1], block_y, QUADS)
     y_back = y_bands(adjoint[1], -offsets[1], block_y, QUADS)
@@ -1007,12 +1096,12 @@
 
     along_z, plain = to_modes(iterate, entry)
     rims = spread(along_z, x_band, rim_selects(block_y, SIXES), size_x, size_y, 1)
-    misfit, weighted = find_misfit(
+    misfit, weighted, *rests = find_misfit(
         *rims, observed, confidence, y_first, blurring.T.astype(bf)
     )
     section_one, section_six, *rims = transform(
-        weighted, plain, x_back, x_band, y_back, rim_select, full_x, full_y,
-        rows_x, rows_y, part_z, size_x, size_y,
+        weighted, plain, *rests, x_bands_back, x_bands_on, y_back, rim_select, full_x, full_y,
+        rows_x, rows_y, eigen_z, size_x, size_y,
     )
     coarse = blurring.T.astype(bf)
     fine = (blurring.T - coarse.astype(jnp.float32)).astype(bf)

time: 697 us -> 693 us (level)
  Pallas kernels: 615 us -> 606 us
    pallas_call x1, Pallas kernels: 445 us -> 436 us  [transform(): pl.pallas_call(functools.partial(transform_kernel, parts, size_x, size_y)...]
where the time goes in v5:
time: 693 us; the launch traced here: 685 us
  Pallas kernels  606 us (87%)
  other arithmetic  49 us (7%)
  between operations  18 us (3%)
  local copies, waits for them, and re-layouts  10.4 us (2%)
    pallas_call x1, Pallas kernels, transform(): pl.pallas_call(functools.partial(transform_kernel, parts, size_x, size_y)...  436 us
    pallas_call x1, Pallas kernels, spread(): pl.pallas_call(functools.partial(spread_kernel, size_x, size_y, groups //...  39.6 us
    pallas_call x1, Pallas kernels, find_direction(): pl.pallas_call(direction_kernel, grid=(shape[2] // BAND_ROWS,), out_shape...  37.7 us
    pallas_call x1, Pallas kernels, find_misfit(): pl.pallas_call(misfit_kernel, grid=(shape[2] // BAND_ROWS,), out_shape=[j...  35 us
    pallas_call x1, Pallas kernels, total_sums(): pl.pallas_call(functools.partial(total_kernel, size_x, size_y), out_shape...  30.6 us
    pallas_call x1, Pallas kernels, to_modes(): pl.pallas_call(to_modes_kernel, grid=(block_x // BAND_ROWS,), out_shape=[...  27.1 us
    add x1, other arithmetic, kernel_shards(): return (iterate + step_size * direction, misfit - step_size * blurred)  17.8 us
  transfers between devices with their start and end apart: 2, of which 0 were waited for; matrix products, arithmetic and copies ran while one was open for 3% of the time, Pallas kernels for 15%

profile of v5, /device:TPU:0, one launch (start us, length us, event | category | flops | bytes accessed | tf_op | source)
XLA Modules:
  0.0 685.2 jit_solution(13114765410237459893)
XLA Ops:
  7.2 0.7 all-gather.3.cloned.1.call-update
  7.9 0.7 all-gather.5.cloned.1.call-update
  8.7 1.4 fusion.110
  10.8 0.7 fusion.86
  12.7 0.9 select_reduce_fusion.6
  13.8 2.0 select_reduce_fusion.1
  16.7 0.9 copy.31
  17.6 0.7 add_subtract_fusion.1
  19.0 0.7 fusion.88
  21.1 1.1 select_reduce_fusion
  22.2 0.8 copy.32.x_band
  23.7 0.9 fusion.8
  24.6 0.9 add_convert_fusion.rim_select
  25.5 27.1 %shard_map.131 = (bf16[22,6,256,128]{3,2,1,0:T(8,128)(2,1)}, bf16[32,4,256,128]{3,2,1,0:T(8,128)(2,1)}) custom-call(bf16[256,128]{1,0:T(8,128)(2,1)} %pad_maximum_fusion.24.matrix, f32[256,128,128]{2,1,0:T(8,128)} %source.1), custom_call_target="tpu_custom_call" | custom-call | tf_op jit(solution)/shard_map/pallas_call | solution.py:704
  52.6 39.6 %shard_map.132 = (bf16[22,6,256,128]{3,2,1,0:T(8,128)(2,1)}, bf16[22,256,128]{2,1,0:T(8,128)(2,1)}, bf16[22,256,128]{2,1,0:T(8,128)(2,1)}) custom-call(bf16[22,6,256,128]{3,2,1,0:T(8,128)(2,1)} %get-tuple-element.19.source, bf16[256,320]{1,0:T(8,128)(2,1)} %copy.32.x_band, bf16[768,256]{1,0:T(8,128)(2,1)} %add_convert_fusion.rim_select), custom_call_target="tpu_custom_call" | custom-call | tf_op jit(solution)/shard_map/pallas_call | solution.py:820
  92.9 0.8 subtract_convert_fusion
  93.7 35.0 %shard_map.133 = (f32[256,128,128]{2,1,0:T(8,128)}, bf16[32,4,256,128]{3,2,1,0:T(8,128)(2,1)}, bf16[32,16,128]{2,1,0:T(8,128)(2,1)}, bf16[32,16,128]{2,1,0:T(8,128)(2,1)}) custom-call(bf16[22,6,256,128]{3,2,1,0:T(8,128)(2,1)} %get-tuple-element.20.along, bf16[22,256,128]{2,1,0:T(8,128)(2,1)} %get-tuple-element.21.from_left, ...), custom_call_target="tpu_custom_call" | custom-call | tf_op jit(solution)/shard_map/pallas_call | solution.py:885
  130.1 0.8 add_convert_fusion.1.rim_select
  130.9 0.8 pad_maximum_fusion.2.y_band
  131.8 0.8 pad_maximum_fusion.3.y_band
  133.0 1.1 pad_maximum_fusion.1.x_band
  134.4 1.1 pad_maximum_fusion.x_back
  136.7 435.6 %shard_map.134 = (bf16[32,4,256,128]{3,2,1,0:T(8,128)(2,1)}, bf16[32,4,256,128]{3,2,1,0:T(8,128)(2,1)}, bf16[32,4,256,128]{3,2,1,0:T(8,128)(2,1)}, bf16[32,256,128]{2,1,0:T(8,128)(2,1)}, bf16[32,256,128]{2,1,0:T(8,128)(2,1)}) custom-call(bf16[32,4,256,128]{3,2,1,0:T(8,128)(2,1)} %get-tuple-element.23.weighted, ...), custom_call_target="tpu_custom_call" | custom-call | tf_op jit(solution)/shard_map/pallas_call | solution.py:602
  572.3 37.7 %shard_map.135 = (f32[256,128,128]{2,1,0:T(8,128)}, f32[256,128,128]{2,1,0:T(8,128)}, f32[8,8,128]{2,1,0:T(8,128)}) custom-call(bf16[32,4,256,128]{3,2,1,0:T(8,128)(2,1)} %get-tuple-element.27.along, bf16[32,256,128]{2,1,0:T(8,128)(2,1)} %get-tuple-element.28.from_left, bf16[32,256,128]{2,1,0:T(8,128)(2,1)} %get-tuple-element.29.from_right, ...), custom_call_target="tpu_custom_call" | custom-call | tf_op jit(solution)/shard_map/pallas_call | solution.py:950
  610.0 30.6 %shard_map.136 = f32[8,128]{1,0:T(8,128)} custom-call(f32[8,8,128]{2,1,0:T(8,128)} %get-tuple-element.32.values), custom_call_target="tpu_custom_call" | custom-call | tf_op jit(solution)/shard_map/pallas_call | solution.py:1008
  640.6 0.8 reduce_sum.93
  641.4 0.7 fusion.109
  644.0 17.8 %multiply_add_fusion = f32[256,128,128]{2,1,0:T(8,128)} fusion(f32[256,128,128]{2,1,0:T(8,128)} %source.1, f32[256,128,128]{2,1,0:T(8,128)} %get-tuple-element.33, f32[]{:T(128)} %bitcast.34), kind=kLoop, calls=%fused_computation.1 | loop fusion | flops 8388608 | bytes 50331652 | tf_op jit(solution)/shard_map/add | solution.py:1114
  661.8 1.3 slice-done.1
  663.1 1.2 slice-done.2
  664.3 1.2 slice-done.3
  665.5 12.4 %multiply_subtract_fusion = f32[256,128,128]{2,1,0:T(8,128)} fusion(f32[256,128,128]{2,1,0:T(8,128)S(1)} %bitcast.74, f32[256,128,128]{2,1,0:T(8,128)} %get-tuple-element.35, f32[]{:T(128)} %bitcast.34), kind=kLoop, calls=%fused_computation | loop fusion | flops 8388608 | bytes 50331652 | tf_op jit(solution)/shard_map/sub | solution.py:1114
  (80 shorter events, 8.4 us)
Async XLA Ops:
  7.2 128.4 %all-gather.3.cloned.1.call-start = ((), (), s32[]{:S(2)}) async-start(), calls=%async_computation | async-start | bytes 2621440 | tf_op jit(solution)/shard_map/all_gather | solution.py:1079
  7.9 127.6 %all-gather.5.cloned.1.call-start = ((), (), s32[]{:S(2)}) async-start(), calls=%async_computation.1 | async-start | bytes 2359296 | tf_op jit(solution)/shard_map/all_gather | solution.py:1080
  17.6 35.0 %copy-start.2 = (bf16[128,128]{0,1:T(8,128)(2,1)}, bf16[128,128]{0,1:T(8,128)(2,1)S(1)}, u32[]{:S(2)}) copy-start(bf16[128,128]{0,1:T(8,128)(2,1)S(1)} %copy.31) | copy-start | bytes 98308
  52.6 40.0 %copy-start.6 = (pred[128]{0:T(512)(128)(4,1)S(1)}, pred[128]{0:T(512)(128)(4,1)}, u32[]{:S(2)}) copy-start(pred[128]{0:T(512)(128)(4,1)} %constant.122.clone.1) | copy-start | bytes 388
  52.6 40.3 %copy-start.3 = (bf16[128,128]{1,0:T(8,128)(2,1)S(1)}, bf16[128,128]{1,0:T(8,128)(2,1)}, u32[]{:S(2)}) copy-start(bf16[128,128]{1,0:T(8,128)(2,1)} %param.20) | copy-start | bytes 98308
  92.9 0.9 copy-start
  93.7 35.1 %copy-start.1 = (bf16[128,128]{1,0:T(8,128)(2,1)S(1)}, bf16[128,128]{1,0:T(8,128)(2,1)}, u32[]{:S(2)}) copy-start(bf16[128,128]{1,0:T(8,128)(2,1)} %get-tuple-element.39.matrix) | copy-start | bytes 98308
  128.7 6.8 copy-start.5
  128.7 7.4 %copy-start.4 = (f32[1024]{0:T(1024)S(1)}, f32[1024]{0:T(1024)}, u32[]{:S(2)}) copy-start(f32[1024]{0:T(1024)} %param.22) | copy-start | bytes 12292
  644.0 17.9 %slice-start = ((s8[16777216]{0:T(1024)(128)(4,1)}), s8[4194304]{0:T(1024)(128)(4,1)S(1)}, s32[]{:S(2)}) async-start(s8[16777216]{0:T(1024)(128)(4,1)} %bitcast.73), calls=%async_computation.2 | async-start | bytes 8388608
  644.0 19.1 %slice-start.1 = ((s8[16777216]{0:T(1024)(128)(4,1)}), s8[4194304]{0:T(1024)(128)(4,1)S(1)}, s32[]{:S(2)}) async-start(s8[16777216]{0:T(1024)(128)(4,1)} %bitcast.73), calls=%async_computation.3 | async-start | bytes 8388608
  644.0 20.3 %slice-start.2 = ((s8[16777216]{0:T(1024)(128)(4,1)}), s8[4194304]{0:T(1024)(128)(4,1)S(1)}, s32[]{:S(2)}) async-start(s8[16777216]{0:T(1024)(128)(4,1)} %bitcast.73), calls=%async_computation.4 | async-start | bytes 8388608
  644.0 21.5 %slice-start.3 = ((s8[16777216]{0:T(1024)(128)(4,1)}), s8[4194304]{0:T(1024)(128)(4,1)S(1)}, s32[]{:S(2)}) async-start(s8[16777216]{0:T(1024)(128)(4,1)} %bitcast.73), calls=%async_computation.5 | async-start | bytes 8388608
Sparse Core Ops, SparseCore 0:
  9.6 48.6 all-gather.2
  60.1 34.9 all-gather.4

commit v6 on v5

--- a/solution.py
+++ b/solution.py
@@ -471,7 +471,7 @@
     for b in range(0, full, block_y):
         x_fwd[pl.ds(b, block_y), :] = x_inv[:, pl.ds(b, block_y)].astype(jnp.float32).T.astype(bf)
 
-    ahead = 2
+    ahead = 3
     for c in range(parts + 1):
         if c < parts:
             load_u[c].wait()

time: 693 us -> 693 us (level)
  no operation moved by 1% of the time
where the time goes in v6:
time: 693 us; the launch traced here: 685 us
  Pallas kernels  605 us (87%)
  other arithmetic  49 us (7%)
  between operations  18 us (3%)
  local copies, waits for them, and re-layouts  10.4 us (2%)
    pallas_call x1, Pallas kernels, transform(): pl.pallas_call(functools.partial(transform_kernel, parts, size_x, size_y)...  435 us
    pallas_call x1, Pallas kernels, spread(): pl.pallas_call(functools.partial(spread_kernel, size_x, size_y, groups //...  39.6 us
    pallas_call x1, Pallas kernels, find_direction(): pl.pallas_call(direction_kernel, grid=(shape[2] // BAND_ROWS,), out_shape...  37.7 us
    pallas_call x1, Pallas kernels, find_misfit(): pl.pallas_call(misfit_kernel, grid=(shape[2] // BAND_ROWS,), out_shape=[j...  35 us
    pallas_call x1, Pallas kernels, total_sums(): pl.pallas_call(functools.partial(total_kernel, size_x, size_y), out_shape...  30.6 us
    pallas_call x1, Pallas kernels, to_modes(): pl.pallas_call(to_modes_kernel, grid=(block_x // BAND_ROWS,), out_shape=[...  27.1 us
    add x1, other arithmetic, kernel_shards(): return (iterate + step_size * direction, misfit - step_size * blurred)  17.8 us
  transfers between devices with their start and end apart: 2, of which 0 were waited for; matrix products, arithmetic and copies ran while one was open for 3% of the time, Pallas kernels for 15%

profile of v6, /device:TPU:0, one launch (start us, length us, event | category | flops | bytes accessed | tf_op | source)
XLA Modules:
  0.0 685.1 jit_solution(16895924052876902385)
XLA Ops:
  7.2 0.7 all-gather.3.cloned.1.call-update
  7.9 0.7 all-gather.5.cloned.1.call-update
  8.7 1.4 fusion.110
  10.8 0.7 fusion.86
  12.7 0.9 select_reduce_fusion.6
  13.8 2.0 select_reduce_fusion.1
  16.7 0.9 copy.31
  17.6 0.7 add_subtract_fusion.1
  19.0 0.7 fusion.88
  21.1 1.1 select_reduce_fusion
  22.2 0.8 copy.32.x_band
  23.7 0.9 fusion.8
  24.6 0.9 add_convert_fusion.rim_select
  25.5 27.1 %shard_map.131 = (bf16[22,6,256,128]{3,2,1,0:T(8,128)(2,1)}, bf16[32,4,256,128]{3,2,1,0:T(8,128)(2,1)}) custom-call(bf16[256,128]{1,0:T(8,128)(2,1)} %pad_maximum_fusion.24.matrix, f32[256,128,128]{2,1,0:T(8,128)} %source.1), custom_call_target="tpu_custom_call" | custom-call | tf_op jit(solution)/shard_map/pallas_call | solution.py:704
  52.6 39.6 %shard_map.132 = (bf16[22,6,256,128]{3,2,1,0:T(8,128)(2,1)}, bf16[22,256,128]{2,1,0:T(8,128)(2,1)}, bf16[22,256,128]{2,1,0:T(8,128)(2,1)}) custom-call(bf16[22,6,256,128]{3,2,1,0:T(8,128)(2,1)} %get-tuple-element.19.source, bf16[256,320]{1,0:T(8,128)(2,1)} %copy.32.x_band, bf16[768,256]{1,0:T(8,128)(2,1)} %add_convert_fusion.rim_select), custom_call_target="tpu_custom_call" | custom-call | tf_op jit(solution)/shard_map/pallas_call | solution.py:820
  92.9 0.8 subtract_convert_fusion
  93.7 35.0 %shard_map.133 = (f32[256,128,128]{2,1,0:T(8,128)}, bf16[32,4,256,128]{3,2,1,0:T(8,128)(2,1)}, bf16[32,16,128]{2,1,0:T(8,128)(2,1)}, bf16[32,16,128]{2,1,0:T(8,128)(2,1)}) custom-call(bf16[22,6,256,128]{3,2,1,0:T(8,128)(2,1)} %get-tuple-element.20.along, bf16[22,256,128]{2,1,0:T(8,128)(2,1)} %get-tuple-element.21.from_left, ...), custom_call_target="tpu_custom_call" | custom-call | tf_op jit(solution)/shard_map/pallas_call | solution.py:885
  130.1 0.8 add_convert_fusion.1.rim_select
  130.9 0.8 pad_maximum_fusion.2.y_band
  131.8 0.8 pad_maximum_fusion.3.y_band
  133.0 1.1 pad_maximum_fusion.1.x_band
  134.4 1.1 pad_maximum_fusion.x_back
  136.7 435.5 %shard_map.134 = (bf16[32,4,256,128]{3,2,1,0:T(8,128)(2,1)}, bf16[32,4,256,128]{3,2,1,0:T(8,128)(2,1)}, bf16[32,4,256,128]{3,2,1,0:T(8,128)(2,1)}, bf16[32,256,128]{2,1,0:T(8,128)(2,1)}, bf16[32,256,128]{2,1,0:T(8,128)(2,1)}) custom-call(bf16[32,4,256,128]{3,2,1,0:T(8,128)(2,1)} %get-tuple-element.23.weighted, ...), custom_call_target="tpu_custom_call" | custom-call | tf_op jit(solution)/shard_map/pallas_call | solution.py:602
  572.2 37.7 %shard_map.135 = (f32[256,128,128]{2,1,0:T(8,128)}, f32[256,128,128]{2,1,0:T(8,128)}, f32[8,8,128]{2,1,0:T(8,128)}) custom-call(bf16[32,4,256,128]{3,2,1,0:T(8,128)(2,1)} %get-tuple-element.27.along, bf16[32,256,128]{2,1,0:T(8,128)(2,1)} %get-tuple-element.28.from_left, bf16[32,256,128]{2,1,0:T(8,128)(2,1)} %get-tuple-element.29.from_right, ...), custom_call_target="tpu_custom_call" | custom-call | tf_op jit(solution)/shard_map/pallas_call | solution.py:950
  609.9 30.6 %shard_map.136 = f32[8,128]{1,0:T(8,128)} custom-call(f32[8,8,128]{2,1,0:T(8,128)} %get-tuple-element.32.values), custom_call_target="tpu_custom_call" | custom-call | tf_op jit(solution)/shard_map/pallas_call | solution.py:1008
  640.5 0.8 reduce_sum.93
  641.3 0.7 fusion.109
  644.0 17.8 %multiply_add_fusion = f32[256,128,128]{2,1,0:T(8,128)} fusion(f32[256,128,128]{2,1,0:T(8,128)} %source.1, f32[256,128,128]{2,1,0:T(8,128)} %get-tuple-element.33, f32[]{:T(128)} %bitcast.34), kind=kLoop, calls=%fused_computation.1 | loop fusion | flops 8388608 | bytes 50331652 | tf_op jit(solution)/shard_map/add | solution.py:1114
  661.8 1.3 slice-done.1
  663.0 1.2 slice-done.2
  664.2 1.2 slice-done.3
  665.4 12.4 %multiply_subtract_fusion = f32[256,128,128]{2,1,0:T(8,128)} fusion(f32[256,128,128]{2,1,0:T(8,128)S(1)} %bitcast.74, f32[256,128,128]{2,1,0:T(8,128)} %get-tuple-element.35, f32[]{:T(128)} %bitcast.34), kind=kLoop, calls=%fused_computation | loop fusion | flops 8388608 | bytes 50331652 | tf_op jit(solution)/shard_map/sub | solution.py:1114
  (80 shorter events, 8.4 us)
Async XLA Ops:
  7.2 128.4 %all-gather.3.cloned.1.call-start = ((), (), s32[]{:S(2)}) async-start(), calls=%async_computation | async-start | bytes 2621440 | tf_op jit(solution)/shard_map/all_gather | solution.py:1079
  7.9 127.6 %all-gather.5.cloned.1.call-start = ((), (), s32[]{:S(2)}) async-start(), calls=%async_computation.1 | async-start | bytes 2359296 | tf_op jit(solution)/shard_map/all_gather | solution.py:1080
  17.6 35.0 %copy-start.2 = (bf16[128,128]{0,1:T(8,128)(2,1)}, bf16[128,128]{0,1:T(8,128)(2,1)S(1)}, u32[]{:S(2)}) copy-start(bf16[128,128]{0,1:T(8,128)(2,1)S(1)} %copy.31) | copy-start | bytes 98308
  52.6 40.0 %copy-start.6 = (pred[128]{0:T(512)(128)(4,1)S(1)}, pred[128]{0:T(512)(128)(4,1)}, u32[]{:S(2)}) copy-start(pred[128]{0:T(512)(128)(4,1)} %constant.122.clone.1) | copy-start | bytes 388
  52.6 40.3 %copy-start.3 = (bf16[128,128]{1,0:T(8,128)(2,1)S(1)}, bf16[128,128]{1,0:T(8,128)(2,1)}, u32[]{:S(2)}) copy-start(bf16[128,128]{1,0:T(8,128)(2,1)} %param.20) | copy-start | bytes 98308
  92.9 0.9 copy-start
  93.7 35.1 %copy-start.1 = (bf16[128,128]{1,0:T(8,128)(2,1)S(1)}, bf16[128,128]{1,0:T(8,128)(2,1)}, u32[]{:S(2)}) copy-start(bf16[128,128]{1,0:T(8,128)(2,1)} %get-tuple-element.39.matrix) | copy-start | bytes 98308
  128.7 6.8 copy-start.5
  128.7 7.4 %copy-start.4 = (f32[1024]{0:T(1024)S(1)}, f32[1024]{0:T(1024)}, u32[]{:S(2)}) copy-start(f32[1024]{0:T(1024)} %param.22) | copy-start | bytes 12292
  643.9 17.9 %slice-start = ((s8[16777216]{0:T(1024)(128)(4,1)}), s8[4194304]{0:T(1024)(128)(4,1)S(1)}, s32[]{:S(2)}) async-start(s8[16777216]{0:T(1024)(128)(4,1)} %bitcast.73), calls=%async_computation.2 | async-start | bytes 8388608
  643.9 19.1 %slice-start.1 = ((s8[16777216]{0:T(1024)(128)(4,1)}), s8[4194304]{0:T(1024)(128)(4,1)S(1)}, s32[]{:S(2)}) async-start(s8[16777216]{0:T(1024)(128)(4,1)} %bitcast.73), calls=%async_computation.3 | async-start | bytes 8388608
  643.9 20.3 %slice-start.2 = ((s8[16777216]{0:T(1024)(128)(4,1)}), s8[4194304]{0:T(1024)(128)(4,1)S(1)}, s32[]{:S(2)}) async-start(s8[16777216]{0:T(1024)(128)(4,1)} %bitcast.73), calls=%async_computation.4 | async-start | bytes 8388608
  643.9 21.5 %slice-start.3 = ((s8[16777216]{0:T(1024)(128)(4,1)}), s8[4194304]{0:T(1024)(128)(4,1)S(1)}, s32[]{:S(2)}) async-start(s8[16777216]{0:T(1024)(128)(4,1)} %bitcast.73), calls=%async_computation.5 | async-start | bytes 8388608
Sparse Core Ops, SparseCore 0:
  9.6 48.6 all-gather.2
  60.1 34.9 all-gather.4
